TPU v7x, 32 devices: a whole 2x2x4 slice. The times are simulated.
32 devices in a mesh: grp: 2 (over x), lat: 16 (over z, y, core).
Axes of the slice: x: 2, y: 2, z: 4, core: 2. Of those that a mesh axis runs over, the one named last changes fastest.
Arguments:
- features: bfloat16 [2, 32, 192, 512], P('grp', 'lat'), parts along dimension 0, may hold values from -120 to 120
- noise_index: int32 [2], P('grp'), parts along dimension 0, may hold values from 0 to 17
- sigma_table: float32 [18], replicated, may hold values from 0.002 to 80
- affine_weight: bfloat16 [128, 1024], replicated, may hold values from -0.5 to 0.5
- norm_gain: float32 [3, 512], replicated, may hold values from 0.1 to 1.9
- norm_bias: float32 [3, 512], replicated, may hold values from -3 to 3
- conv1_weight: bfloat16 [3, 3, 512, 512], replicated, may hold values from -0.09375 to 0.09375
- conv2_weight: bfloat16 [3, 3, 512, 512], replicated, may hold values from -0.09375 to 0.09375
- conv_bias: float32 [2, 512], replicated, may hold values from -3 to 3
- qkv_weight: bfloat16 [512, 1536], replicated, may hold values from -3 to 3
- proj_weight: bfloat16 [512, 512], replicated, may hold values from -0.25 to 0.25
- proj_bias: float32 [512], replicated, may hold values from -3 to 3
Outputs:
- bottleneck: bfloat16 [2, 16, 96, 512], P('grp', 'lat'), parts along dimension 0
There are 2 independent parts, one for each index of `grp`. A program takes and returns all parts, laid end to end along the dimension named above; an argument that names none is the same for every part. Nothing has to cross between parts.
All inputs are finite; a program needn't handle non-finite values.
Results may differ from a plain program's by a relative error of at most 0.012.
The roundings to bfloat16 on the way count: a program that leaves them out, or rounds other values in their place, can miss the bound.
Values may be sent and summed in bfloat16 or wider, within the bound.
No kernel may reach another device: no remote copies, remote signals or barrier semaphores. Data moves between devices by JAX's collectives and lax.ppermute only.
A program may use at most 128 MiB of HBM per device.

v0:
```python
import math

import jax
import jax.numpy as jnp
from jax import lax
from jax.sharding import PartitionSpec as P

HEAD_DIM = 64
GROUPS = 32
FREQS = 64


eps = 1e-05
skip_gain = 0.7071067811865476


def with_halo(block, sides, width):
    for axis, dim in sides:
        count = lax.axis_size(axis)
        forward = [(i, i + 1) for i in range(count - 1)]
        backward = [(target, source) for source, target in forward]
        low = lax.ppermute(
            lax.slice_in_dim(block, block.shape[dim] - width, None, axis=dim), axis, forward
        )
        high = lax.ppermute(lax.slice_in_dim(block, 0, width, axis=dim), axis, backward)
        block = jnp.concatenate([low, block, high], axis=dim)
    return block


def noise_terms(noise_index, sigma_table, affine_weight):
    levels_count = sigma_table.shape[0]
    chosen = (noise_index[:, None] == jnp.arange(levels_count, dtype=jnp.int32)[None, :]).astype(
        jnp.float32
    )
    sigmas = jnp.sum(chosen * sigma_table[None, :], axis=1)
    log_level = jnp.log(sigmas) / 4.0
    frequency = jnp.exp(-math.log(10000.0) * jnp.arange(FREQS, dtype=jnp.float32) / FREQS)
    angles = log_level[:, None] * frequency[None, :]
    fourier = jnp.concatenate([jnp.cos(angles), jnp.sin(angles)], axis=1).astype(jnp.bfloat16)
    affine = jnp.dot(fourier, affine_weight, preferred_element_type=jnp.float32)
    channels = affine.shape[1] // 2
    return (affine[:, :channels], affine[:, channels:])


def band_moments(values):
    members, height, breadth, channels = values.shape
    group_width = channels // GROUPS
    entries = height * breadth * group_width * lax.axis_size("lat")
    column_sums = jnp.sum(values, axis=(1, 2)).reshape(members, GROUPS, group_width).sum(axis=2)
    column_squares = (
        jnp.sum(jnp.square(values), axis=(1, 2)).reshape(members, GROUPS, group_width).sum(axis=2)
    )
    totals, squares = lax.psum((column_sums, column_squares), "lat")
    center = totals / entries
    spread = squares / entries - center * center
    return (center, spread)


def normalize(values, center, spread, norm_scale, norm_offset):
    group_width = values.shape[-1] // GROUPS
    center_full = jnp.repeat(center, group_width, axis=1)[:, None, None, :]
    factor_full = jnp.repeat(lax.rsqrt(spread + eps), group_width, axis=1)[:, None, None, :]
    return (values - center_full) * factor_full * norm_scale + norm_offset


def convolve(values, kernel):
    return lax.conv_general_dilated(
        values,
        kernel,
        (1, 1),
        ((0, 0), (1, 1)),
        dimension_numbers=("NHWC", "HWIO", "NHWC"),
        preferred_element_type=jnp.float32,
    )


def with_rims(values):
    return with_halo(values, (("lat", 1),), 1)


def key_span(total_rows, breadth):
    row_limit = max(1, 1024 // breadth)
    return math.gcd(total_rows, 1 << row_limit.bit_length() - 1)


def accumulate(running, queries, key_block, value_block):
    blended, largest, totals = running
    scores = jnp.einsum(
        "mqhd,mkhd->mqhk", queries, key_block, preferred_element_type=jnp.float32
    ) * HEAD_DIM ** (-0.5)
    rising = jnp.maximum(largest, jnp.max(scores, axis=-1))
    fading = jnp.exp(largest - rising)
    weights = jnp.exp(scores - rising[..., None])
    totals = totals * fading + jnp.sum(weights, axis=-1)
    blended = blended * fading[..., None] + jnp.einsum(
        "mqhk,mkhd->mqhd",
        weights.astype(jnp.bfloat16),
        value_block,
        preferred_element_type=jnp.float32,
    )
    return (blended, rising, totals)


def local(
    features,
    noise_index,
    sigma_table,
    affine_weight,
    norm_gain,
    norm_bias,
    conv1_weight,
    conv2_weight,
    conv_bias,
    qkv_weight,
    proj_weight,
    proj_bias,
):
    film_scale, film_shift = noise_terms(noise_index, sigma_table, affine_weight)
    film_scale = film_scale[:, None, None, :]
    film_shift = film_shift[:, None, None, :]
    source = features.astype(jnp.float32)
    center, spread = band_moments(source)
    active = jax.nn.silu(normalize(source, center, spread, norm_gain[0], norm_bias[0])).astype(
        jnp.bfloat16
    )
    first_conv = convolve(with_rims(active), conv1_weight) + conv_bias[0]
    center, spread = band_moments(first_conv)
    middle = jax.nn.silu(
        normalize(first_conv, center, spread, norm_gain[1], norm_bias[1]) * (1.0 + film_scale)
        + film_shift
    ).astype(jnp.bfloat16)
    second_conv = convolve(with_rims(middle), conv2_weight)
    level_one = ((source + second_conv + conv_bias[1]) * skip_gain).astype(jnp.bfloat16)
    level_one = lax.optimization_barrier(level_one)
    members, height, breadth, channels = level_one.shape
    low_rows = height // 2
    breadth_low = breadth // 2
    pooled = jnp.mean(
        level_one.astype(jnp.float32).reshape(members, low_rows, 2, breadth_low, 2, channels),
        axis=(2, 4),
    )
    center, spread = band_moments(pooled)
    normed = normalize(pooled, center, spread, norm_gain[2], norm_bias[2]).astype(jnp.bfloat16)
    tokens = low_rows * breadth_low
    head_count = channels // HEAD_DIM
    flat_rows = normed.reshape(members * tokens, channels)
    all_rows = low_rows * lax.axis_size("lat")
    span_rows = key_span(all_rows, breadth_low)
    span_count = all_rows // span_rows
    running = (
        jnp.zeros((members, tokens, head_count, HEAD_DIM), jnp.float32),
        jnp.full((members, tokens, head_count), -1e30, jnp.float32),
        jnp.zeros((members, tokens, head_count), jnp.float32),
    )
    projected = jnp.dot(flat_rows, qkv_weight, preferred_element_type=jnp.float32).astype(
        jnp.bfloat16
    )
    projected = projected.reshape(members, low_rows, breadth_low, 3, channels)
    queries = projected[:, :, :, 0].reshape(members, tokens, head_count, HEAD_DIM)
    key_all, value_all = (
        lax.all_gather(projected[:, :, :, 1], "lat", axis=1, tiled=True),
        lax.all_gather(projected[:, :, :, 2], "lat", axis=1, tiled=True),
    )

    def key_span_step(step_index, inner_state):
        key_slab = lax.dynamic_slice_in_dim(key_all, step_index * span_rows, span_rows, 1).reshape(
            members, span_rows * breadth_low, head_count, HEAD_DIM
        )
        value_slab = lax.dynamic_slice_in_dim(
            value_all, step_index * span_rows, span_rows, 1
        ).reshape(members, span_rows * breadth_low, head_count, HEAD_DIM)
        return accumulate(inner_state, queries, key_slab, value_slab)

    running = lax.fori_loop(0, span_count, key_span_step, running)
    blended, largest, totals = running
    attended = (
        (blended / totals[..., None]).reshape(members * tokens, channels).astype(jnp.bfloat16)
    )
    output_proj = jnp.dot(attended, proj_weight, preferred_element_type=jnp.float32) + proj_bias
    return ((pooled + output_proj.reshape(pooled.shape)) * skip_gain).astype(jnp.bfloat16)


def solution(mesh):
    return jax.shard_map(
        local,
        mesh=mesh,
        in_specs=(
            P("grp", "lat", None, None),
            P("grp"),
            P(),
            P(),
            P(),
            P(),
            P(),
            P(),
            P(),
            P(),
            P(),
            P(),
        ),
        out_specs=P("grp", "lat", None, None),
        check_vma=False,
    )
```

profile of v0, /device:TPU:0, one launch (start us, length us, event | category | flops | bytes accessed | tf_op | source)
XLA Modules:
  0.0 249.0 jit_solution(6614196855762687472)
XLA Ops:
  6.5 1.2 convert_reduce_fusion
  7.8 0.8 fusion.72
  8.6 0.8 fusion.73
  9.8 34.9 %all-reduce.2 = (f32[1,32]{1,0:T(1,128)S(1)}, f32[1,32]{1,0:T(1,128)S(1)}) all-reduce(f32[1,32]{1,0:T(1,128)S(1)} %bitcast.170, f32[1,32]{1,0:T(1,128)S(1)} %bitcast.168), channel_id=1, replica_groups=mesh['grp'=2,'lat'=16] {'lat'}, use_global_device_ids=true, to_apply=%region_5.0 | all-reduce | flops 64 | bytes 512 | tf_op jit(solution)/shard_map/psum | solution.py:53
  45.1 1.3 fusion.45
  46.4 1.3 collective-permute-start
  47.7 1.3 collective-permute-start.1
  49.6 1.3 fusion.57
  51.8 0.8 fusion.74
  52.5 1.1 fusion.58
  53.8 0.6 copy.115
  54.5 0.3 pad.clone
  54.8 0.1 copy.95
  55.0 1.2 copy-done.7
  56.2 2.2 select_reduce_fusion.1
  58.7 30.7 %all-reduce.1 = (f32[1,32]{1,0:T(1,128)S(1)}, f32[1,32]{1,0:T(1,128)S(1)}) all-reduce(f32[1,32]{1,0:T(1,128)S(1)} %bitcast.171, f32[1,32]{1,0:T(1,128)S(1)} %bitcast.167), channel_id=1, replica_groups=mesh['grp'=2,'lat'=16] {'lat'}, use_global_device_ids=true, to_apply=%region_11.12 | all-reduce | flops 64 | bytes 512 | tf_op jit(solution)/shard_map/psum | solution.py:53
  89.7 0.3 multiply_convert_fusion
  90.1 0.3 copy.97
  90.6 1.3 collective-permute-start.2
  92.0 0.2 reshape.311
  92.2 0.4 slice.91
  92.6 1.5 collective-permute-start.3
  94.1 0.3 slice_bitcast_fusion
  94.4 0.3 copy.100
  94.7 1.5 collective-permute-done.3
  96.2 1.3 maximum_bitcast_fusion.1
  97.5 0.3 pad.2
  97.9 0.1 copy.102
  98.0 4.4 %convolution_select_fusion = f32[2,8,25,512]{3,1,2,0:T(8,128)S(1)} fusion(bf16[3,3,512,512]{3,2,1,0:T(8,128)(2,1)} %param.21, bf16[4,1,7,2,512]{4,2,3,0,1:T(8,128)(2,1)S(1)} %slice.92, bf16[4,1,8,25,512]{4,2,3,0,1:T(8,128)(2,1)S(1)} %copy.102, pred[8,25]{0,1:T(8,128)(4,1)S(1)} %copy-done.8), kind=kOutput, calls=%fused_computation.30 | convolution fusion | flops 1890295808 | bytes 6414536 | tf_op jit(solution)/shard_map/conv_general_dilated | solution.py:67
  102.5 0.6 copy.103
  103.1 0.3 slice.93
  103.5 0.2 fusion.49
  103.7 0.2 reduce_sum.172
  103.9 0.5 reduce_sum.173
  104.9 34.2 %all-reduce = (f32[1,32]{1,0:T(1,128)S(1)}, f32[1,32]{1,0:T(1,128)S(1)}) all-reduce(f32[1,32]{1,0:T(1,128)S(1)} %bitcast.169, f32[1,32]{1,0:T(1,128)S(1)} %bitcast.166), channel_id=1, replica_groups=mesh['grp'=2,'lat'=16] {'lat'}, use_global_device_ids=true, to_apply=%region_20.21 | all-reduce | flops 64 | bytes 512 | tf_op jit(solution)/shard_map/psum | solution.py:53
  139.4 0.4 convolution_convert_fusion
  139.8 0.2 reshape.268
  140.0 0.4 fusion.70
  140.5 0.6 copy.108
  141.2 0.7 copy.106
  141.9 0.2 copy.107
  142.1 36.1 %all-gather.7.cloned.1.call-done = bf16[1,16,96,1,512]{4,2,3,0,1:T(8,128)(2,1)} async-done(((bf16[1,1,96,1,512]{4,2,3,0,1:T(8,128)(2,1)}), bf16[1,16,96,1,512]{4,2,3,0,1:T(8,128)(2,1)}) %all-gather.7.cloned.1.call-update) | async-done | bytes 1572880 | tf_op jit(solution)/shard_map/all_gather | solution.py:162
  178.2 40.9 %all-gather.5.cloned.1.call-done = bf16[1,16,96,1,512]{4,2,3,0,1:T(8,128)(2,1)} async-done(((bf16[1,1,96,1,512]{4,2,3,0,1:T(8,128)(2,1)}), bf16[1,16,96,1,512]{4,2,3,0,1:T(8,128)(2,1)}) %all-gather.5.cloned.1.call-update) | async-done | bytes 1572880 | tf_op jit(solution)/shard_map/all_gather | solution.py:161
  219.1 20.1 %while.18 = (s32[]{:T(128)}, f32[1,96,8,64]{1,3,2,0:T(8,128)}, f32[1,96,8]{1,2,0:T(8,128)S(1)}, f32[1,96,8]{1,2,0:T(8,128)S(1)}, bf16[1,16,96,512]{3,2,1,0:T(8,1...) while((s32[]{:T(128)}, f32[1,96,8,64]{1,3,2,0:T(8,128)}, ...), condition=%wide.region_24.25_spmd.clone, body=%wide.region_21.24_spmd.clone.sunk | while | flops 155865600 | bytes 23347460 | solution.py:174
  219.1 2.4 constant_dynamic-slice_fusion.3
  221.5 1.7 copy.121
  223.2 1.8 reshape.314
  225.0 0.7 copy.122
  225.7 0.9 reshape.315
  226.6 0.6 bitcast_reduce_fusion.2
  227.2 0.5 copy-done.1
  227.8 0.7 fusion.93
  228.5 0.6 fusion.94
  229.2 2.4 constant_dynamic-slice_fusion.3
  231.6 1.7 copy.121
  233.3 1.8 reshape.314
  235.0 0.7 copy.122
  235.8 0.9 reshape.315
  236.7 0.6 bitcast_reduce_fusion.2
  237.3 0.5 copy-done.1
  237.8 0.7 fusion.93
  238.5 0.6 fusion.94
  239.2 1.0 divide_convert_fusion
  240.2 2.0 fusion.24
  (77 shorter events, 3.2 us)
Async XLA Ops:
  6.5 132.9 %copy-start = (bf16[512,1536]{1,0:T(8,128)(2,1)S(1)}, bf16[512,1536]{1,0:T(8,128)(2,1)}, u32[]{:S(2)}) copy-start(bf16[512,1536]{1,0:T(8,128)(2,1)} %param.23) | copy-start | bytes 4718596
  6.5 171.7 %all-gather.7.cloned.1.call-start = ((), (), s32[]{:S(2)}) async-start(), calls=%async_computation.1 | async-start | bytes 1671168 | tf_op jit(solution)/shard_map/all_gather | solution.py:162
  46.4 7.3 %collective-permute-start = (bf16[1,1,192,512]{3,2,1,0:T(8,128)(2,1)S(1)}, bf16[1,1,192,512]{3,2,1,0:T(8,128)(2,1)S(1)}, u32[]{:S(2)}, u32[]{:S(2)}) collective-permute-start(bf16[1,1,192,512]{3,2,1,0:T(8,128)(2,1)S(1)} %get-tuple-element.235), channel_id=1, source_target_pairs={{0,1},{1,2},{2,3},{3,4},{4,5},{5,6},{6,7},{7,8},{8,9},{9,10},{10,1... | collective-permute-start | bytes 589832 | tf_op jit(solution)/shard_map/ppermute | solution.py:22
  47.7 6.0 %collective-permute-start.1 = (bf16[1,1,192,512]{3,2,1,0:T(8,128)(2,1)S(1)}, bf16[1,1,192,512]{3,2,1,0:T(8,128)(2,1)S(1)}, u32[]{:S(2)}, u32[]{:S(2)}) collective-permute-start(bf16[1,1,192,512]{3,2,1,0:T(8,128)(2,1)S(1)} %get-tuple-element.236), channel_id=1, source_target_pairs={{1,0},{2,1},{3,2},{4,3},{5,4},{6,5},{7,6},{8,7},{9,8},{10,9},{11,1... | collective-permute-start | bytes 589832 | tf_op jit(solution)/shard_map/ppermute | solution.py:25
  53.8 2.3 copy-start.7
  53.8 2.3 copy-start.8
  90.6 3.7 %collective-permute-start.2 = (bf16[1,1,192,512]{3,2,1,0:T(8,128)(2,1)S(1)}, bf16[1,1,192,512]{3,2,1,0:T(8,128)(2,1)S(1)}, u32[]{:S(2)}, u32[]{:S(2)}) collective-permute-start(bf16[1,1,192,512]{3,2,1,0:T(8,128)(2,1)S(1)} %slice.88), channel_id=1, source_target_pairs={{0,1},{1,2},{2,3},{3,4},{4,5},{5,6},{6,7},{7,8},{8,9},{9,10},{10,1... | collective-permute-start | bytes 589832 | tf_op jit(solution)/shard_map/ppermute | solution.py:22
  92.6 3.6 %collective-permute-start.3 = (bf16[1,1,192,512]{3,1,2,0:T(2,128)(2,1)S(1)}, bf16[1,1,192,512]{3,1,2,0:T(2,128)(2,1)S(1)}, u32[]{:S(2)}, u32[]{:S(2)}) collective-permute-start(bf16[1,1,192,512]{3,1,2,0:T(2,128)(2,1)S(1)} %slice.91), channel_id=1, source_target_pairs={{1,0},{2,1},{3,2},{4,3},{5,4},{6,5},{7,6},{8,7},{9,8},{10,9},{11,1... | collective-permute-start | bytes 589832 | tf_op jit(solution)/shard_map/ppermute | solution.py:25
  102.5 1.0 copy-start.4
  104.4 37.4 %copy-start.5 = (f32[96,512]{1,0:T(8,128)}, f32[96,512]{1,0:T(8,128)S(1)}, u32[]{:S(2)}) copy-start(f32[96,512]{1,0:T(8,128)S(1)} %reduce_sum.173) | copy-start | bytes 589828
  141.1 78.0 %all-gather.5.cloned.1.call-start = ((), (), s32[]{:S(2)}) async-start(), calls=%async_computation | async-start | bytes 1671168 | tf_op jit(solution)/shard_map/all_gather | solution.py:161
  219.1 21.1 %copy-start.6 = (f32[512]{0:T(512)S(1)}, f32[512]{0:T(512)}, u32[]{:S(2)}) copy-start(f32[512]{0:T(512)} %param.25) | copy-start | bytes 6148
  226.6 1.1 copy-start.1
  226.6 1.2 copy-start.2
  228.5 0.7 copy-start.3
  236.6 1.1 copy-start.1
  236.6 1.2 copy-start.2
  238.5 0.7 copy-start.3
Sparse Core Ops, SparseCore 0:
  141.3 36.9 all-gather.6
  180.5 38.5 all-gather.4
where the time goes:
time: 250 us; the launch traced here: 249 us
  blocking collectives  99.9 us (40%)
  waiting for transfers between devices  78.6 us (31%)
  local copies, waits for them, and re-layouts  27.8 us (11%)
  between operations  15.2 us (6%)
  matrix products  12.7 us (5%)
  other arithmetic  9.37 us (4%)
  starting transfers between devices  5.41 us (2%)
    psum x3, blocking collectives, band_moments(): totals, squares = lax.psum((column_sums, column_squares), 'lat')  99.9 us
    all_gather x1, waiting for transfers between devices, local(): lax.all_gather(projected[:, :, :, 1], 'lat', axis=1, tiled=True)  40.9 us
    all_gather x1, waiting for transfers between devices, local(): lax.all_gather(projected[:, :, :, 2], 'lat', axis=1, tiled=True)  36.1 us
    dynamic_slice x4, local copies, waits for them, and re-layouts, key_span_step(): lax.dynamic_slice_in_dim(value_all, step_index * span_rows, span_rows, 1)  8.14 us
    conv_general_dilated x2, matrix products, convolve(): lax.conv_general_dilated(values, kernel, (1, 1), ((0, 0), (1, 1)), dimens...  6.59 us
    another operation x4, local copies, waits for them, and re-layouts  5.28 us
  transfers between devices with their start and end apart: 6, of which 3 were waited for; matrix products, arithmetic and copies ran while one was open for 2% of the time, Pallas kernels for 0%

commit v1 on v0

v1 whole, which is shorter than its diff:
```python
import functools
import math

import jax
import jax.numpy as jnp
from jax import lax
from jax.experimental import pallas as pl
from jax.experimental.pallas import tpu as pltpu
from jax.sharding import PartitionSpec as P

HEAD_DIM = 64
GROUPS = 32
FREQS = 64


eps = 1e-05
skip_gain = 0.7071067811865476


def noise_terms(noise_index, sigma_table, affine_weight):
    levels_count = sigma_table.shape[0]
    chosen = (noise_index[:, None] == jnp.arange(levels_count, dtype=jnp.int32)[None, :]).astype(
        jnp.float32
    )
    sigmas = jnp.sum(chosen * sigma_table[None, :], axis=1)
    log_level = jnp.log(sigmas) / 4.0
    frequency = jnp.exp(-math.log(10000.0) * jnp.arange(FREQS, dtype=jnp.float32) / FREQS)
    angles = log_level[:, None] * frequency[None, :]
    fourier = jnp.concatenate([jnp.cos(angles), jnp.sin(angles)], axis=1).astype(jnp.bfloat16)
    affine = jnp.dot(fourier, affine_weight, preferred_element_type=jnp.float32)
    channels = affine.shape[1] // 2
    return (affine[:, :channels], affine[:, channels:])


def shared_sum(vector):
    count = lax.axis_size("lat")
    sent = jnp.broadcast_to(vector[None, None, :], (count, 1, vector.shape[0]))
    return jnp.sum(lax.all_to_all(sent, "lat", 0, 0), axis=(0, 1))


def band_moments(values):
    members, height, breadth, channels = values.shape
    group_width = channels // GROUPS
    entries = height * breadth * group_width * lax.axis_size("lat")
    sums = jnp.sum(values, axis=(0, 1, 2)).reshape(GROUPS, group_width).sum(axis=1)
    squares = jnp.sum(jnp.square(values), axis=(0, 1, 2)).reshape(GROUPS, group_width).sum(axis=1)
    totals = shared_sum(jnp.concatenate([sums, squares, jnp.zeros((128 - 2 * GROUPS,), jnp.float32)]))
    center = totals[:GROUPS] / entries
    spread = totals[GROUPS : 2 * GROUPS] / entries - center * center
    return (center, spread)


def normalize(values, center, spread, norm_scale, norm_offset):
    group_width = values.shape[-1] // GROUPS
    center_full = jnp.repeat(center, group_width)
    factor_full = jnp.repeat(lax.rsqrt(spread + eps), group_width)
    return (values - center_full) * (factor_full * norm_scale) + norm_offset


def convolve(values, kernel):
    return lax.conv_general_dilated(
        values,
        kernel,
        (1, 1),
        ((0, 0), (1, 1)),
        dimension_numbers=("NHWC", "HWIO", "NHWC"),
        preferred_element_type=jnp.float32,
    )


def exchange(block, stride):
    count = lax.axis_size("lat")
    return lax.ppermute(block, "lat", [(i, i ^ stride) for i in range(count)])


def gather_blocks(block):
    count = lax.axis_size("lat")
    slow = [block] + [exchange(block, stride) for stride in range(4, count, 4)]
    wide = slow + [exchange(each, 2) for each in slow]
    return wide + [exchange(each, 1) for each in wide]


def group_total(rows):
    width = rows.shape[1]
    lane = lax.broadcasted_iota(jnp.int32, rows.shape, 1)
    step = 1
    while step < width // GROUPS:
        below = pltpu.roll(rows, step, 1)
        above = pltpu.roll(rows, width - step, 1)
        rows = rows + jnp.where((lane & step) != 0, below, above)
        step *= 2
    return rows


def attention_kernel(count, *refs):
    blocks = refs[:count]
    pooled, norm_gain, norm_bias, qkv_weight, proj_weight, proj_bias, out, keys, values = refs[count:]
    tokens, channels = pooled.shape
    group_width = channels // GROUPS
    sums = jnp.zeros((8, channels), jnp.float32)
    squares = jnp.zeros((8, channels), jnp.float32)
    for block in blocks:
        entry = block[...].astype(jnp.float32).reshape(tokens // 8, 8, channels)
        sums = sums + jnp.sum(entry, axis=0)
        squares = squares + jnp.sum(entry * entry, axis=0)
    sums = jnp.sum(sums, axis=0, keepdims=True)
    squares = jnp.sum(squares, axis=0, keepdims=True)
    row = lax.broadcasted_iota(jnp.int32, (8, channels), 0)
    moments = group_total(jnp.where(row == 0, sums, squares)) / (count * tokens * group_width)
    center = moments[0:1]
    spread = moments[1:2] - center * center
    factor = lax.rsqrt(spread + eps) * norm_gain[...]
    offset = norm_bias[...]

    def normed(entry):
        return ((entry.astype(jnp.float32) - center) * factor + offset).astype(jnp.bfloat16)

    for i, block in enumerate(blocks):
        projected = jnp.dot(
            normed(block[...]), qkv_weight[:, channels:], preferred_element_type=jnp.float32
        ).astype(jnp.bfloat16)
        keys[i * tokens : (i + 1) * tokens, :] = projected[:, :channels]
        values[i * tokens : (i + 1) * tokens, :] = projected[:, channels:]
    queries = jnp.dot(
        normed(pooled[...]), qkv_weight[:, :channels], preferred_element_type=jnp.float32
    ).astype(jnp.bfloat16) * jnp.bfloat16(HEAD_DIM ** (-0.5))
    first = lax.broadcasted_iota(jnp.int32, (tokens, 2 * HEAD_DIM), 1) < HEAD_DIM
    attended = []
    for start in range(0, channels, 2 * HEAD_DIM):
        pair = slice(start, start + 2 * HEAD_DIM)
        query = queries[:, pair]
        zero = jnp.zeros_like(query)
        both = jnp.concatenate([jnp.where(first, query, zero), jnp.where(first, zero, query)], axis=0)
        scores = lax.dot_general(
            both, keys[:, pair], (((1,), (1,)), ((), ())), preferred_element_type=jnp.float32
        )
        weights = jnp.exp(scores - jnp.max(scores, axis=1, keepdims=True))
        totals = jnp.sum(weights, axis=1, keepdims=True)
        blended = (
            jnp.dot(weights.astype(jnp.bfloat16), values[:, pair], preferred_element_type=jnp.float32)
            / totals
        )
        attended.append(jnp.where(first, blended[:tokens], blended[tokens:]).astype(jnp.bfloat16))
    projected = jnp.dot(
        jnp.concatenate(attended, axis=1), proj_weight[...], preferred_element_type=jnp.float32
    )
    out[...] = ((pooled[...] + projected + proj_bias[...]) * skip_gain).astype(jnp.bfloat16)


def attention(blocks, pooled, norm_gain, norm_bias, qkv_weight, proj_weight, proj_bias):
    tokens, channels = pooled.shape
    count = len(blocks)
    return pl.pallas_call(
        functools.partial(attention_kernel, count),
        out_shape=jax.ShapeDtypeStruct((tokens, channels), jnp.bfloat16),
        scratch_shapes=[
            pltpu.VMEM((count * tokens, channels), jnp.bfloat16),
            pltpu.VMEM((count * tokens, channels), jnp.bfloat16),
        ],
        compiler_params=pltpu.CompilerParams(vmem_limit_bytes=48 * 1024 * 1024),
    )(
        *blocks,
        pooled,
        norm_gain.reshape(1, channels),
        norm_bias.reshape(1, channels),
        qkv_weight,
        proj_weight,
        proj_bias.reshape(1, channels),
    )


def local(
    features,
    noise_index,
    sigma_table,
    affine_weight,
    norm_gain,
    norm_bias,
    conv1_weight,
    conv2_weight,
    conv_bias,
    qkv_weight,
    proj_weight,
    proj_bias,
):
    members, height, breadth, channels = features.shape
    count = lax.axis_size("lat")
    place = lax.axis_index("lat")
    below = lax.ppermute(features[:, -2:], "lat", [(i, i + 1) for i in range(count - 1)])
    above = lax.ppermute(features[:, :2], "lat", [(i + 1, i) for i in range(count - 1)])
    film_scale, film_shift = noise_terms(noise_index, sigma_table, affine_weight)
    source = features.astype(jnp.float32)
    center, spread = band_moments(source)

    def inside(rows):
        first = place * height - (rows - height) // 2
        row = first + jnp.arange(rows)
        return ((row >= 0) & (row < count * height))[None, :, None, None]

    wide = jnp.concatenate([below, features, above], axis=1).astype(jnp.float32)
    active = jax.nn.silu(normalize(wide, center, spread, norm_gain[0], norm_bias[0]))
    active = jnp.where(inside(height + 4), active, 0.0).astype(jnp.bfloat16)
    first_conv = convolve(active, conv1_weight) + conv_bias[0]
    center, spread = band_moments(first_conv[:, 1:-1])
    middle = jax.nn.silu(
        normalize(first_conv, center, spread, norm_gain[1], norm_bias[1]) * (1.0 + film_scale[0])
        + film_shift[0]
    )
    middle = jnp.where(inside(height + 2), middle, 0.0).astype(jnp.bfloat16)
    second_conv = convolve(middle, conv2_weight)
    level_one = ((source + second_conv + conv_bias[1]) * skip_gain).astype(jnp.bfloat16)
    level_one = lax.optimization_barrier(level_one)
    low_rows = height // 2
    breadth_low = breadth // 2
    pooled = jnp.mean(
        level_one.astype(jnp.float32).reshape(members, low_rows, 2, breadth_low, 2, channels),
        axis=(2, 4),
    ).reshape(low_rows * breadth_low, channels)
    blocks = gather_blocks(pooled.astype(jnp.bfloat16))
    out = attention(blocks, pooled, norm_gain[2], norm_bias[2], qkv_weight, proj_weight, proj_bias)
    return out.reshape(members, low_rows, breadth_low, channels)


def solution(mesh):
    return jax.shard_map(
        local,
        mesh=mesh,
        in_specs=(
            P("grp", "lat", None, None),
            P("grp"),
            P(),
            P(),
            P(),
            P(),
            P(),
            P(),
            P(),
            P(),
            P(),
            P(),
        ),
        out_specs=P("grp", "lat", None, None),
        check_vma=False,
    )
```

time: 250 us -> 106 us (0.42)
  blocking collectives: 99.9 us -> 0 us
  waiting for transfers between devices: 78.6 us -> 17.8 us
  matrix products: 12.7 us -> 42.3 us
  local copies, waits for them, and re-layouts: 27.8 us -> 4.01 us
  starting transfers between devices: 5.41 us -> 26.1 us
  between operations: 15.2 us -> 1.52 us
  Pallas kernels: 0 us -> 6.54 us
  other arithmetic: 9.37 us -> 6.78 us
    psum x3 -> x0, blocking collectives: 99.9 us -> none  [band_moments(): totals, squares = lax.psum((column_sums, column_squares), 'lat')]
    all_gather x2 -> x0, waiting for transfers between devices: 77 us -> none  [the longest x1 40.9 us: local(): lax.all_gather(projected[:, :, :, 1], 'lat', axis=1, tiled=True)]
    conv_general_dilated x2, matrix products: 6.59 us -> 42.1 us  [convolve(): lax.conv_general_dilated(values, kernel, (1, 1), ((0, 0), (1, 1)), dimens...]
    all_to_all x0 -> x2, starting transfers between devices: none -> 13.4 us  [shared_sum(): return jnp.sum(lax.all_to_all(sent, 'lat', 0, 0), axis=(0, 1))]
    dynamic_slice x6 -> x0, local copies, waits for them, and re-layouts: 9.6 us -> none  [the longest x4 8.14 us: key_span_step(): lax.dynamic_slice_in_dim(value_all, step_index * span_rows, span_rows, 1)]
    all_to_all x0 -> x2, waiting for transfers between devices: none -> 8.24 us  [shared_sum(): return jnp.sum(lax.all_to_all(sent, 'lat', 0, 0), axis=(0, 1))]
    ppermute x4 -> x17, waiting for transfers between devices: 1.54 us -> 9.53 us  [the longest x15 9.52 us: exchange(): return lax.ppermute(block, 'lat', [(i, i ^ stride) for i in range(count)])]
    ppermute x4 -> x17, starting transfers between devices: 5.37 us -> 12.8 us  [the longest x15 8.96 us: exchange(): return lax.ppermute(block, 'lat', [(i, i ^ stride) for i in range(count)])]
  transfers between devices with their start and end apart: 6 -> 19, of which waited for: 3 -> 9; matrix products, arithmetic and copies ran while one was open for 2% -> 5% of each run, Pallas kernels for 0% -> 0%
where the time goes in v1:
time: 106 us; the launch traced here: 105 us
  matrix products  42.3 us (40%)
  starting transfers between devices  26.1 us (25%)
  waiting for transfers between devices  17.8 us (17%)
  other arithmetic  6.78 us (6%)
  Pallas kernels  6.54 us (6%)
  local copies, waits for them, and re-layouts  4.01 us (4%)
  between operations  1.52 us (1%)
    conv_general_dilated x2, matrix products, convolve(): lax.conv_general_dilated(values, kernel, (1, 1), ((0, 0), (1, 1)), dimens...  42.1 us
    all_to_all x2, starting transfers between devices, shared_sum(): return jnp.sum(lax.all_to_all(sent, 'lat', 0, 0), axis=(0, 1))  13.4 us
    ppermute x15, waiting for transfers between devices, exchange(): return lax.ppermute(block, 'lat', [(i, i ^ stride) for i in range(count)])  9.52 us
    ppermute x15, starting transfers between devices, exchange(): return lax.ppermute(block, 'lat', [(i, i ^ stride) for i in range(count)])  8.96 us
    all_to_all x2, waiting for transfers between devices, shared_sum(): return jnp.sum(lax.all_to_all(sent, 'lat', 0, 0), axis=(0, 1))  8.24 us
    pallas_call x1, Pallas kernels, attention(): pl.pallas_call(functools.partial(attention_kernel, count), out_shape=jax....  6.54 us
    ppermute x1, starting transfers between devices, local(): lax.ppermute(features[:, -2:], 'lat', [(i, i + 1) for i in range(count -...  2.5 us
  transfers between devices with their start and end apart: 19, of which 9 were waited for; matrix products, arithmetic and copies ran while one was open for 5% of the time, Pallas kernels for 0%

profile of v1, /device:TPU:0, one launch (start us, length us, event | category | flops | bytes accessed | tf_op | source)
XLA Modules:
  0.0 105.0 jit_solution(7316254056399300690)
XLA Ops:
  0.0 2.5 %collective-permute-start = (bf16[1,2,192,512]{3,2,1,0:T(8,128)(2,1)}, bf16[1,2,192,512]{3,2,1,0:T(8,128)(2,1)S(1)}, u32[]{:S(2)}, u32[]{:S(2)}) collective-permute-start(bf16[1,2,192,512]{3,2,1,0:T(8,128)(2,1)} %param.12), channel_id=1, source_target_pairs={{0,1},{1,2},{2,3},{3,4},{4,5},{5,6},{6,7},{7,8},{8,9},{9,10},{10,1... | collective-permute-start | bytes 1179656 | tf_op jit(solution)/shard_map/ppermute | solution.py:189
  2.5 1.3 %collective-permute-start.1 = (bf16[1,2,192,512]{3,2,1,0:T(8,128)(2,1)}, bf16[1,2,192,512]{3,2,1,0:T(8,128)(2,1)S(1)}, u32[]{:S(2)}, u32[]{:S(2)}) collective-permute-start(bf16[1,2,192,512]{3,2,1,0:T(8,128)(2,1)} %param.12), channel_id=1, source_target_pairs={{1,0},{2,1},{3,2},{4,3},{5,4},{6,5},{7,6},{8,7},{9,8},{10,9},{11,1... | collective-permute-start | bytes 1179656 | tf_op jit(solution)/shard_map/ppermute | solution.py:190
  3.8 1.1 %convert_reduce_fusion = (f32[512]{0:T(512)S(1)}, f32[512]{0:T(512)S(1)}) fusion(bf16[1,2,192,512]{3,2,1,0:T(8,128)(2,1)} %param.12), kind=kLoop, calls=%fused_computation.9 | loop fusion | flops 785408 | bytes 397312 | tf_op jit(solution)/shard_map/reduce_sum | solution.py:45
  4.9 0.1 reshape.218
  5.0 0.1 reshape.219
  5.1 0.1 reduce_sum.116
  5.2 0.1 reduce_sum.118
  5.4 0.1 pad_maximum_fusion.1
  5.4 0.6 broadcast_in_dim.60
  6.0 9.3 %all-to-all-start = ((f32[16,1,128]{2,1,0:T(1,128)}), f32[16,1,128]{2,1,0:T(1,128)S(1)}, u32[]{:S(2)}, u32[]{:S(2)}) async-start(f32[16,1,128]{2,1,0:T(1,128)} %broadcast_in_dim.60), calls=%async_computation | async-start | bytes 16384 | tf_op jit(solution)/shard_map/all_to_all | solution.py:38
  15.3 0.8 fusion.16
  16.8 1.3 %fusion.8 = f32[]{:T(128)} fusion(f32[18]{0:T(128)} %param.14, s32[]{:T(128)} %bitcast.20), kind=kLoop, calls=%fused_computation.24 | loop fusion | flops 53 | bytes 80 | tf_op jit(solution)/shard_map/reduce_sum | solution.py:25
  18.6 0.1 sine_convert_fusion
  18.7 0.8 fusion.14
  19.5 0.2 fusion.9
  19.7 1.9 %all-to-all-done = f32[16,1,128]{2,1,0:T(1,128)S(1)} async-done(((f32[16,1,128]{2,1,0:T(1,128)}), f32[16,1,128]{2,1,0:T(1,128)S(1)}, u32[]{:S(2)}, u32[]{:S(2)}) %all-to-all-start) | async-done | bytes 8224 | tf_op jit(solution)/shard_map/all_to_all | solution.py:38
  21.7 0.1 slice_multiply_fusion.1
  21.8 0.1 broadcast_in_dim.62
  21.8 0.1 reshape.220
  21.9 0.1 broadcast_in_dim.61
  22.0 0.1 sub.42
  22.1 1.8 %select_convert_fusion = bf16[1,6,192,512]{3,2,1,0:T(8,128)(2,1)S(1)} fusion(bf16[1,2,192,512]{3,2,1,0:T(8,128)(2,1)S(1)} %collective-permute-done.1, bf16[1,2,192,512]{3,2,1,0:T(8,128)(2,1)} %param.12, bf16[1,2,192,512]{3,2,1,0:T(8,128)(2,1)S(1)} %collective-permute-done, f32[512]{0:T(512)S(1)} %bitcast.26, f32[512]{0:T(512)S(1)} %mul.102, f32[512]{0:T(512)S(1)} %sub.42, ...), kind=kLoop, calls=%fused_computation | loop fusion | flops 7077888 | bytes 2365446 | tf_op jit(solution)/shard_map/convert_element_type | solution.py:202
  23.9 28.0 %fusion = f32[1,4,192,512]{3,0,2,1:T(1,128)S(1)} fusion(bf16[3,3,512,512]{3,2,1,0:T(8,128)(2,1)} %param.18, bf16[1,6,192,512]{3,2,1,0:T(8,128)(2,1)S(1)} %select_convert_fusion), kind=kOutput, calls=%fused_computation.1 | convolution fusion | flops 3611295744 | bytes 7471104 | tf_op jit(solution)/shard_map/conv_general_dilated | solution.py:61
  52.0 0.2 copy_add_fusion
  52.2 0.1 slice_reduce_fusion
  52.3 0.1 reshape.221
  52.4 0.1 reduce_sum.121
  52.5 0.1 reshape.222
  52.6 0.1 reduce_sum.123
  52.7 0.1 pad_maximum_fusion
  52.8 0.6 broadcast_in_dim.64
  53.4 4.1 %all-to-all-start.1 = ((f32[16,1,128]{2,1,0:T(1,128)}), f32[16,1,128]{2,1,0:T(1,128)S(1)}, u32[]{:S(2)}, u32[]{:S(2)}) async-start(f32[16,1,128]{2,1,0:T(1,128)} %broadcast_in_dim.64), calls=%async_computation.1 | async-start | bytes 16384 | tf_op jit(solution)/shard_map/all_to_all | solution.py:38
  57.5 6.3 %all-to-all-done.1 = f32[16,1,128]{2,1,0:T(1,128)S(1)} async-done(((f32[16,1,128]{2,1,0:T(1,128)}), f32[16,1,128]{2,1,0:T(1,128)S(1)}, u32[]{:S(2)}, u32[]{:S(2)}) %all-to-all-start.1) | async-done | bytes 8224 | tf_op jit(solution)/shard_map/all_to_all | solution.py:38
  63.8 0.1 slice_multiply_fusion
  63.9 0.1 broadcast_in_dim.66
  64.0 0.1 reshape.223
  64.1 0.1 broadcast_in_dim.65
  64.1 0.1 sub.46
  64.2 0.7 select_convert_fusion.1
  64.9 0.0 copy-start.4
  64.9 14.1 %fusion.2 = f32[1,2,192,512]{3,0,2,1:T(1,128)S(1)} fusion(bf16[3,3,512,512]{3,2,1,0:T(8,128)(2,1)} %param.19, bf16[1,4,192,512]{3,2,1,0:T(8,128)(2,1)S(1)} %select_convert_fusion.1), kind=kOutput, calls=%fused_computation.5 | convolution fusion | flops 1805647872 | bytes 6291456 | tf_op jit(solution)/shard_map/conv_general_dilated | solution.py:61
  79.0 0.1 fusion.7
  79.2 0.1 convert_reduce_fusion.1
  79.2 0.2 reduce_sum.127
  79.5 0.5 reduce_sum.128
  80.0 0.6 collective-permute-start.2
  80.6 0.6 collective-permute-start.3
  81.2 3.3 %collective-permute-start.4 = (bf16[96,512]{1,0:T(8,128)(2,1)S(1)}, bf16[96,512]{1,0:T(8,128)(2,1)S(1)}, u32[]{:S(2)}, u32[]{:S(2)}) collective-permute-start(bf16[96,512]{1,0:T(8,128)(2,1)S(1)} %get-tuple-element.10.refs_0_), channel_id=1, source_target_pairs={{0,12},{1,13},{2,14},{3,15},{4,8},{5,9},{6,10},{7,11},{8,4},{9,5},... | collective-permute-start | bytes 294920 | tf_op jit(solution)/shard_map/ppermute | solution.py:73
  84.4 0.5 collective-permute-start.5
  84.9 0.7 collective-permute-done.2.refs_1_
  85.7 0.8 collective-permute-start.6
  86.5 4.5 %collective-permute-done.3.refs_2_ = bf16[96,512]{1,0:T(8,128)(2,1)S(1)} collective-permute-done((bf16[96,512]{1,0:T(8,128)(2,1)S(1)}, bf16[96,512]{1,0:T(8,128)(2,1)S(1)}, u32[]{:S(2)}, u32[]{:S(2)}) %collective-permute-start.3) | collective-permute-done | bytes 98336 | tf_op jit(solution)/shard_map/ppermute | solution.py:73
  91.0 0.6 collective-permute-start.7
  91.6 1.5 %collective-permute-start.8 = (bf16[96,512]{1,0:T(8,128)(2,1)S(1)}, bf16[96,512]{1,0:T(8,128)(2,1)S(1)}, u32[]{:S(2)}, u32[]{:S(2)}) collective-permute-start(bf16[96,512]{1,0:T(8,128)(2,1)S(1)} %collective-permute-done.4.refs_3_), channel_id=1, source_target_pairs={{0,2},{1,3},{2,0},{3,1},{4,6},{5,7},{6,4},{7,5},{8,10},{9,11},{10,... | collective-permute-start | bytes 294920 | tf_op jit(solution)/shard_map/ppermute | solution.py:73
  93.0 0.5 collective-permute-start.11
  93.5 0.1 collective-permute-start.12
  93.6 2.0 %collective-permute-done.7.refs_6_ = bf16[96,512]{1,0:T(8,128)(2,1)S(1)} collective-permute-done((bf16[96,512]{1,0:T(8,128)(2,1)S(1)}, bf16[96,512]{1,0:T(8,128)(2,1)S(1)}, u32[]{:S(2)}, u32[]{:S(2)}) %collective-permute-start.7) | collective-permute-done | bytes 98336 | tf_op jit(solution)/shard_map/ppermute | solution.py:73
  95.6 1.0 collective-permute-done.8.refs_7_
  96.7 0.5 collective-permute-start.15
  97.2 0.1 collective-permute-start.16
  97.3 0.7 collective-permute-done.14.refs_13_
  98.0 0.2 collective-permute-done.15.refs_14_
  98.1 0.4 collective-permute-done.16.refs_15_
  98.5 6.5 %shard_map.118 = bf16[96,512]{1,0:T(8,128)(2,1)} custom-call(bf16[96,512]{1,0:T(8,128)(2,1)S(1)} %get-tuple-element.10.refs_0_, bf16[96,512]{1,0:T(8,128)(2,1)S(1)} %collective-permute-done.2.refs_1_, bf16[96,512]{1,0:T(8,128)(2,1)S(1)} %collective-permute-done.3.refs_2_, bf16[96,512]{1,0:T(8,128)(2,1)S(1)} %collective-permute-done.4.refs_3_, ...), custom_call_target="tpu_custom_call" | custom-call | tf_op jit(solution)/shard_map/pallas_call | solution.py:153
  (32 shorter events, 0.2 us)
Async XLA Ops:
  0.0 19.5 %copy-start = (bf16[128,1024]{1,0:T(8,128)(2,1)S(1)}, bf16[128,1024]{1,0:T(8,128)(2,1)}, u32[]{:S(2)}) copy-start(bf16[128,1024]{1,0:T(8,128)(2,1)} %param.15) | copy-start | bytes 786436
  0.0 22.1 %collective-permute-start = (bf16[1,2,192,512]{3,2,1,0:T(8,128)(2,1)}, bf16[1,2,192,512]{3,2,1,0:T(8,128)(2,1)S(1)}, u32[]{:S(2)}, u32[]{:S(2)}) collective-permute-start(bf16[1,2,192,512]{3,2,1,0:T(8,128)(2,1)} %param.12), channel_id=1, source_target_pairs={{0,1},{1,2},{2,3},{3,4},{4,5},{5,6},{6,7},{7,8},{8,9},{9,10},{10,1... | collective-permute-start | bytes 1179656 | tf_op jit(solution)/shard_map/ppermute | solution.py:189
  2.5 19.6 %collective-permute-start.1 = (bf16[1,2,192,512]{3,2,1,0:T(8,128)(2,1)}, bf16[1,2,192,512]{3,2,1,0:T(8,128)(2,1)S(1)}, u32[]{:S(2)}, u32[]{:S(2)}) collective-permute-start(bf16[1,2,192,512]{3,2,1,0:T(8,128)(2,1)} %param.12), channel_id=1, source_target_pairs={{1,0},{2,1},{3,2},{4,3},{5,4},{6,5},{7,6},{8,7},{9,8},{10,9},{11,1... | collective-permute-start | bytes 1179656 | tf_op jit(solution)/shard_map/ppermute | solution.py:190
  6.0 15.6 %all-to-all-start = ((f32[16,1,128]{2,1,0:T(1,128)}), f32[16,1,128]{2,1,0:T(1,128)S(1)}, u32[]{:S(2)}, u32[]{:S(2)}) async-start(f32[16,1,128]{2,1,0:T(1,128)} %broadcast_in_dim.60), calls=%async_computation | async-start | bytes 16384 | tf_op jit(solution)/shard_map/all_to_all | solution.py:38
  53.4 10.4 %all-to-all-start.1 = ((f32[16,1,128]{2,1,0:T(1,128)}), f32[16,1,128]{2,1,0:T(1,128)S(1)}, u32[]{:S(2)}, u32[]{:S(2)}) async-start(f32[16,1,128]{2,1,0:T(1,128)} %broadcast_in_dim.64), calls=%async_computation.1 | async-start | bytes 16384 | tf_op jit(solution)/shard_map/all_to_all | solution.py:38
  64.9 14.1 %copy-start.4 = (bf16[1,2,192,512]{3,2,1,0:T(8,128)(2,1)S(1)}, bf16[1,2,192,512]{3,2,1,0:T(8,128)(2,1)}, u32[]{:S(2)}) copy-start(bf16[1,2,192,512]{3,2,1,0:T(8,128)(2,1)} %param.12) | copy-start | bytes 1179652
  79.1 19.3 %copy-start.1 = (bf16[512,1536]{1,0:T(8,128)(2,1)S(1)}, bf16[512,1536]{1,0:T(8,128)(2,1)}, u32[]{:S(2)}) copy-start(bf16[512,1536]{1,0:T(8,128)(2,1)} %refs_19_.1) | copy-start | bytes 4718596
  79.1 19.3 %copy-start.2 = (bf16[512,512]{1,0:T(8,128)(2,1)S(1)}, bf16[512,512]{1,0:T(8,128)(2,1)}, u32[]{:S(2)}) copy-start(bf16[512,512]{1,0:T(8,128)(2,1)} %refs_20_.1) | copy-start | bytes 1572868
  79.2 19.3 %copy-start.3 = (f32[512]{0:T(512)S(1)}, f32[512]{0:T(512)}, u32[]{:S(2)}) copy-start(f32[512]{0:T(512)} %param.23) | copy-start | bytes 6148
  80.0 5.7 %collective-permute-start.2 = (bf16[96,512]{1,0:T(8,128)(2,1)S(1)}, bf16[96,512]{1,0:T(8,128)(2,1)S(1)}, u32[]{:S(2)}, u32[]{:S(2)}) collective-permute-start(bf16[96,512]{1,0:T(8,128)(2,1)S(1)} %get-tuple-element.10.refs_0_), channel_id=1, source_target_pairs={{0,4},{1,5},{2,6},{3,7},{4,0},{5,1},{6,2},{7,3},{8,12},{9,13},{10,... | collective-permute-start | bytes 294920 | tf_op jit(solution)/shard_map/ppermute | solution.py:73
  80.6 10.4 %collective-permute-start.3 = (bf16[96,512]{1,0:T(8,128)(2,1)S(1)}, bf16[96,512]{1,0:T(8,128)(2,1)S(1)}, u32[]{:S(2)}, u32[]{:S(2)}) collective-permute-start(bf16[96,512]{1,0:T(8,128)(2,1)S(1)} %get-tuple-element.10.refs_0_), channel_id=1, source_target_pairs={{0,8},{1,9},{2,10},{3,11},{4,12},{5,13},{6,14},{7,15},{8,0},{9,1},... | collective-permute-start | bytes 294920 | tf_op jit(solution)/shard_map/ppermute | solution.py:73
  81.2 10.4 %collective-permute-start.4 = (bf16[96,512]{1,0:T(8,128)(2,1)S(1)}, bf16[96,512]{1,0:T(8,128)(2,1)S(1)}, u32[]{:S(2)}, u32[]{:S(2)}) collective-permute-start(bf16[96,512]{1,0:T(8,128)(2,1)S(1)} %get-tuple-element.10.refs_0_), channel_id=1, source_target_pairs={{0,12},{1,13},{2,14},{3,15},{4,8},{5,9},{6,10},{7,11},{8,4},{9,5},... | collective-permute-start | bytes 294920 | tf_op jit(solution)/shard_map/ppermute | solution.py:73
  84.4 8.6 %collective-permute-start.5 = (bf16[96,512]{1,0:T(8,128)(2,1)S(1)}, bf16[96,512]{1,0:T(8,128)(2,1)S(1)}, u32[]{:S(2)}, u32[]{:S(2)}) collective-permute-start(bf16[96,512]{1,0:T(8,128)(2,1)S(1)} %get-tuple-element.10.refs_0_), channel_id=1, source_target_pairs={{0,2},{1,3},{2,0},{3,1},{4,6},{5,7},{6,4},{7,5},{8,10},{9,11},{10,... | collective-permute-start | bytes 294920 | tf_op jit(solution)/shard_map/ppermute | solution.py:73
  84.9 8.1 %collective-permute-start.9 = (bf16[96,512]{1,0:T(8,128)(2,1)S(1)}, bf16[96,512]{1,0:T(8,128)(2,1)S(1)}, u32[]{:S(2)}, u32[]{:S(2)}) collective-permute-start(bf16[96,512]{1,0:T(8,128)(2,1)S(1)} %get-tuple-element.10.refs_0_), channel_id=1, source_target_pairs={{0,1},{1,0},{2,3},{3,2},{4,5},{5,4},{6,7},{7,6},{8,9},{9,8},{10,11... | collective-permute-start | bytes 294920 | tf_op jit(solution)/shard_map/ppermute | solution.py:73
  85.7 7.9 %collective-permute-start.6 = (bf16[96,512]{1,0:T(8,128)(2,1)S(1)}, bf16[96,512]{1,0:T(8,128)(2,1)S(1)}, u32[]{:S(2)}, u32[]{:S(2)}) collective-permute-start(bf16[96,512]{1,0:T(8,128)(2,1)S(1)} %collective-permute-done.2.refs_1_), channel_id=1, source_target_pairs={{0,2},{1,3},{2,0},{3,1},{4,6},{5,7},{6,4},{7,5},{8,10},{9,11},{10,... | collective-permute-start | bytes 294920 | tf_op jit(solution)/shard_map/ppermute | solution.py:73
  91.0 4.6 %collective-permute-start.7 = (bf16[96,512]{1,0:T(8,128)(2,1)S(1)}, bf16[96,512]{1,0:T(8,128)(2,1)S(1)}, u32[]{:S(2)}, u32[]{:S(2)}) collective-permute-start(bf16[96,512]{1,0:T(8,128)(2,1)S(1)} %collective-permute-done.3.refs_2_), channel_id=1, source_target_pairs={{0,2},{1,3},{2,0},{3,1},{4,6},{5,7},{6,4},{7,5},{8,10},{9,11},{10,... | collective-permute-start | bytes 294920 | tf_op jit(solution)/shard_map/ppermute | solution.py:73
  91.6 5.1 %collective-permute-start.8 = (bf16[96,512]{1,0:T(8,128)(2,1)S(1)}, bf16[96,512]{1,0:T(8,128)(2,1)S(1)}, u32[]{:S(2)}, u32[]{:S(2)}) collective-permute-start(bf16[96,512]{1,0:T(8,128)(2,1)S(1)} %collective-permute-done.4.refs_3_), channel_id=1, source_target_pairs={{0,2},{1,3},{2,0},{3,1},{4,6},{5,7},{6,4},{7,5},{8,10},{9,11},{10,... | collective-permute-start | bytes 294920 | tf_op jit(solution)/shard_map/ppermute | solution.py:73
  93.0 3.6 %collective-permute-start.10 = (bf16[96,512]{1,0:T(8,128)(2,1)S(1)}, bf16[96,512]{1,0:T(8,128)(2,1)S(1)}, u32[]{:S(2)}, u32[]{:S(2)}) collective-permute-start(bf16[96,512]{1,0:T(8,128)(2,1)S(1)} %collective-permute-done.2.refs_1_), channel_id=1, source_target_pairs={{0,1},{1,0},{2,3},{3,2},{4,5},{5,4},{6,7},{7,6},{8,9},{9,8},{10,11... | collective-permute-start | bytes 294920 | tf_op jit(solution)/shard_map/ppermute | solution.py:73
  93.0 4.1 %collective-permute-start.11 = (bf16[96,512]{1,0:T(8,128)(2,1)S(1)}, bf16[96,512]{1,0:T(8,128)(2,1)S(1)}, u32[]{:S(2)}, u32[]{:S(2)}) collective-permute-start(bf16[96,512]{1,0:T(8,128)(2,1)S(1)} %collective-permute-done.3.refs_2_), channel_id=1, source_target_pairs={{0,1},{1,0},{2,3},{3,2},{4,5},{5,4},{6,7},{7,6},{8,9},{9,8},{10,11... | collective-permute-start | bytes 294920 | tf_op jit(solution)/shard_map/ppermute | solution.py:73
  93.5 3.7 %collective-permute-start.12 = (bf16[96,512]{1,0:T(8,128)(2,1)S(1)}, bf16[96,512]{1,0:T(8,128)(2,1)S(1)}, u32[]{:S(2)}, u32[]{:S(2)}) collective-permute-start(bf16[96,512]{1,0:T(8,128)(2,1)S(1)} %collective-permute-done.4.refs_3_), channel_id=1, source_target_pairs={{0,1},{1,0},{2,3},{3,2},{4,5},{5,4},{6,7},{7,6},{8,9},{9,8},{10,11... | collective-permute-start | bytes 294920 | tf_op jit(solution)/shard_map/ppermute | solution.py:73
  95.6 1.6 %collective-permute-start.13 = (bf16[96,512]{1,0:T(8,128)(2,1)S(1)}, bf16[96,512]{1,0:T(8,128)(2,1)S(1)}, u32[]{:S(2)}, u32[]{:S(2)}) collective-permute-start(bf16[96,512]{1,0:T(8,128)(2,1)S(1)} %collective-permute-done.5.refs_4_), channel_id=1, source_target_pairs={{0,1},{1,0},{2,3},{3,2},{4,5},{5,4},{6,7},{7,6},{8,9},{9,8},{10,11... | collective-permute-start | bytes 294920 | tf_op jit(solution)/shard_map/ppermute | solution.py:73
  96.7 1.3 %collective-permute-start.14 = (bf16[96,512]{1,0:T(8,128)(2,1)S(1)}, bf16[96,512]{1,0:T(8,128)(2,1)S(1)}, u32[]{:S(2)}, u32[]{:S(2)}) collective-permute-start(bf16[96,512]{1,0:T(8,128)(2,1)S(1)} %collective-permute-done.6.refs_5_), channel_id=1, source_target_pairs={{0,1},{1,0},{2,3},{3,2},{4,5},{5,4},{6,7},{7,6},{8,9},{9,8},{10,11... | collective-permute-start | bytes 294920 | tf_op jit(solution)/shard_map/ppermute | solution.py:73
  96.7 1.5 %collective-permute-start.15 = (bf16[96,512]{1,0:T(8,128)(2,1)S(1)}, bf16[96,512]{1,0:T(8,128)(2,1)S(1)}, u32[]{:S(2)}, u32[]{:S(2)}) collective-permute-start(bf16[96,512]{1,0:T(8,128)(2,1)S(1)} %collective-permute-done.7.refs_6_), channel_id=1, source_target_pairs={{0,1},{1,0},{2,3},{3,2},{4,5},{5,4},{6,7},{7,6},{8,9},{9,8},{10,11... | collective-permute-start | bytes 294920 | tf_op jit(solution)/shard_map/ppermute | solution.py:73
  97.2 1.3 %collective-permute-start.16 = (bf16[96,512]{1,0:T(8,128)(2,1)S(1)}, bf16[96,512]{1,0:T(8,128)(2,1)S(1)}, u32[]{:S(2)}, u32[]{:S(2)}) collective-permute-start(bf16[96,512]{1,0:T(8,128)(2,1)S(1)} %collective-permute-done.8.refs_7_), channel_id=1, source_target_pairs={{0,1},{1,0},{2,3},{3,2},{4,5},{5,4},{6,7},{7,6},{8,9},{9,8},{10,11... | collective-permute-start | bytes 294920 | tf_op jit(solution)/shard_map/ppermute | solution.py:73

commit v2 on v1

--- a/solution.py
+++ b/solution.py
@@ -11,6 +11,8 @@
 HEAD_DIM = 64
 GROUPS = 32
 FREQS = 64
+GROUP_WIDTH = 16
+LANES = 128
 
 
 eps = 1e-05
@@ -27,69 +29,224 @@
     frequency = jnp.exp(-math.log(10000.0) * jnp.arange(FREQS, dtype=jnp.float32) / FREQS)
     angles = log_level[:, None] * frequency[None, :]
     fourier = jnp.concatenate([jnp.cos(angles), jnp.sin(angles)], axis=1).astype(jnp.bfloat16)
-    affine = jnp.dot(fourier, affine_weight, preferred_element_type=jnp.float32)
-    channels = affine.shape[1] // 2
-    return (affine[:, :channels], affine[:, channels:])
-
-
-def shared_sum(vector):
-    count = lax.axis_size("lat")
-    sent = jnp.broadcast_to(vector[None, None, :], (count, 1, vector.shape[0]))
-    return jnp.sum(lax.all_to_all(sent, "lat", 0, 0), axis=(0, 1))
-
-
-def band_moments(values):
-    members, height, breadth, channels = values.shape
-    group_width = channels // GROUPS
-    entries = height * breadth * group_width * lax.axis_size("lat")
-    sums = jnp.sum(values, axis=(0, 1, 2)).reshape(GROUPS, group_width).sum(axis=1)
-    squares = jnp.sum(jnp.square(values), axis=(0, 1, 2)).reshape(GROUPS, group_width).sum(axis=1)
-    totals = shared_sum(jnp.concatenate([sums, squares, jnp.zeros((128 - 2 * GROUPS,), jnp.float32)]))
-    center = totals[:GROUPS] / entries
-    spread = totals[GROUPS : 2 * GROUPS] / entries - center * center
-    return (center, spread)
-
-
-def normalize(values, center, spread, norm_scale, norm_offset):
-    group_width = values.shape[-1] // GROUPS
-    center_full = jnp.repeat(center, group_width)
-    factor_full = jnp.repeat(lax.rsqrt(spread + eps), group_width)
-    return (values - center_full) * (factor_full * norm_scale) + norm_offset
-
-
-def convolve(values, kernel):
-    return lax.conv_general_dilated(
-        values,
-        kernel,
-        (1, 1),
-        ((0, 0), (1, 1)),
-        dimension_numbers=("NHWC", "HWIO", "NHWC"),
-        preferred_element_type=jnp.float32,
-    )
-
-
-def exchange(block, stride):
-    count = lax.axis_size("lat")
-    return lax.ppermute(block, "lat", [(i, i ^ stride) for i in range(count)])
-
-
-def gather_blocks(block):
-    count = lax.axis_size("lat")
-    slow = [block] + [exchange(block, stride) for stride in range(4, count, 4)]
-    wide = slow + [exchange(each, 2) for each in slow]
-    return wide + [exchange(each, 1) for each in wide]
+    return jnp.dot(fourier, affine_weight, preferred_element_type=jnp.float32)
 
 
 def group_total(rows):
     width = rows.shape[1]
     lane = lax.broadcasted_iota(jnp.int32, rows.shape, 1)
     step = 1
-    while step < width // GROUPS:
+    while step < GROUP_WIDTH:
         below = pltpu.roll(rows, step, 1)
         above = pltpu.roll(rows, width - step, 1)
         rows = rows + jnp.where((lane & step) != 0, below, above)
         step *= 2
     return rows
+
+
+def packed_moments(sums, squares):
+    channels = sums.shape[1]
+    row = lax.broadcasted_iota(jnp.int32, (8, channels), 0)
+    totals = group_total(jnp.where(row == 0, sums, squares))
+    slot = lax.broadcasted_iota(jnp.int32, (1, LANES), 1) % GROUP_WIDTH
+    packed = jnp.zeros((1, LANES), jnp.float32)
+    for tile in range(channels // LANES):
+        for kind in range(2):
+            part = totals[kind : kind + 1, tile * LANES : (tile + 1) * LANES]
+            packed = jnp.where(slot == 2 * tile + kind, part, packed)
+    return packed
+
+
+def unpacked_moments(shared, entries, channels):
+    packed = jnp.sum(shared, axis=0, keepdims=True)
+    row = lax.broadcasted_iota(jnp.int32, (8, LANES), 0)
+    slot = lax.broadcasted_iota(jnp.int32, (8, LANES), 1) % GROUP_WIDTH
+    totals = group_total(jnp.where(row == slot, packed, 0.0)) / entries
+    tiles = channels // LANES
+    center = jnp.concatenate([totals[2 * tile : 2 * tile + 1] for tile in range(tiles)], axis=1)
+    second = jnp.concatenate([totals[2 * tile + 1 : 2 * tile + 2] for tile in range(tiles)], axis=1)
+    return center, second - center * center
+
+
+def column_sums(values):
+    rows, channels = values.shape
+    folded = values.reshape(rows // 8, 8, channels)
+    sums = jnp.sum(folded, axis=0)
+    squares = jnp.sum(folded * folded, axis=0)
+    return jnp.sum(sums, axis=0, keepdims=True), jnp.sum(squares, axis=0, keepdims=True)
+
+
+def silu(values):
+    return values / (1.0 + jnp.exp(-values))
+
+
+def shared(rows):
+    count, lanes = rows.shape
+    return lax.all_to_all(rows.reshape(count, 1, lanes), "lat", 0, 0).reshape(count, lanes)
+
+
+def moments_kernel(features, out):
+    sums, squares = column_sums(features[...].astype(jnp.float32))
+    out[...] = jnp.broadcast_to(packed_moments(sums, squares), out.shape)
+
+
+def moments(features):
+    return pl.pallas_call(
+        moments_kernel,
+        out_shape=jax.ShapeDtypeStruct((lax.axis_size("lat"), LANES), jnp.float32),
+    )(features)
+
+
+def shifted(line, breadth, lines, spread):
+    channels = line.shape[1]
+    lines[8 : 8 + breadth, :] = line
+    spread[:, channels : 2 * channels] = line.astype(jnp.bfloat16)
+    spread[:, :channels] = lines[7 : 7 + breadth, :].astype(jnp.bfloat16)
+    spread[:, 2 * channels :] = lines[9 : 9 + breadth, :].astype(jnp.bfloat16)
+
+
+def convolved(spread, weight, copies, first, rows, breadth):
+    total = None
+    for tap in range(3):
+        copies[tap].wait()
+        patch = spread[(first + tap) * breadth : (first + tap + rows) * breadth, :]
+        part = jnp.dot(patch, weight[tap], preferred_element_type=jnp.float32)
+        total = part if total is None else total + part
+    return total
+
+
+def weight_copies(source, weight, sems):
+    copies = [pltpu.make_async_copy(source.at[tap], weight.at[tap], sems.at[tap]) for tap in range(3)]
+    for each in copies:
+        each.start()
+    return copies
+
+
+def first_kernel(
+    height, breadth, below, own, above, sums, gain, bias, weight_hbm, conv_bias, out, packed, spread, lines, weight, sems
+):
+    count = lax.axis_size("lat")
+    place = lax.axis_index("lat")
+    channels = own.shape[1]
+    copies = weight_copies(weight_hbm, weight, sems)
+    lines[...] = jnp.zeros_like(lines)
+    center, variance = unpacked_moments(
+        sums[...], count * height * breadth * (channels // GROUPS), channels
+    )
+    factor = lax.rsqrt(variance + eps) * gain[...]
+    offset = bias[...]
+    for row in range(height + 4):
+        near = row - 2
+        if near < 0:
+            block, at = below, near + 2
+        elif near < height:
+            block, at = own, near
+        else:
+            block, at = above, near - height
+        values = block[at * breadth : (at + 1) * breadth, :].astype(jnp.float32)
+        values = silu((values - center) * factor + offset)
+        if near < 0:
+            values = jnp.where(place > 0, values, 0.0)
+        elif near >= height:
+            values = jnp.where(place < count - 1, values, 0.0)
+        shifted(values, breadth, lines, spread.at[row * breadth : (row + 1) * breadth, :])
+    result = convolved(spread, weight, copies, 0, height + 2, breadth) + conv_bias[...]
+    out[...] = result
+    total, squares = column_sums(result[breadth : (1 + height) * breadth])
+    packed[...] = jnp.broadcast_to(packed_moments(total, squares), packed.shape)
+
+
+def first_convolution(height, breadth, below, own, above, sums, gain, bias, weight, conv_bias):
+    channels = own.shape[1]
+    count = sums.shape[0]
+    plain = pl.BlockSpec(memory_space=pltpu.VMEM)
+    return pl.pallas_call(
+        functools.partial(first_kernel, height, breadth),
+        in_specs=[plain] * 6 + [pl.BlockSpec(memory_space=pl.ANY), plain],
+        out_shape=(
+            jax.ShapeDtypeStruct(((height + 2) * breadth, channels), jnp.float32),
+            jax.ShapeDtypeStruct((count, LANES), jnp.float32),
+        ),
+        scratch_shapes=[
+            pltpu.VMEM(((height + 4) * breadth, 3 * channels), jnp.bfloat16),
+            pltpu.VMEM((breadth + 16, channels), jnp.float32),
+            pltpu.VMEM((3, 3 * channels, channels), jnp.bfloat16),
+            pltpu.SemaphoreType.DMA((3,)),
+        ],
+        compiler_params=pltpu.CompilerParams(vmem_limit_bytes=40 * 1024 * 1024),
+    )(below, own, above, sums, gain, bias, weight.reshape(3, 3 * channels, channels), conv_bias)
+
+
+def second_kernel(
+    height, breadth, first, own, sums, gain, bias, film, weight_hbm, conv_bias, pooled, sent, spread, lines, pairs, weight, sems
+):
+    count = lax.axis_size("lat")
+    place = lax.axis_index("lat")
+    channels = own.shape[1]
+    copies = weight_copies(weight_hbm, weight, sems)
+    lines[...] = jnp.zeros_like(lines)
+    center, variance = unpacked_moments(
+        sums[...], count * height * breadth * (channels // GROUPS), channels
+    )
+    factor = lax.rsqrt(variance + eps) * gain[...]
+    offset = bias[...]
+    scale = 1.0 + film[:, :channels]
+    shift = film[:, channels:]
+    for row in range(height + 2):
+        values = first[row * breadth : (row + 1) * breadth, :]
+        values = silu(((values - center) * factor + offset) * scale + shift)
+        if row == 0:
+            values = jnp.where(place > 0, values, 0.0)
+        elif row == height + 1:
+            values = jnp.where(place < count - 1, values, 0.0)
+        shifted(values, breadth, lines, spread.at[row * breadth : (row + 1) * breadth, :])
+    result = convolved(spread, weight, copies, 0, height, breadth)
+    level = ((own[...].astype(jnp.float32) + result + conv_bias[...]) * skip_gain).astype(jnp.bfloat16)
+    level = level.astype(jnp.float32)
+    half = breadth // 2
+    for row in range(height // 2):
+        start = 2 * row * breadth
+        both = level[start : start + breadth] + level[start + breadth : start + 2 * breadth]
+        for tile in range(channels // LANES):
+            lanes = slice(tile * LANES, (tile + 1) * LANES)
+            pairs[...] = both[:, lanes]
+            mean = (pairs[pl.ds(0, half, stride=2), :] + pairs[pl.ds(1, half, stride=2), :]) * 0.25
+            pooled[row * half : (row + 1) * half, lanes] = mean
+            sent[row * half : (row + 1) * half, lanes] = mean.astype(jnp.bfloat16)
+
+
+def second_convolution(height, breadth, first, own, sums, gain, bias, film, weight, conv_bias):
+    channels = own.shape[1]
+    tokens = (height // 2) * (breadth // 2)
+    plain = pl.BlockSpec(memory_space=pltpu.VMEM)
+    return pl.pallas_call(
+        functools.partial(second_kernel, height, breadth),
+        in_specs=[plain] * 6 + [pl.BlockSpec(memory_space=pl.ANY), plain],
+        out_shape=(
+            jax.ShapeDtypeStruct((tokens, channels), jnp.float32),
+            jax.ShapeDtypeStruct((tokens, channels), jnp.bfloat16),
+        ),
+        scratch_shapes=[
+            pltpu.VMEM(((height + 2) * breadth, 3 * channels), jnp.bfloat16),
+            pltpu.VMEM((breadth + 16, channels), jnp.float32),
+            pltpu.VMEM((breadth, LANES), jnp.float32),
+            pltpu.VMEM((3, 3 * channels, channels), jnp.bfloat16),
+            pltpu.SemaphoreType.DMA((3,)),
+        ],
+        compiler_params=pltpu.CompilerParams(vmem_limit_bytes=40 * 1024 * 1024),
+    )(first, own, sums, gain, bias, film, weight.reshape(3, 3 * channels, channels), conv_bias)
+
+
+def exchange(block, stride):
+    count = lax.axis_size("lat")
+    return lax.ppermute(block, "lat", [(i, i ^ stride) for i in range(count)])
+
+
+def gather_blocks(block):
+    count = lax.axis_size("lat")
+    slow = [block] + [exchange(block, stride) for stride in range(4, count, 4)]
+    wide = slow + [exchange(each, 2) for each in slow]
+    return wide + [exchange(each, 1) for each in wide]
 
 
 def attention_kernel(count, *refs):
@@ -185,40 +342,23 @@
 ):
     members, height, breadth, channels = features.shape
     count = lax.axis_size("lat")
-    place = lax.axis_index("lat")
     below = lax.ppermute(features[:, -2:], "lat", [(i, i + 1) for i in range(count - 1)])
     above = lax.ppermute(features[:, :2], "lat", [(i + 1, i) for i in range(count - 1)])
-    film_scale, film_shift = noise_terms(noise_index, sigma_table, affine_weight)
-    source = features.astype(jnp.float32)
-    center, spread = band_moments(source)
-
-    def inside(rows):
-        first = place * height - (rows - height) // 2
-        row = first + jnp.arange(rows)
-        return ((row >= 0) & (row < count * height))[None, :, None, None]
-
-    wide = jnp.concatenate([below, features, above], axis=1).astype(jnp.float32)
-    active = jax.nn.silu(normalize(wide, center, spread, norm_gain[0], norm_bias[0]))
-    active = jnp.where(inside(height + 4), active, 0.0).astype(jnp.bfloat16)
-    first_conv = convolve(active, conv1_weight) + conv_bias[0]
-    center, spread = band_moments(first_conv[:, 1:-1])
-    middle = jax.nn.silu(
-        normalize(first_conv, center, spread, norm_gain[1], norm_bias[1]) * (1.0 + film_scale[0])
-        + film_shift[0]
-    )
-    middle = jnp.where(inside(height + 2), middle, 0.0).astype(jnp.bfloat16)
-    second_conv = convolve(middle, conv2_weight)
-    level_one = ((source + second_conv + conv_bias[1]) * skip_gain).astype(jnp.bfloat16)
-    level_one = lax.optimization_barrier(level_one)
-    low_rows = height // 2
-    breadth_low = breadth // 2
-    pooled = jnp.mean(
-        level_one.astype(jnp.float32).reshape(members, low_rows, 2, breadth_low, 2, channels),
-        axis=(2, 4),
-    ).reshape(low_rows * breadth_low, channels)
-    blocks = gather_blocks(pooled.astype(jnp.bfloat16))
+    film = noise_terms(noise_index, sigma_table, affine_weight)
+    own = features.reshape(height * breadth, channels)
+    below = below.reshape(2 * breadth, channels)
+    above = above.reshape(2 * breadth, channels)
+    sums = shared(moments(own))
+    first, packed = first_convolution(
+        height, breadth, below, own, above, sums, norm_gain[0:1], norm_bias[0:1], conv1_weight, conv_bias[0:1]
+    )
+    sums = shared(packed)
+    pooled, sent = second_convolution(
+        height, breadth, first, own, sums, norm_gain[1:2], norm_bias[1:2], film, conv2_weight, conv_bias[1:2]
+    )
+    blocks = gather_blocks(sent)
     out = attention(blocks, pooled, norm_gain[2], norm_bias[2], qkv_weight, proj_weight, proj_bias)
-    return out.reshape(members, low_rows, breadth_low, channels)
+    return out.reshape(members, height // 2, breadth // 2, channels)
 
 
 def solution(mesh):

time: 106 us -> 82.9 us (0.78)
  matrix products: 42.3 us -> 0.87 us
  Pallas kernels: 6.54 us -> 19.2 us
  local copies, waits for them, and re-layouts: 4.01 us -> 15.7 us
  other arithmetic: 6.78 us -> 1.91 us
  waiting for transfers between devices: 17.8 us -> 15.3 us
  starting transfers between devices: 26.1 us -> 27.8 us
    conv_general_dilated x2 -> x0, matrix products: 42.1 us -> none  [convolve(): lax.conv_general_dilated(values, kernel, (1, 1), ((0, 0), (1, 1)), dimens...]
    unnamed x10 -> x34, local copies, waits for them, and re-layouts: 0.03 us -> 12.9 us
    pallas_call x0 -> x3, Pallas kernels: none -> 12.7 us  [the longest x1 6.57 us: first_convolution(): pl.pallas_call(functools.partial(first_kernel, height, breadth), in_specs...]
    convert_element_type x3 -> x0, other arithmetic: 2.62 us -> none  [the longest x1 1.83 us: local(): active = jnp.where(inside(height + 4), active, 0.0).astype(jnp.bfloat16)]
    all_to_all x2, waiting for transfers between devices: 8.24 us -> 5.82 us  [shared(): lax.all_to_all(rows.reshape(count, 1, lanes), 'lat', 0, 0)]
    reduce_sum x10 -> x0, other arithmetic: 2.29 us -> none  [the longest x4 1.49 us: band_moments(): jnp.sum(values, axis=(0, 1, 2)).reshape(GROUPS, group_width).sum(axis=1)]
    all_to_all x2, starting transfers between devices: 13.4 us -> 15.1 us  [shared(): lax.all_to_all(rows.reshape(count, 1, lanes), 'lat', 0, 0)]
    broadcast_in_dim x6 -> x0, local copies, waits for them, and re-layouts: 1.51 us -> none  [the longest x2 1.23 us: shared_sum(): sent = jnp.broadcast_to(vector[None, None, :], (count, 1, vector.shape[0]))]
  transfers between devices with their start and end apart: 19 -> 19, of which waited for: 9 -> 9; matrix products, arithmetic and copies ran while one was open for 5% -> 7% of each run, Pallas kernels for 0% -> 2%
where the time goes in v2:
time: 82.9 us; the launch traced here: 82.2 us
  starting transfers between devices  27.8 us (34%)
  Pallas kernels  19.2 us (23%)
  local copies, waits for them, and re-layouts  15.7 us (19%)
  waiting for transfers between devices  15.3 us (18%)
  other arithmetic  1.91 us (2%)
  between operations  1.38 us (2%)
  matrix products  0.87 us (1%)
    all_to_all x2, starting transfers between devices, shared(): lax.all_to_all(rows.reshape(count, 1, lanes), 'lat', 0, 0)  15.1 us
    unnamed x34, local copies, waits for them, and re-layouts  12.9 us
    ppermute x15, waiting for transfers between devices, exchange(): return lax.ppermute(block, 'lat', [(i, i ^ stride) for i in range(count)])  9.52 us
    ppermute x15, starting transfers between devices, exchange(): return lax.ppermute(block, 'lat', [(i, i ^ stride) for i in range(count)])  8.96 us
    pallas_call x1, Pallas kernels, first_convolution(): pl.pallas_call(functools.partial(first_kernel, height, breadth), in_specs...  6.57 us
    pallas_call x1, Pallas kernels, attention(): pl.pallas_call(functools.partial(attention_kernel, count), out_shape=jax....  6.52 us
    all_to_all x2, waiting for transfers between devices, shared(): lax.all_to_all(rows.reshape(count, 1, lanes), 'lat', 0, 0)  5.82 us
    pallas_call x1, Pallas kernels, second_convolution(): pl.pallas_call(functools.partial(second_kernel, height, breadth), in_spec...  4.14 us
  transfers between devices with their start and end apart: 19, of which 9 were waited for; matrix products, arithmetic and copies ran while one was open for 7% of the time, Pallas kernels for 2%

profile of v2, /device:TPU:0, one launch (start us, length us, event | category | flops | bytes accessed | tf_op | source)
XLA Modules:
  0.0 82.2 jit_solution(14415323336451200234)
XLA Ops:
  0.0 0.0 copy-start
  0.0 2.5 %collective-permute-start = (bf16[1,2,192,512]{3,2,1,0:T(8,128)(2,1)}, bf16[1,2,192,512]{3,2,1,0:T(8,128)(2,1)S(1)}, u32[]{:S(2)}, u32[]{:S(2)}) collective-permute-start(bf16[1,2,192,512]{3,2,1,0:T(8,128)(2,1)} %param.12), channel_id=1, source_target_pairs={{0,1},{1,2},{2,3},{3,4},{4,5},{5,6},{6,7},{7,8},{8,9},{9,10},{10,1... | collective-permute-start | bytes 1179656 | tf_op jit(solution)/shard_map/ppermute | solution.py:345
  2.5 1.3 %collective-permute-start.1 = (bf16[1,2,192,512]{3,2,1,0:T(8,128)(2,1)}, bf16[1,2,192,512]{3,2,1,0:T(8,128)(2,1)S(1)}, u32[]{:S(2)}, u32[]{:S(2)}) collective-permute-start(bf16[1,2,192,512]{3,2,1,0:T(8,128)(2,1)} %param.12), channel_id=1, source_target_pairs={{1,0},{2,1},{3,2},{4,3},{5,4},{6,5},{7,6},{8,7},{9,8},{10,9},{11,1... | collective-permute-start | bytes 1179656 | tf_op jit(solution)/shard_map/ppermute | solution.py:346
  3.8 2.0 %shard_map.118 = f32[16,128]{1,0:T(8,128)} custom-call(bf16[384,512]{1,0:T(8,128)(2,1)} %bitcast.24), custom_call_target="tpu_custom_call" | custom-call | tf_op jit(solution)/shard_map/pallas_call | solution.py:94
  5.8 9.3 %all-to-all-start = ((f32[16,1,128]{2,1,0:T(1,128)}), f32[16,1,128]{2,1,0:T(1,128)S(1)}, u32[]{:S(2)}, u32[]{:S(2)}) async-start(f32[16,1,128]{2,1,0:T(1,128)} %bitcast.33), calls=%async_computation | async-start | bytes 16384 | tf_op jit(solution)/shard_map/all_to_all | solution.py:85
  15.1 1.4 %fusion.7 = (f32[1,512]{1,0:T(1,128)}, f32[1,512]{1,0:T(1,128)}) fusion(f32[2,512]{1,0:T(2,128)} %param.20), kind=kLoop, calls=%fused_computation.12 | loop fusion | bytes 8192 | tf_op jit(solution)/shard_map/slice | solution.py:357
  17.1 1.3 %fusion = f32[]{:T(128)} fusion(f32[18]{0:T(128)} %param.14, s32[]{:T(128)} %bitcast.21), kind=kLoop, calls=%fused_computation.1 | loop fusion | flops 53 | bytes 80 | tf_op jit(solution)/shard_map/reduce_sum | solution.py:27
  19.0 1.4 %fusion.5 = (f32[1,512]{1,0:T(1,128)S(1)}, f32[1,512]{1,0:T(1,128)}, f32[1,512]{1,0:T(1,128)}, f32[1,512]{1,0:T(1,128)}, f32[1,512]{1,0:T(1,128)}, /*index=5*/f32[1,512]{1,0:T(1,128)S(1)}) fusion(f32[3,512]{1,0:T(4,128)} %param.17, f32[3,512]{1,0:T(4,128)} %param.16), kind=kLoop, calls=%fused_computation.10 | loop fusion | bytes 24576 | tf_op jit(solution)/shard_map/slice | solution.py:360
  20.4 0.6 sine_convert_fusion
  21.0 0.4 all-to-all-done
  21.4 0.0 collective-permute-done
  21.4 0.0 collective-permute-done.1
  21.4 2.3 %copy-done.1 = bf16[3,3,512,512]{3,2,1,0:T(8,128)(2,1)S(1)} copy-done((bf16[3,3,512,512]{3,2,1,0:T(8,128)(2,1)S(1)}, bf16[3,3,512,512]{3,2,1,0:T(8,128)(2,1)}, u32[]{:S(2)}) %copy-start.1) | copy-done | bytes 4718616
  23.8 1.0 %copy-done.3 = bf16[1,2,192,512]{3,2,1,0:T(8,128)(2,1)S(1)} copy-done((bf16[1,2,192,512]{3,2,1,0:T(8,128)(2,1)S(1)}, bf16[1,2,192,512]{3,2,1,0:T(8,128)(2,1)}, u32[]{:S(2)}) %copy-start.3) | copy-done | bytes 393240
  24.8 0.7 copy-done.11
  25.4 0.7 copy-done.12
  26.1 0.7 copy-done.14
  26.8 6.6 %shard_map.119 = (f32[768,512]{1,0:T(8,128)S(1)}, f32[16,128]{1,0:T(8,128)S(1)}) custom-call(bf16[384,512]{1,0:T(8,128)(2,1)S(1)} %bitcast.27, bf16[384,512]{1,0:T(8,128)(2,1)S(1)} %bitcast.25, bf16[384,512]{1,0:T(8,128)(2,1)S(1)} %bitcast.28, f32[16,128]{1,0:T(8,128)S(1)} %bitcast.29, f32[1,512]{1,0:T(1,128)S(1)} %copy-done.12, f32[1,512]{1,0:T(1,128)S(1)} %copy-done.11, ...), custom_call_target="tpu_custom_call" | custom-call | tf_op jit(solution)/shard_map/pallas_call | solution.py:163
  33.3 0.0 copy-start.6
  33.3 1.2 %copy-done.6 = f32[768,512]{1,0:T(8,128)} copy-done((f32[768,512]{1,0:T(8,128)}, f32[768,512]{1,0:T(8,128)S(1)}, u32[]{:S(2)}) %copy-start.6) | copy-done | bytes 1572888
  34.5 0.6 copy-done.15
  35.1 5.8 %all-to-all-start.1 = ((f32[16,1,128]{2,1,0:T(1,128)}), f32[16,1,128]{2,1,0:T(1,128)S(1)}, u32[]{:S(2)}, u32[]{:S(2)}) async-start(f32[16,1,128]{2,1,0:T(1,128)} %bitcast.31), calls=%async_computation.1 | async-start | bytes 16384 | tf_op jit(solution)/shard_map/all_to_all | solution.py:85
  40.9 0.0 copy-done
  40.9 0.9 %fusion.1.film = f32[1,1024]{1,0:T(1,128)S(1)} fusion(bf16[128,1024]{1,0:T(8,128)(2,1)S(1)} %copy-done, bf16[64]{0:T(256)(128)(2,1)} %get-tuple-element.24, bf16[64]{0:T(256)(128)(2,1)} %get-tuple-element.25), kind=kOutput, calls=%fused_computation.3 | convolution fusion | flops 262656 | bytes 266496 | tf_op jit(solution)/shard_map/dot_general | solution.py:32
  41.8 5.4 %all-to-all-done.1 = f32[16,1,128]{2,1,0:T(1,128)S(1)} async-done(((f32[16,1,128]{2,1,0:T(1,128)}), f32[16,1,128]{2,1,0:T(1,128)S(1)}, u32[]{:S(2)}, u32[]{:S(2)}) %all-to-all-start.1) | async-done | bytes 8224 | tf_op jit(solution)/shard_map/all_to_all | solution.py:85
  47.3 0.0 copy-done.4
  47.3 2.3 %copy-done.2 = bf16[3,3,512,512]{3,2,1,0:T(8,128)(2,1)S(1)} copy-done((bf16[3,3,512,512]{3,2,1,0:T(8,128)(2,1)S(1)}, bf16[3,3,512,512]{3,2,1,0:T(8,128)(2,1)}, u32[]{:S(2)}) %copy-start.2) | copy-done | bytes 4718616
  49.6 1.4 %copy-done.7 = f32[768,512]{1,0:T(8,128)S(1)} copy-done((f32[768,512]{1,0:T(8,128)S(1)}, f32[768,512]{1,0:T(8,128)}, u32[]{:S(2)}) %copy-start.7) | copy-done | bytes 1572888
  51.0 0.7 copy-done.9
  51.7 0.7 copy-done.10
  52.4 0.7 copy-done.13
  53.0 4.1 %shard_map.120 = (f32[96,512]{1,0:T(8,128)S(1)}, bf16[96,512]{1,0:T(8,128)(2,1)S(1)}) custom-call(f32[768,512]{1,0:T(8,128)S(1)} %copy-done.7, bf16[384,512]{1,0:T(8,128)(2,1)S(1)} %bitcast.26, f32[16,128]{1,0:T(8,128)S(1)} %bitcast.30, f32[1,512]{1,0:T(1,128)S(1)} %copy-done.10, f32[1,512]{1,0:T(1,128)S(1)} %copy-done.9, f32[1,1024]{1,0:T(1,128)S(1)} %fusion.1.film, ...), custom_call_target="tpu_custom_call" | custom-call | tf_op jit(solution)/shard_map/pallas_call | solution.py:222
  57.2 0.6 collective-permute-start.2
  57.8 0.6 collective-permute-start.3
  58.4 3.3 %collective-permute-start.4 = (bf16[96,512]{1,0:T(8,128)(2,1)S(1)}, bf16[96,512]{1,0:T(8,128)(2,1)S(1)}, u32[]{:S(2)}, u32[]{:S(2)}) collective-permute-start(bf16[96,512]{1,0:T(8,128)(2,1)S(1)} %get-tuple-element.11.refs_0_), channel_id=1, source_target_pairs={{0,12},{1,13},{2,14},{3,15},{4,8},{5,9},{6,10},{7,11},{8,4},{9,5},... | collective-permute-start | bytes 294920 | tf_op jit(solution)/shard_map/ppermute | solution.py:242
  61.6 0.5 collective-permute-start.5
  62.1 0.0 collective-permute-start.9
  62.1 0.7 collective-permute-done.2.refs_1_
  62.9 0.8 collective-permute-start.6
  63.7 4.5 %collective-permute-done.3.refs_2_ = bf16[96,512]{1,0:T(8,128)(2,1)S(1)} collective-permute-done((bf16[96,512]{1,0:T(8,128)(2,1)S(1)}, bf16[96,512]{1,0:T(8,128)(2,1)S(1)}, u32[]{:S(2)}, u32[]{:S(2)}) %collective-permute-start.3) | collective-permute-done | bytes 98336 | tf_op jit(solution)/shard_map/ppermute | solution.py:242
  68.2 0.6 collective-permute-start.7
  68.8 0.0 collective-permute-done.4.refs_3_
  68.8 1.4 %collective-permute-start.8 = (bf16[96,512]{1,0:T(8,128)(2,1)S(1)}, bf16[96,512]{1,0:T(8,128)(2,1)S(1)}, u32[]{:S(2)}, u32[]{:S(2)}) collective-permute-start(bf16[96,512]{1,0:T(8,128)(2,1)S(1)} %collective-permute-done.4.refs_3_), channel_id=1, source_target_pairs={{0,2},{1,3},{2,0},{3,1},{4,6},{5,7},{6,4},{7,5},{8,10},{9,11},{10,... | collective-permute-start | bytes 294920 | tf_op jit(solution)/shard_map/ppermute | solution.py:242
  70.2 0.0 collective-permute-done.5.refs_4_
  70.2 0.0 collective-permute-start.10
  70.2 0.0 collective-permute-done.9.refs_8_
  70.2 0.5 collective-permute-start.11
  70.7 0.0 collective-permute-done.6.refs_5_
  70.7 0.1 collective-permute-start.12
  70.8 2.0 %collective-permute-done.7.refs_6_ = bf16[96,512]{1,0:T(8,128)(2,1)S(1)} collective-permute-done((bf16[96,512]{1,0:T(8,128)(2,1)S(1)}, bf16[96,512]{1,0:T(8,128)(2,1)S(1)}, u32[]{:S(2)}, u32[]{:S(2)}) %collective-permute-start.7) | collective-permute-done | bytes 98336 | tf_op jit(solution)/shard_map/ppermute | solution.py:242
  72.8 0.0 collective-permute-start.13
  72.8 1.0 %collective-permute-done.8.refs_7_ = bf16[96,512]{1,0:T(8,128)(2,1)S(1)} collective-permute-done((bf16[96,512]{1,0:T(8,128)(2,1)S(1)}, bf16[96,512]{1,0:T(8,128)(2,1)S(1)}, u32[]{:S(2)}, u32[]{:S(2)}) %collective-permute-start.8) | collective-permute-done | bytes 98336 | tf_op jit(solution)/shard_map/ppermute | solution.py:242
  73.9 0.0 collective-permute-start.14
  73.9 0.0 collective-permute-done.10.refs_9_
  73.9 0.5 collective-permute-start.15
  74.4 0.0 collective-permute-done.11.refs_10_
  74.4 0.1 collective-permute-start.16
  74.4 0.0 collective-permute-done.12.refs_11_
  74.4 0.0 collective-permute-done.13.refs_12_
  74.4 0.7 collective-permute-done.14.refs_13_
  75.2 0.2 collective-permute-done.15.refs_14_
  75.3 0.4 collective-permute-done.16.refs_15_
  75.7 0.0 copy-done.5
  75.7 6.5 %shard_map.121 = bf16[96,512]{1,0:T(8,128)(2,1)} custom-call(bf16[96,512]{1,0:T(8,128)(2,1)S(1)} %get-tuple-element.11.refs_0_, bf16[96,512]{1,0:T(8,128)(2,1)S(1)} %collective-permute-done.2.refs_1_, bf16[96,512]{1,0:T(8,128)(2,1)S(1)} %collective-permute-done.3.refs_2_, bf16[96,512]{1,0:T(8,128)(2,1)S(1)} %collective-permute-done.4.refs_3_, ...), custom_call_target="tpu_custom_call" | custom-call | tf_op jit(solution)/shard_map/pallas_call | solution.py:310
  (17 shorter events, 0.0 us)
Async XLA Ops:
  0.0 40.9 %copy-start = (bf16[128,1024]{1,0:T(8,128)(2,1)S(1)}, bf16[128,1024]{1,0:T(8,128)(2,1)}, u32[]{:S(2)}) copy-start(bf16[128,1024]{1,0:T(8,128)(2,1)} %param.15) | copy-start | bytes 786436
  0.0 47.3 %copy-start.4 = (bf16[1,2,192,512]{3,2,1,0:T(8,128)(2,1)S(1)}, bf16[1,2,192,512]{3,2,1,0:T(8,128)(2,1)}, u32[]{:S(2)}) copy-start(bf16[1,2,192,512]{3,2,1,0:T(8,128)(2,1)} %param.12) | copy-start | bytes 1179652
  0.0 21.4 %collective-permute-start = (bf16[1,2,192,512]{3,2,1,0:T(8,128)(2,1)}, bf16[1,2,192,512]{3,2,1,0:T(8,128)(2,1)S(1)}, u32[]{:S(2)}, u32[]{:S(2)}) collective-permute-start(bf16[1,2,192,512]{3,2,1,0:T(8,128)(2,1)} %param.12), channel_id=1, source_target_pairs={{0,1},{1,2},{2,3},{3,4},{4,5},{5,6},{6,7},{7,8},{8,9},{9,10},{10,1... | collective-permute-start | bytes 1179656 | tf_op jit(solution)/shard_map/ppermute | solution.py:345
  2.5 18.9 %collective-permute-start.1 = (bf16[1,2,192,512]{3,2,1,0:T(8,128)(2,1)}, bf16[1,2,192,512]{3,2,1,0:T(8,128)(2,1)S(1)}, u32[]{:S(2)}, u32[]{:S(2)}) collective-permute-start(bf16[1,2,192,512]{3,2,1,0:T(8,128)(2,1)} %param.12), channel_id=1, source_target_pairs={{1,0},{2,1},{3,2},{4,3},{5,4},{6,5},{7,6},{8,7},{9,8},{10,9},{11,1... | collective-permute-start | bytes 1179656 | tf_op jit(solution)/shard_map/ppermute | solution.py:346
  5.8 15.6 %all-to-all-start = ((f32[16,1,128]{2,1,0:T(1,128)}), f32[16,1,128]{2,1,0:T(1,128)S(1)}, u32[]{:S(2)}, u32[]{:S(2)}) async-start(f32[16,1,128]{2,1,0:T(1,128)} %bitcast.33), calls=%async_computation | async-start | bytes 16384 | tf_op jit(solution)/shard_map/all_to_all | solution.py:85
  21.4 2.3 %copy-start.1 = (bf16[3,3,512,512]{3,2,1,0:T(8,128)(2,1)S(1)}, bf16[3,3,512,512]{3,2,1,0:T(8,128)(2,1)}, u32[]{:S(2)}) copy-start(bf16[3,3,512,512]{3,2,1,0:T(8,128)(2,1)} %param.18) | copy-start | bytes 14155780
  23.8 1.0 %copy-start.3 = (bf16[1,2,192,512]{3,2,1,0:T(8,128)(2,1)S(1)}, bf16[1,2,192,512]{3,2,1,0:T(8,128)(2,1)}, u32[]{:S(2)}) copy-start(bf16[1,2,192,512]{3,2,1,0:T(8,128)(2,1)} %param.12) | copy-start | bytes 1179652
  24.8 0.7 copy-start.11
  25.4 0.7 copy-start.12
  26.1 0.7 copy-start.14
  26.8 48.9 %copy-start.5 = (bf16[512,1536]{1,0:T(8,128)(2,1)S(1)}, bf16[512,1536]{1,0:T(8,128)(2,1)}, u32[]{:S(2)}) copy-start(bf16[512,1536]{1,0:T(8,128)(2,1)} %refs_19_.1) | copy-start | bytes 4718596
  26.8 48.9 %copy-start.8 = (bf16[512,512]{1,0:T(8,128)(2,1)S(1)}, bf16[512,512]{1,0:T(8,128)(2,1)}, u32[]{:S(2)}) copy-start(bf16[512,512]{1,0:T(8,128)(2,1)} %refs_20_.1) | copy-start | bytes 1572868
  33.3 1.2 %copy-start.6 = (f32[768,512]{1,0:T(8,128)}, f32[768,512]{1,0:T(8,128)S(1)}, u32[]{:S(2)}) copy-start(f32[768,512]{1,0:T(8,128)S(1)} %get-tuple-element.9.first) | copy-start | bytes 4718596
  34.5 0.6 copy-start.15
  35.1 40.6 %copy-start.16 = (f32[512]{0:T(512)S(1)}, f32[512]{0:T(512)}, u32[]{:S(2)}) copy-start(f32[512]{0:T(512)} %param.23) | copy-start | bytes 6148
  35.1 12.1 %all-to-all-start.1 = ((f32[16,1,128]{2,1,0:T(1,128)}), f32[16,1,128]{2,1,0:T(1,128)S(1)}, u32[]{:S(2)}, u32[]{:S(2)}) async-start(f32[16,1,128]{2,1,0:T(1,128)} %bitcast.31), calls=%async_computation.1 | async-start | bytes 16384 | tf_op jit(solution)/shard_map/all_to_all | solution.py:85
  47.3 2.3 %copy-start.2 = (bf16[3,3,512,512]{3,2,1,0:T(8,128)(2,1)S(1)}, bf16[3,3,512,512]{3,2,1,0:T(8,128)(2,1)}, u32[]{:S(2)}) copy-start(bf16[3,3,512,512]{3,2,1,0:T(8,128)(2,1)} %param.19) | copy-start | bytes 14155780
  49.6 1.4 %copy-start.7 = (f32[768,512]{1,0:T(8,128)S(1)}, f32[768,512]{1,0:T(8,128)}, u32[]{:S(2)}) copy-start(f32[768,512]{1,0:T(8,128)} %copy-done.6) | copy-start | bytes 4718596
  51.0 0.7 copy-start.9
  51.7 0.7 copy-start.10
  52.4 0.7 copy-start.13
  57.2 5.7 %collective-permute-start.2 = (bf16[96,512]{1,0:T(8,128)(2,1)S(1)}, bf16[96,512]{1,0:T(8,128)(2,1)S(1)}, u32[]{:S(2)}, u32[]{:S(2)}) collective-permute-start(bf16[96,512]{1,0:T(8,128)(2,1)S(1)} %get-tuple-element.11.refs_0_), channel_id=1, source_target_pairs={{0,4},{1,5},{2,6},{3,7},{4,0},{5,1},{6,2},{7,3},{8,12},{9,13},{10,... | collective-permute-start | bytes 294920 | tf_op jit(solution)/shard_map/ppermute | solution.py:242
  57.8 10.4 %collective-permute-start.3 = (bf16[96,512]{1,0:T(8,128)(2,1)S(1)}, bf16[96,512]{1,0:T(8,128)(2,1)S(1)}, u32[]{:S(2)}, u32[]{:S(2)}) collective-permute-start(bf16[96,512]{1,0:T(8,128)(2,1)S(1)} %get-tuple-element.11.refs_0_), channel_id=1, source_target_pairs={{0,8},{1,9},{2,10},{3,11},{4,12},{5,13},{6,14},{7,15},{8,0},{9,1},... | collective-permute-start | bytes 294920 | tf_op jit(solution)/shard_map/ppermute | solution.py:242
  58.4 10.4 %collective-permute-start.4 = (bf16[96,512]{1,0:T(8,128)(2,1)S(1)}, bf16[96,512]{1,0:T(8,128)(2,1)S(1)}, u32[]{:S(2)}, u32[]{:S(2)}) collective-permute-start(bf16[96,512]{1,0:T(8,128)(2,1)S(1)} %get-tuple-element.11.refs_0_), channel_id=1, source_target_pairs={{0,12},{1,13},{2,14},{3,15},{4,8},{5,9},{6,10},{7,11},{8,4},{9,5},... | collective-permute-start | bytes 294920 | tf_op jit(solution)/shard_map/ppermute | solution.py:242
  61.6 8.6 %collective-permute-start.5 = (bf16[96,512]{1,0:T(8,128)(2,1)S(1)}, bf16[96,512]{1,0:T(8,128)(2,1)S(1)}, u32[]{:S(2)}, u32[]{:S(2)}) collective-permute-start(bf16[96,512]{1,0:T(8,128)(2,1)S(1)} %get-tuple-element.11.refs_0_), channel_id=1, source_target_pairs={{0,2},{1,3},{2,0},{3,1},{4,6},{5,7},{6,4},{7,5},{8,10},{9,11},{10,... | collective-permute-start | bytes 294920 | tf_op jit(solution)/shard_map/ppermute | solution.py:242
  62.1 8.1 %collective-permute-start.9 = (bf16[96,512]{1,0:T(8,128)(2,1)S(1)}, bf16[96,512]{1,0:T(8,128)(2,1)S(1)}, u32[]{:S(2)}, u32[]{:S(2)}) collective-permute-start(bf16[96,512]{1,0:T(8,128)(2,1)S(1)} %get-tuple-element.11.refs_0_), channel_id=1, source_target_pairs={{0,1},{1,0},{2,3},{3,2},{4,5},{5,4},{6,7},{7,6},{8,9},{9,8},{10,11... | collective-permute-start | bytes 294920 | tf_op jit(solution)/shard_map/ppermute | solution.py:242
  62.9 7.9 %collective-permute-start.6 = (bf16[96,512]{1,0:T(8,128)(2,1)S(1)}, bf16[96,512]{1,0:T(8,128)(2,1)S(1)}, u32[]{:S(2)}, u32[]{:S(2)}) collective-permute-start(bf16[96,512]{1,0:T(8,128)(2,1)S(1)} %collective-permute-done.2.refs_1_), channel_id=1, source_target_pairs={{0,2},{1,3},{2,0},{3,1},{4,6},{5,7},{6,4},{7,5},{8,10},{9,11},{10,... | collective-permute-start | bytes 294920 | tf_op jit(solution)/shard_map/ppermute | solution.py:242
  68.2 4.6 %collective-permute-start.7 = (bf16[96,512]{1,0:T(8,128)(2,1)S(1)}, bf16[96,512]{1,0:T(8,128)(2,1)S(1)}, u32[]{:S(2)}, u32[]{:S(2)}) collective-permute-start(bf16[96,512]{1,0:T(8,128)(2,1)S(1)} %collective-permute-done.3.refs_2_), channel_id=1, source_target_pairs={{0,2},{1,3},{2,0},{3,1},{4,6},{5,7},{6,4},{7,5},{8,10},{9,11},{10,... | collective-permute-start | bytes 294920 | tf_op jit(solution)/shard_map/ppermute | solution.py:242
  68.8 5.1 %collective-permute-start.8 = (bf16[96,512]{1,0:T(8,128)(2,1)S(1)}, bf16[96,512]{1,0:T(8,128)(2,1)S(1)}, u32[]{:S(2)}, u32[]{:S(2)}) collective-permute-start(bf16[96,512]{1,0:T(8,128)(2,1)S(1)} %collective-permute-done.4.refs_3_), channel_id=1, source_target_pairs={{0,2},{1,3},{2,0},{3,1},{4,6},{5,7},{6,4},{7,5},{8,10},{9,11},{10,... | collective-permute-start | bytes 294920 | tf_op jit(solution)/shard_map/ppermute | solution.py:242
  70.2 3.6 %collective-permute-start.10 = (bf16[96,512]{1,0:T(8,128)(2,1)S(1)}, bf16[96,512]{1,0:T(8,128)(2,1)S(1)}, u32[]{:S(2)}, u32[]{:S(2)}) collective-permute-start(bf16[96,512]{1,0:T(8,128)(2,1)S(1)} %collective-permute-done.2.refs_1_), channel_id=1, source_target_pairs={{0,1},{1,0},{2,3},{3,2},{4,5},{5,4},{6,7},{7,6},{8,9},{9,8},{10,11... | collective-permute-start | bytes 294920 | tf_op jit(solution)/shard_map/ppermute | solution.py:242
  70.2 4.1 %collective-permute-start.11 = (bf16[96,512]{1,0:T(8,128)(2,1)S(1)}, bf16[96,512]{1,0:T(8,128)(2,1)S(1)}, u32[]{:S(2)}, u32[]{:S(2)}) collective-permute-start(bf16[96,512]{1,0:T(8,128)(2,1)S(1)} %collective-permute-done.3.refs_2_), channel_id=1, source_target_pairs={{0,1},{1,0},{2,3},{3,2},{4,5},{5,4},{6,7},{7,6},{8,9},{9,8},{10,11... | collective-permute-start | bytes 294920 | tf_op jit(solution)/shard_map/ppermute | solution.py:242
  70.7 3.7 %collective-permute-start.12 = (bf16[96,512]{1,0:T(8,128)(2,1)S(1)}, bf16[96,512]{1,0:T(8,128)(2,1)S(1)}, u32[]{:S(2)}, u32[]{:S(2)}) collective-permute-start(bf16[96,512]{1,0:T(8,128)(2,1)S(1)} %collective-permute-done.4.refs_3_), channel_id=1, source_target_pairs={{0,1},{1,0},{2,3},{3,2},{4,5},{5,4},{6,7},{7,6},{8,9},{9,8},{10,11... | collective-permute-start | bytes 294920 | tf_op jit(solution)/shard_map/ppermute | solution.py:242
  72.8 1.6 %collective-permute-start.13 = (bf16[96,512]{1,0:T(8,128)(2,1)S(1)}, bf16[96,512]{1,0:T(8,128)(2,1)S(1)}, u32[]{:S(2)}, u32[]{:S(2)}) collective-permute-start(bf16[96,512]{1,0:T(8,128)(2,1)S(1)} %collective-permute-done.5.refs_4_), channel_id=1, source_target_pairs={{0,1},{1,0},{2,3},{3,2},{4,5},{5,4},{6,7},{7,6},{8,9},{9,8},{10,11... | collective-permute-start | bytes 294920 | tf_op jit(solution)/shard_map/ppermute | solution.py:242
  73.9 1.3 %collective-permute-start.14 = (bf16[96,512]{1,0:T(8,128)(2,1)S(1)}, bf16[96,512]{1,0:T(8,128)(2,1)S(1)}, u32[]{:S(2)}, u32[]{:S(2)}) collective-permute-start(bf16[96,512]{1,0:T(8,128)(2,1)S(1)} %collective-permute-done.6.refs_5_), channel_id=1, source_target_pairs={{0,1},{1,0},{2,3},{3,2},{4,5},{5,4},{6,7},{7,6},{8,9},{9,8},{10,11... | collective-permute-start | bytes 294920 | tf_op jit(solution)/shard_map/ppermute | solution.py:242
  73.9 1.5 %collective-permute-start.15 = (bf16[96,512]{1,0:T(8,128)(2,1)S(1)}, bf16[96,512]{1,0:T(8,128)(2,1)S(1)}, u32[]{:S(2)}, u32[]{:S(2)}) collective-permute-start(bf16[96,512]{1,0:T(8,128)(2,1)S(1)} %collective-permute-done.7.refs_6_), channel_id=1, source_target_pairs={{0,1},{1,0},{2,3},{3,2},{4,5},{5,4},{6,7},{7,6},{8,9},{9,8},{10,11... | collective-permute-start | bytes 294920 | tf_op jit(solution)/shard_map/ppermute | solution.py:242
  74.4 1.3 %collective-permute-start.16 = (bf16[96,512]{1,0:T(8,128)(2,1)S(1)}, bf16[96,512]{1,0:T(8,128)(2,1)S(1)}, u32[]{:S(2)}, u32[]{:S(2)}) collective-permute-start(bf16[96,512]{1,0:T(8,128)(2,1)S(1)} %collective-permute-done.8.refs_7_), channel_id=1, source_target_pairs={{0,1},{1,0},{2,3},{3,2},{4,5},{5,4},{6,7},{7,6},{8,9},{9,8},{10,11... | collective-permute-start | bytes 294920 | tf_op jit(solution)/shard_map/ppermute | solution.py:242

commit v3 on v2

--- a/solution.py
+++ b/solution.py
@@ -13,6 +13,10 @@
 FREQS = 64
 GROUP_WIDTH = 16
 LANES = 128
+GAIN, BIAS, CONV_BIAS, PROJ_BIAS = 0, 3, 6, 8
+VMEM_BYTES = 52 * 1024 * 1024
+FAR = pl.BlockSpec(memory_space=pltpu.HBM)
+NEAR = pl.BlockSpec(memory_space=pltpu.VMEM)
 
 
 eps = 1e-05
@@ -85,15 +89,36 @@
     return lax.all_to_all(rows.reshape(count, 1, lanes), "lat", 0, 0).reshape(count, lanes)
 
 
-def moments_kernel(features, out):
-    sums, squares = column_sums(features[...].astype(jnp.float32))
+def fetched(pairs, sems):
+    copies = [pltpu.make_async_copy(source, target, sems.at[i]) for i, (source, target) in enumerate(pairs)]
+    for each in copies:
+        each.start()
+    return copies
+
+
+def moments_kernel(parts, features, out, held, sems):
+    rows = features.shape[0] // parts
+    spans = [pl.ds(part * rows, rows) for part in range(parts)]
+    copies = fetched([(features.at[span], held.at[span]) for span in spans], sems)
+    sums, squares = 0.0, 0.0
+    for part, copy in enumerate(copies):
+        copy.wait()
+        more = column_sums(held[part * rows : (part + 1) * rows, :].astype(jnp.float32))
+        sums, squares = sums + more[0], squares + more[1]
     out[...] = jnp.broadcast_to(packed_moments(sums, squares), out.shape)
 
 
 def moments(features):
+    parts = 4
     return pl.pallas_call(
-        moments_kernel,
-        out_shape=jax.ShapeDtypeStruct((lax.axis_size("lat"), LANES), jnp.float32),
+        functools.partial(moments_kernel, parts),
+        in_specs=[FAR],
+        out_shape=(
+            jax.ShapeDtypeStruct((lax.axis_size("lat"), LANES), jnp.float32),
+            jax.ShapeDtypeStruct(features.shape, features.dtype),
+        ),
+        scratch_shapes=[pltpu.SemaphoreType.DMA((parts,))],
+        compiler_params=pltpu.CompilerParams(vmem_limit_bytes=VMEM_BYTES),
     )(features)
 
 
@@ -105,103 +130,104 @@
     spread[:, 2 * channels :] = lines[9 : 9 + breadth, :].astype(jnp.bfloat16)
 
 
-def convolved(spread, weight, copies, first, rows, breadth):
+def convolved(spread, weight, copies, rows, breadth):
     total = None
-    for tap in range(3):
-        copies[tap].wait()
-        patch = spread[(first + tap) * breadth : (first + tap + rows) * breadth, :]
+    for tap, copy in enumerate(copies):
+        copy.wait()
+        patch = spread[tap * breadth : (tap + rows) * breadth, :]
         part = jnp.dot(patch, weight[tap], preferred_element_type=jnp.float32)
         total = part if total is None else total + part
     return total
 
 
-def weight_copies(source, weight, sems):
-    copies = [pltpu.make_async_copy(source.at[tap], weight.at[tap], sems.at[tap]) for tap in range(3)]
-    for each in copies:
-        each.start()
-    return copies
-
-
 def first_kernel(
-    height, breadth, below, own, above, sums, gain, bias, weight_hbm, conv_bias, out, packed, spread, lines, weight, sems
+    height, breadth, below, own, above, sums, table, taps, out, packed, weight, spread, lines, result, sems
 ):
     count = lax.axis_size("lat")
     place = lax.axis_index("lat")
     channels = own.shape[1]
-    copies = weight_copies(weight_hbm, weight, sems)
+    copies = fetched([(taps.at[tap], weight.at[tap]) for tap in range(3)], sems)
     lines[...] = jnp.zeros_like(lines)
     center, variance = unpacked_moments(
         sums[...], count * height * breadth * (channels // GROUPS), channels
     )
-    factor = lax.rsqrt(variance + eps) * gain[...]
-    offset = bias[...]
+    factor = lax.rsqrt(variance + eps) * table[GAIN : GAIN + 1]
+    offset = table[BIAS : BIAS + 1]
     for row in range(height + 4):
-        near = row - 2
-        if near < 0:
-            block, at = below, near + 2
-        elif near < height:
-            block, at = own, near
+        if row < 2:
+            values = below[row * breadth : (row + 1) * breadth, :]
+        elif row < height + 2:
+            values = own[(row - 2) * breadth : (row - 1) * breadth, :]
         else:
-            block, at = above, near - height
-        values = block[at * breadth : (at + 1) * breadth, :].astype(jnp.float32)
+            values = above[(row - height - 2) * breadth : (row - height - 1) * breadth, :]
+        values = values.astype(jnp.float32)
         values = silu((values - center) * factor + offset)
-        if near < 0:
+        if row < 2:
             values = jnp.where(place > 0, values, 0.0)
-        elif near >= height:
+        elif row >= height + 2:
             values = jnp.where(place < count - 1, values, 0.0)
         shifted(values, breadth, lines, spread.at[row * breadth : (row + 1) * breadth, :])
-    result = convolved(spread, weight, copies, 0, height + 2, breadth) + conv_bias[...]
-    out[...] = result
-    total, squares = column_sums(result[breadth : (1 + height) * breadth])
+    result[...] = convolved(spread, weight, copies, height + 2, breadth) + table[CONV_BIAS : CONV_BIAS + 1]
+    away = pltpu.make_async_copy(result, out, sems.at[3])
+    away.start()
+    total, squares = column_sums(result[breadth : (1 + height) * breadth, :])
     packed[...] = jnp.broadcast_to(packed_moments(total, squares), packed.shape)
-
-
-def first_convolution(height, breadth, below, own, above, sums, gain, bias, weight, conv_bias):
+    away.wait()
+
+
+def first_convolution(height, breadth, below, own, above, sums, table, weight):
     channels = own.shape[1]
     count = sums.shape[0]
-    plain = pl.BlockSpec(memory_space=pltpu.VMEM)
     return pl.pallas_call(
         functools.partial(first_kernel, height, breadth),
-        in_specs=[plain] * 6 + [pl.BlockSpec(memory_space=pl.ANY), plain],
+        in_specs=[NEAR] * 5 + [FAR],
+        out_specs=(FAR, NEAR),
         out_shape=(
             jax.ShapeDtypeStruct(((height + 2) * breadth, channels), jnp.float32),
             jax.ShapeDtypeStruct((count, LANES), jnp.float32),
         ),
         scratch_shapes=[
+            pltpu.VMEM((3, 3 * channels, channels), jnp.bfloat16),
             pltpu.VMEM(((height + 4) * breadth, 3 * channels), jnp.bfloat16),
             pltpu.VMEM((breadth + 16, channels), jnp.float32),
-            pltpu.VMEM((3, 3 * channels, channels), jnp.bfloat16),
-            pltpu.SemaphoreType.DMA((3,)),
+            pltpu.VMEM(((height + 2) * breadth, channels), jnp.float32),
+            pltpu.SemaphoreType.DMA((4,)),
         ],
-        compiler_params=pltpu.CompilerParams(vmem_limit_bytes=40 * 1024 * 1024),
-    )(below, own, above, sums, gain, bias, weight.reshape(3, 3 * channels, channels), conv_bias)
+        compiler_params=pltpu.CompilerParams(vmem_limit_bytes=VMEM_BYTES),
+    )(below, own, above, sums, table, weight.reshape(3, 3 * channels, channels))
 
 
 def second_kernel(
-    height, breadth, first, own, sums, gain, bias, film, weight_hbm, conv_bias, pooled, sent, spread, lines, pairs, weight, sems
+    height, breadth, first, own, sums, table, film, taps, pooled, sent, rows, weight, spread, lines, pairs, sems
 ):
     count = lax.axis_size("lat")
     place = lax.axis_index("lat")
     channels = own.shape[1]
-    copies = weight_copies(weight_hbm, weight, sems)
+    spans = [pl.ds(row * breadth, breadth) for row in range(height + 2)]
+    copies = fetched(
+        [(first.at[span], rows.at[span]) for span in spans]
+        + [(taps.at[tap], weight.at[tap]) for tap in range(3)],
+        sems,
+    )
     lines[...] = jnp.zeros_like(lines)
     center, variance = unpacked_moments(
         sums[...], count * height * breadth * (channels // GROUPS), channels
     )
-    factor = lax.rsqrt(variance + eps) * gain[...]
-    offset = bias[...]
+    factor = lax.rsqrt(variance + eps) * table[GAIN + 1 : GAIN + 2]
+    offset = table[BIAS + 1 : BIAS + 2]
     scale = 1.0 + film[:, :channels]
     shift = film[:, channels:]
     for row in range(height + 2):
-        values = first[row * breadth : (row + 1) * breadth, :]
+        copies[row].wait()
+        values = rows[row * breadth : (row + 1) * breadth, :]
         values = silu(((values - center) * factor + offset) * scale + shift)
         if row == 0:
             values = jnp.where(place > 0, values, 0.0)
         elif row == height + 1:
             values = jnp.where(place < count - 1, values, 0.0)
         shifted(values, breadth, lines, spread.at[row * breadth : (row + 1) * breadth, :])
-    result = convolved(spread, weight, copies, 0, height, breadth)
-    level = ((own[...].astype(jnp.float32) + result + conv_bias[...]) * skip_gain).astype(jnp.bfloat16)
+    result = convolved(spread, weight, copies[height + 2 :], height, breadth)
+    level = ((own[...].astype(jnp.float32) + result + table[CONV_BIAS + 1 : CONV_BIAS + 2]) * skip_gain).astype(jnp.bfloat16)
     level = level.astype(jnp.float32)
     half = breadth // 2
     for row in range(height // 2):
@@ -215,26 +241,26 @@
             sent[row * half : (row + 1) * half, lanes] = mean.astype(jnp.bfloat16)
 
 
-def second_convolution(height, breadth, first, own, sums, gain, bias, film, weight, conv_bias):
+def second_convolution(height, breadth, first, own, sums, table, film, weight):
     channels = own.shape[1]
     tokens = (height // 2) * (breadth // 2)
-    plain = pl.BlockSpec(memory_space=pltpu.VMEM)
     return pl.pallas_call(
         functools.partial(second_kernel, height, breadth),
-        in_specs=[plain] * 6 + [pl.BlockSpec(memory_space=pl.ANY), plain],
+        in_specs=[FAR] + [NEAR] * 4 + [FAR],
         out_shape=(
             jax.ShapeDtypeStruct((tokens, channels), jnp.float32),
             jax.ShapeDtypeStruct((tokens, channels), jnp.bfloat16),
         ),
         scratch_shapes=[
+            pltpu.VMEM(first.shape, jnp.float32),
+            pltpu.VMEM((3, 3 * channels, channels), jnp.bfloat16),
             pltpu.VMEM(((height + 2) * breadth, 3 * channels), jnp.bfloat16),
             pltpu.VMEM((breadth + 16, channels), jnp.float32),
             pltpu.VMEM((breadth, LANES), jnp.float32),
-            pltpu.VMEM((3, 3 * channels, channels), jnp.bfloat16),
-            pltpu.SemaphoreType.DMA((3,)),
+            pltpu.SemaphoreType.DMA((height + 5,)),
         ],
-        compiler_params=pltpu.CompilerParams(vmem_limit_bytes=40 * 1024 * 1024),
-    )(first, own, sums, gain, bias, film, weight.reshape(3, 3 * channels, channels), conv_bias)
+        compiler_params=pltpu.CompilerParams(vmem_limit_bytes=VMEM_BYTES),
+    )(first, own, sums, table, film, weight.reshape(3, 3 * channels, channels))
 
 
 def exchange(block, stride):
@@ -251,7 +277,7 @@
 
 def attention_kernel(count, *refs):
     blocks = refs[:count]
-    pooled, norm_gain, norm_bias, qkv_weight, proj_weight, proj_bias, out, keys, values = refs[count:]
+    pooled, table, qkv_weight, proj_weight, out, keys, values = refs[count:]
     tokens, channels = pooled.shape
     group_width = channels // GROUPS
     sums = jnp.zeros((8, channels), jnp.float32)
@@ -266,8 +292,8 @@
     moments = group_total(jnp.where(row == 0, sums, squares)) / (count * tokens * group_width)
     center = moments[0:1]
     spread = moments[1:2] - center * center
-    factor = lax.rsqrt(spread + eps) * norm_gain[...]
-    offset = norm_bias[...]
+    factor = lax.rsqrt(spread + eps) * table[GAIN + 2 : GAIN + 3]
+    offset = table[BIAS + 2 : BIAS + 3]
 
     def normed(entry):
         return ((entry.astype(jnp.float32) - center) * factor + offset).astype(jnp.bfloat16)
@@ -301,10 +327,10 @@
     projected = jnp.dot(
         jnp.concatenate(attended, axis=1), proj_weight[...], preferred_element_type=jnp.float32
     )
-    out[...] = ((pooled[...] + projected + proj_bias[...]) * skip_gain).astype(jnp.bfloat16)
-
-
-def attention(blocks, pooled, norm_gain, norm_bias, qkv_weight, proj_weight, proj_bias):
+    out[...] = ((pooled[...] + projected + table[PROJ_BIAS : PROJ_BIAS + 1]) * skip_gain).astype(jnp.bfloat16)
+
+
+def attention(blocks, pooled, table, qkv_weight, proj_weight):
     tokens, channels = pooled.shape
     count = len(blocks)
     return pl.pallas_call(
@@ -314,15 +340,13 @@
             pltpu.VMEM((count * tokens, channels), jnp.bfloat16),
             pltpu.VMEM((count * tokens, channels), jnp.bfloat16),
         ],
-        compiler_params=pltpu.CompilerParams(vmem_limit_bytes=48 * 1024 * 1024),
+        compiler_params=pltpu.CompilerParams(vmem_limit_bytes=(12 + count) * 1024 * 1024),
     )(
         *blocks,
         pooled,
-        norm_gain.reshape(1, channels),
-        norm_bias.reshape(1, channels),
+        table,
         qkv_weight,
         proj_weight,
-        proj_bias.reshape(1, channels),
     )
 
 
@@ -348,16 +372,13 @@
     own = features.reshape(height * breadth, channels)
     below = below.reshape(2 * breadth, channels)
     above = above.reshape(2 * breadth, channels)
-    sums = shared(moments(own))
-    first, packed = first_convolution(
-        height, breadth, below, own, above, sums, norm_gain[0:1], norm_bias[0:1], conv1_weight, conv_bias[0:1]
-    )
-    sums = shared(packed)
+    table = jnp.concatenate([norm_gain, norm_bias, conv_bias, proj_bias[None]], axis=0)
+    packed, own = moments(own)
+    first, packed = first_convolution(height, breadth, below, own, above, shared(packed), table, conv1_weight)
     pooled, sent = second_convolution(
-        height, breadth, first, own, sums, norm_gain[1:2], norm_bias[1:2], film, conv2_weight, conv_bias[1:2]
-    )
-    blocks = gather_blocks(sent)
-    out = attention(blocks, pooled, norm_gain[2], norm_bias[2], qkv_weight, proj_weight, proj_bias)
+        height, breadth, first, own, shared(packed), table, film, conv2_weight
+    )
+    out = attention(gather_blocks(sent), pooled, table, qkv_weight, proj_weight)
     return out.reshape(members, height // 2, breadth // 2, channels)
 
 

time: 82.9 us -> 69.7 us (0.84)
  local copies, waits for them, and re-layouts: 15.7 us -> 1.01 us
  waiting for transfers between devices: 15.3 us -> 18.2 us
  starting transfers between devices: 27.8 us -> 25.8 us
  Pallas kernels: 19.2 us -> 20.4 us
    unnamed x34 -> x8, local copies, waits for them, and re-layouts: 12.9 us -> 1.01 us
    all_to_all x2, waiting for transfers between devices: 5.82 us -> 8.72 us  [shared(): lax.all_to_all(rows.reshape(count, 1, lanes), 'lat', 0, 0)]
    slice x2 -> x0, local copies, waits for them, and re-layouts: 2.78 us -> none  [the longest x1 1.42 us: local(): norm_bias[2]]
    all_to_all x2, starting transfers between devices: 15.1 us -> 13.1 us  [shared(): lax.all_to_all(rows.reshape(count, 1, lanes), 'lat', 0, 0)]
    pallas_call x1, Pallas kernels: 6.57 us -> 7.76 us  [first_convolution(): pl.pallas_call(functools.partial(first_kernel, height, breadth), in_specs...]
  transfers between devices with their start and end apart: 19 -> 19, of which waited for: 9 -> 9; matrix products, arithmetic and copies ran while one was open for 7% -> 3% of each run, Pallas kernels for 2% -> 2%
where the time goes in v3:
time: 69.7 us; the launch traced here: 69.4 us
  starting transfers between devices  25.8 us (37%)
  Pallas kernels  20.4 us (29%)
  waiting for transfers between devices  18.2 us (26%)
  other arithmetic  2.14 us (3%)
  between operations  1.48 us (2%)
  local copies, waits for them, and re-layouts  1.01 us (1%)
    all_to_all x2, starting transfers between devices, shared(): lax.all_to_all(rows.reshape(count, 1, lanes), 'lat', 0, 0)  13.1 us
    ppermute x15, waiting for transfers between devices, exchange(): return lax.ppermute(block, 'lat', [(i, i ^ stride) for i in range(count)])  9.52 us
    ppermute x15, starting transfers between devices, exchange(): return lax.ppermute(block, 'lat', [(i, i ^ stride) for i in range(count)])  8.96 us
    all_to_all x2, waiting for transfers between devices, shared(): lax.all_to_all(rows.reshape(count, 1, lanes), 'lat', 0, 0)  8.72 us
    pallas_call x1, Pallas kernels, first_convolution(): pl.pallas_call(functools.partial(first_kernel, height, breadth), in_specs...  7.76 us
    pallas_call x1, Pallas kernels, attention(): pl.pallas_call(functools.partial(attention_kernel, count), out_shape=jax....  6.5 us
    pallas_call x1, Pallas kernels, second_convolution(): pl.pallas_call(functools.partial(second_kernel, height, breadth), in_spec...  4.65 us
    ppermute x1, starting transfers between devices, local(): lax.ppermute(features[:, -2:], 'lat', [(i, i + 1) for i in range(count -...  2.5 us
  transfers between devices with their start and end apart: 19, of which 9 were waited for; matrix products, arithmetic and copies ran while one was open for 3% of the time, Pallas kernels for 2%

profile of v3, /device:TPU:0, one launch (start us, length us, event | category | flops | bytes accessed | tf_op | source)
XLA Modules:
  0.0 69.4 jit_solution(12076612109639202672)
XLA Ops:
  0.0 0.0 copy-start
  0.0 2.5 %collective-permute-start = (bf16[1,2,192,512]{3,2,1,0:T(8,128)(2,1)}, bf16[1,2,192,512]{3,2,1,0:T(8,128)(2,1)S(1)}, u32[]{:S(2)}, u32[]{:S(2)}) collective-permute-start(bf16[1,2,192,512]{3,2,1,0:T(8,128)(2,1)} %param.12), channel_id=1, source_target_pairs={{0,1},{1,2},{2,3},{3,4},{4,5},{5,6},{6,7},{7,8},{8,9},{9,10},{10,1... | collective-permute-start | bytes 1179656 | tf_op jit(solution)/shard_map/ppermute | solution.py:369
  2.5 1.3 %collective-permute-start.1 = (bf16[1,2,192,512]{3,2,1,0:T(8,128)(2,1)}, bf16[1,2,192,512]{3,2,1,0:T(8,128)(2,1)S(1)}, u32[]{:S(2)}, u32[]{:S(2)}) collective-permute-start(bf16[1,2,192,512]{3,2,1,0:T(8,128)(2,1)} %param.12), channel_id=1, source_target_pairs={{1,0},{2,1},{3,2},{4,3},{5,4},{6,5},{7,6},{8,7},{9,8},{10,9},{11,1... | collective-permute-start | bytes 1179656 | tf_op jit(solution)/shard_map/ppermute | solution.py:370
  3.8 0.0 copy-start.3
  3.8 1.0 %copy-done.3 = bf16[1,2,192,512]{3,2,1,0:T(8,128)(2,1)S(1)} copy-done((bf16[1,2,192,512]{3,2,1,0:T(8,128)(2,1)S(1)}, bf16[1,2,192,512]{3,2,1,0:T(8,128)(2,1)}, u32[]{:S(2)}) %copy-start.3) | copy-done | bytes 393240
  4.8 1.5 %shard_map.118 = (f32[16,128]{1,0:T(8,128)}, bf16[384,512]{1,0:T(8,128)(2,1)S(1)}) custom-call(bf16[384,512]{1,0:T(8,128)(2,1)S(1)} %bitcast.24), custom_call_target="tpu_custom_call" | custom-call | tf_op jit(solution)/shard_map/pallas_call | solution.py:113
  6.3 9.3 %all-to-all-start = ((f32[16,1,128]{2,1,0:T(1,128)}), f32[16,1,128]{2,1,0:T(1,128)S(1)}, u32[]{:S(2)}, u32[]{:S(2)}) async-start(f32[16,1,128]{2,1,0:T(1,128)} %bitcast.4), calls=%async_computation | async-start | bytes 16384 | tf_op jit(solution)/shard_map/all_to_all | solution.py:89
  16.3 1.3 %fusion = f32[]{:T(128)} fusion(f32[18]{0:T(128)} %param.14, s32[]{:T(128)} %bitcast.21), kind=kLoop, calls=%fused_computation.2 | loop fusion | flops 53 | bytes 80 | tf_op jit(solution)/shard_map/reduce_sum | solution.py:31
  18.3 0.8 %pad_maximum_fusion.table.refs_17_ = f32[9,512]{1,0:T(8,128)S(1)} fusion(f32[1,512]{1,0:T(1,128)} %bitcast.29, f32[2,512]{1,0:T(2,128)} %param.20, f32[3,512]{1,0:T(4,128)} %param.17, f32[3,512]{1,0:T(4,128)} %param.16), kind=kLoop, calls=%fused_computation | loop fusion | flops 13824 | bytes 36864 | tf_op jit(solution)/shard_map/concatenate | solution.py:375
  19.1 0.1 sine_convert_fusion
  19.2 2.8 %all-to-all-done = f32[16,1,128]{2,1,0:T(1,128)S(1)} async-done(((f32[16,1,128]{2,1,0:T(1,128)}), f32[16,1,128]{2,1,0:T(1,128)S(1)}, u32[]{:S(2)}, u32[]{:S(2)}) %all-to-all-start) | async-done | bytes 8224 | tf_op jit(solution)/shard_map/all_to_all | solution.py:89
  22.0 0.0 collective-permute-done
  22.0 0.0 collective-permute-done.1
  22.0 7.8 %shard_map.119 = (f32[768,512]{1,0:T(8,128)}, f32[16,128]{1,0:T(8,128)}) custom-call(bf16[384,512]{1,0:T(8,128)(2,1)S(1)} %bitcast.22, bf16[384,512]{1,0:T(8,128)(2,1)S(1)} %get-tuple-element.11.own, bf16[384,512]{1,0:T(8,128)(2,1)S(1)} %bitcast.23, f32[16,128]{1,0:T(8,128)S(1)} %bitcast.25, f32[9,512]{1,0:T(8,128)S(1)} %pad_maximum_fusion.table.refs_17_, ...), custom_call_target="tpu_custom_call" | custom-call | tf_op jit(solution)/shard_map/pallas_call | solution.py:181
  29.8 0.0 copy-start.1
  29.8 0.0 copy-start.2
  29.8 3.8 %all-to-all-start.1 = ((f32[16,1,128]{2,1,0:T(1,128)}), f32[16,1,128]{2,1,0:T(1,128)S(1)}, u32[]{:S(2)}, u32[]{:S(2)}) async-start(f32[16,1,128]{2,1,0:T(1,128)} %bitcast.9), calls=%async_computation.1 | async-start | bytes 16384 | tf_op jit(solution)/shard_map/all_to_all | solution.py:89
  33.6 0.0 copy-done
  33.6 0.2 fusion.1.film
  33.8 5.9 %all-to-all-done.1 = f32[16,1,128]{2,1,0:T(1,128)S(1)} async-done(((f32[16,1,128]{2,1,0:T(1,128)}), f32[16,1,128]{2,1,0:T(1,128)S(1)}, u32[]{:S(2)}, u32[]{:S(2)}) %all-to-all-start.1) | async-done | bytes 8224 | tf_op jit(solution)/shard_map/all_to_all | solution.py:89
  39.7 4.7 %shard_map.120 = (f32[96,512]{1,0:T(8,128)S(1)}, bf16[96,512]{1,0:T(8,128)(2,1)S(1)}) custom-call(f32[768,512]{1,0:T(8,128)} %get-tuple-element.13.first, bf16[384,512]{1,0:T(8,128)(2,1)S(1)} %get-tuple-element.11.own, f32[16,128]{1,0:T(8,128)S(1)} %bitcast.26, f32[9,512]{1,0:T(8,128)S(1)} %pad_maximum_fusion.table.refs_17_, f32[1,1024]{1,0:T(1,128)S(1)} %fusion.1.film, ...), custom_call_target="tpu_custom_call" | custom-call | tf_op jit(solution)/shard_map/pallas_call | solution.py:247
  44.4 0.6 collective-permute-start.2
  44.9 0.6 collective-permute-start.3
  45.5 3.3 %collective-permute-start.4 = (bf16[96,512]{1,0:T(8,128)(2,1)S(1)}, bf16[96,512]{1,0:T(8,128)(2,1)S(1)}, u32[]{:S(2)}, u32[]{:S(2)}) collective-permute-start(bf16[96,512]{1,0:T(8,128)(2,1)S(1)} %get-tuple-element.15.refs_0_), channel_id=1, source_target_pairs={{0,12},{1,13},{2,14},{3,15},{4,8},{5,9},{6,10},{7,11},{8,4},{9,5},... | collective-permute-start | bytes 294920 | tf_op jit(solution)/shard_map/ppermute | solution.py:268
  48.8 0.5 collective-permute-start.5
  49.3 0.0 collective-permute-start.9
  49.3 0.7 %collective-permute-done.2.refs_1_ = bf16[96,512]{1,0:T(8,128)(2,1)S(1)} collective-permute-done((bf16[96,512]{1,0:T(8,128)(2,1)S(1)}, bf16[96,512]{1,0:T(8,128)(2,1)S(1)}, u32[]{:S(2)}, u32[]{:S(2)}) %collective-permute-start.2) | collective-permute-done | bytes 98336 | tf_op jit(solution)/shard_map/ppermute | solution.py:268
  50.0 0.8 %collective-permute-start.6 = (bf16[96,512]{1,0:T(8,128)(2,1)S(1)}, bf16[96,512]{1,0:T(8,128)(2,1)S(1)}, u32[]{:S(2)}, u32[]{:S(2)}) collective-permute-start(bf16[96,512]{1,0:T(8,128)(2,1)S(1)} %collective-permute-done.2.refs_1_), channel_id=1, source_target_pairs={{0,2},{1,3},{2,0},{3,1},{4,6},{5,7},{6,4},{7,5},{8,10},{9,11},{10,... | collective-permute-start | bytes 294920 | tf_op jit(solution)/shard_map/ppermute | solution.py:268
  50.9 4.5 %collective-permute-done.3.refs_2_ = bf16[96,512]{1,0:T(8,128)(2,1)S(1)} collective-permute-done((bf16[96,512]{1,0:T(8,128)(2,1)S(1)}, bf16[96,512]{1,0:T(8,128)(2,1)S(1)}, u32[]{:S(2)}, u32[]{:S(2)}) %collective-permute-start.3) | collective-permute-done | bytes 98336 | tf_op jit(solution)/shard_map/ppermute | solution.py:268
  55.4 0.6 collective-permute-start.7
  55.9 0.0 collective-permute-done.4.refs_3_
  56.0 1.5 %collective-permute-start.8 = (bf16[96,512]{1,0:T(8,128)(2,1)S(1)}, bf16[96,512]{1,0:T(8,128)(2,1)S(1)}, u32[]{:S(2)}, u32[]{:S(2)}) collective-permute-start(bf16[96,512]{1,0:T(8,128)(2,1)S(1)} %collective-permute-done.4.refs_3_), channel_id=1, source_target_pairs={{0,2},{1,3},{2,0},{3,1},{4,6},{5,7},{6,4},{7,5},{8,10},{9,11},{10,... | collective-permute-start | bytes 294920 | tf_op jit(solution)/shard_map/ppermute | solution.py:268
  57.4 0.0 collective-permute-done.5.refs_4_
  57.4 0.0 collective-permute-start.10
  57.4 0.0 collective-permute-done.9.refs_8_
  57.4 0.5 collective-permute-start.11
  57.9 0.0 collective-permute-done.6.refs_5_
  57.9 0.1 collective-permute-start.12
  58.0 2.0 %collective-permute-done.7.refs_6_ = bf16[96,512]{1,0:T(8,128)(2,1)S(1)} collective-permute-done((bf16[96,512]{1,0:T(8,128)(2,1)S(1)}, bf16[96,512]{1,0:T(8,128)(2,1)S(1)}, u32[]{:S(2)}, u32[]{:S(2)}) %collective-permute-start.7) | collective-permute-done | bytes 98336 | tf_op jit(solution)/shard_map/ppermute | solution.py:268
  60.0 0.0 collective-permute-start.13
  60.0 1.0 %collective-permute-done.8.refs_7_ = bf16[96,512]{1,0:T(8,128)(2,1)S(1)} collective-permute-done((bf16[96,512]{1,0:T(8,128)(2,1)S(1)}, bf16[96,512]{1,0:T(8,128)(2,1)S(1)}, u32[]{:S(2)}, u32[]{:S(2)}) %collective-permute-start.8) | collective-permute-done | bytes 98336 | tf_op jit(solution)/shard_map/ppermute | solution.py:268
  61.0 0.0 collective-permute-start.14
  61.0 0.0 collective-permute-done.10.refs_9_
  61.0 0.5 collective-permute-start.15
  61.6 0.0 collective-permute-done.11.refs_10_
  61.6 0.1 collective-permute-start.16
  61.6 0.0 collective-permute-done.12.refs_11_
  61.6 0.0 collective-permute-done.13.refs_12_
  61.6 0.7 %collective-permute-done.14.refs_13_ = bf16[96,512]{1,0:T(8,128)(2,1)S(1)} collective-permute-done((bf16[96,512]{1,0:T(8,128)(2,1)S(1)}, bf16[96,512]{1,0:T(8,128)(2,1)S(1)}, u32[]{:S(2)}, u32[]{:S(2)}) %collective-permute-start.14) | collective-permute-done | bytes 98336 | tf_op jit(solution)/shard_map/ppermute | solution.py:268
  62.3 0.2 collective-permute-done.15.refs_14_
  62.5 0.4 collective-permute-done.16.refs_15_
  62.9 0.0 copy-done.1
  62.9 0.0 copy-done.2
  62.9 6.5 %shard_map.121 = bf16[96,512]{1,0:T(8,128)(2,1)} custom-call(bf16[96,512]{1,0:T(8,128)(2,1)S(1)} %get-tuple-element.15.refs_0_, bf16[96,512]{1,0:T(8,128)(2,1)S(1)} %collective-permute-done.2.refs_1_, bf16[96,512]{1,0:T(8,128)(2,1)S(1)} %collective-permute-done.3.refs_2_, bf16[96,512]{1,0:T(8,128)(2,1)S(1)} %collective-permute-done.4.refs_3_, ...), custom_call_target="tpu_custom_call" | custom-call | tf_op jit(solution)/shard_map/pallas_call | solution.py:336
Async XLA Ops:
  0.0 33.6 %copy-start = (bf16[128,1024]{1,0:T(8,128)(2,1)S(1)}, bf16[128,1024]{1,0:T(8,128)(2,1)}, u32[]{:S(2)}) copy-start(bf16[128,1024]{1,0:T(8,128)(2,1)} %param.15) | copy-start | bytes 786436
  0.0 22.0 %collective-permute-start = (bf16[1,2,192,512]{3,2,1,0:T(8,128)(2,1)}, bf16[1,2,192,512]{3,2,1,0:T(8,128)(2,1)S(1)}, u32[]{:S(2)}, u32[]{:S(2)}) collective-permute-start(bf16[1,2,192,512]{3,2,1,0:T(8,128)(2,1)} %param.12), channel_id=1, source_target_pairs={{0,1},{1,2},{2,3},{3,4},{4,5},{5,6},{6,7},{7,8},{8,9},{9,10},{10,1... | collective-permute-start | bytes 1179656 | tf_op jit(solution)/shard_map/ppermute | solution.py:369
  2.5 19.5 %collective-permute-start.1 = (bf16[1,2,192,512]{3,2,1,0:T(8,128)(2,1)}, bf16[1,2,192,512]{3,2,1,0:T(8,128)(2,1)S(1)}, u32[]{:S(2)}, u32[]{:S(2)}) collective-permute-start(bf16[1,2,192,512]{3,2,1,0:T(8,128)(2,1)} %param.12), channel_id=1, source_target_pairs={{1,0},{2,1},{3,2},{4,3},{5,4},{6,5},{7,6},{8,7},{9,8},{10,9},{11,1... | collective-permute-start | bytes 1179656 | tf_op jit(solution)/shard_map/ppermute | solution.py:370
  3.8 1.0 %copy-start.3 = (bf16[1,2,192,512]{3,2,1,0:T(8,128)(2,1)S(1)}, bf16[1,2,192,512]{3,2,1,0:T(8,128)(2,1)}, u32[]{:S(2)}) copy-start(bf16[1,2,192,512]{3,2,1,0:T(8,128)(2,1)} %param.12) | copy-start | bytes 1179652
  6.3 15.6 %all-to-all-start = ((f32[16,1,128]{2,1,0:T(1,128)}), f32[16,1,128]{2,1,0:T(1,128)S(1)}, u32[]{:S(2)}, u32[]{:S(2)}) async-start(f32[16,1,128]{2,1,0:T(1,128)} %bitcast.4), calls=%async_computation | async-start | bytes 16384 | tf_op jit(solution)/shard_map/all_to_all | solution.py:89
  29.8 33.1 %copy-start.1 = (bf16[512,1536]{1,0:T(8,128)(2,1)S(1)}, bf16[512,1536]{1,0:T(8,128)(2,1)}, u32[]{:S(2)}) copy-start(bf16[512,1536]{1,0:T(8,128)(2,1)} %refs_18_.1) | copy-start | bytes 4718596
  29.8 33.1 %copy-start.2 = (bf16[512,512]{1,0:T(8,128)(2,1)S(1)}, bf16[512,512]{1,0:T(8,128)(2,1)}, u32[]{:S(2)}) copy-start(bf16[512,512]{1,0:T(8,128)(2,1)} %refs_19_.1) | copy-start | bytes 1572868
  29.8 9.9 %all-to-all-start.1 = ((f32[16,1,128]{2,1,0:T(1,128)}), f32[16,1,128]{2,1,0:T(1,128)S(1)}, u32[]{:S(2)}, u32[]{:S(2)}) async-start(f32[16,1,128]{2,1,0:T(1,128)} %bitcast.9), calls=%async_computation.1 | async-start | bytes 16384 | tf_op jit(solution)/shard_map/all_to_all | solution.py:89
  44.4 5.7 %collective-permute-start.2 = (bf16[96,512]{1,0:T(8,128)(2,1)S(1)}, bf16[96,512]{1,0:T(8,128)(2,1)S(1)}, u32[]{:S(2)}, u32[]{:S(2)}) collective-permute-start(bf16[96,512]{1,0:T(8,128)(2,1)S(1)} %get-tuple-element.15.refs_0_), channel_id=1, source_target_pairs={{0,4},{1,5},{2,6},{3,7},{4,0},{5,1},{6,2},{7,3},{8,12},{9,13},{10,... | collective-permute-start | bytes 294920 | tf_op jit(solution)/shard_map/ppermute | solution.py:268
  44.9 10.4 %collective-permute-start.3 = (bf16[96,512]{1,0:T(8,128)(2,1)S(1)}, bf16[96,512]{1,0:T(8,128)(2,1)S(1)}, u32[]{:S(2)}, u32[]{:S(2)}) collective-permute-start(bf16[96,512]{1,0:T(8,128)(2,1)S(1)} %get-tuple-element.15.refs_0_), channel_id=1, source_target_pairs={{0,8},{1,9},{2,10},{3,11},{4,12},{5,13},{6,14},{7,15},{8,0},{9,1},... | collective-permute-start | bytes 294920 | tf_op jit(solution)/shard_map/ppermute | solution.py:268
  45.5 10.4 %collective-permute-start.4 = (bf16[96,512]{1,0:T(8,128)(2,1)S(1)}, bf16[96,512]{1,0:T(8,128)(2,1)S(1)}, u32[]{:S(2)}, u32[]{:S(2)}) collective-permute-start(bf16[96,512]{1,0:T(8,128)(2,1)S(1)} %get-tuple-element.15.refs_0_), channel_id=1, source_target_pairs={{0,12},{1,13},{2,14},{3,15},{4,8},{5,9},{6,10},{7,11},{8,4},{9,5},... | collective-permute-start | bytes 294920 | tf_op jit(solution)/shard_map/ppermute | solution.py:268
  48.8 8.6 %collective-permute-start.5 = (bf16[96,512]{1,0:T(8,128)(2,1)S(1)}, bf16[96,512]{1,0:T(8,128)(2,1)S(1)}, u32[]{:S(2)}, u32[]{:S(2)}) collective-permute-start(bf16[96,512]{1,0:T(8,128)(2,1)S(1)} %get-tuple-element.15.refs_0_), channel_id=1, source_target_pairs={{0,2},{1,3},{2,0},{3,1},{4,6},{5,7},{6,4},{7,5},{8,10},{9,11},{10,... | collective-permute-start | bytes 294920 | tf_op jit(solution)/shard_map/ppermute | solution.py:268
  49.3 8.1 %collective-permute-start.9 = (bf16[96,512]{1,0:T(8,128)(2,1)S(1)}, bf16[96,512]{1,0:T(8,128)(2,1)S(1)}, u32[]{:S(2)}, u32[]{:S(2)}) collective-permute-start(bf16[96,512]{1,0:T(8,128)(2,1)S(1)} %get-tuple-element.15.refs_0_), channel_id=1, source_target_pairs={{0,1},{1,0},{2,3},{3,2},{4,5},{5,4},{6,7},{7,6},{8,9},{9,8},{10,11... | collective-permute-start | bytes 294920 | tf_op jit(solution)/shard_map/ppermute | solution.py:268
  50.0 7.9 %collective-permute-start.6 = (bf16[96,512]{1,0:T(8,128)(2,1)S(1)}, bf16[96,512]{1,0:T(8,128)(2,1)S(1)}, u32[]{:S(2)}, u32[]{:S(2)}) collective-permute-start(bf16[96,512]{1,0:T(8,128)(2,1)S(1)} %collective-permute-done.2.refs_1_), channel_id=1, source_target_pairs={{0,2},{1,3},{2,0},{3,1},{4,6},{5,7},{6,4},{7,5},{8,10},{9,11},{10,... | collective-permute-start | bytes 294920 | tf_op jit(solution)/shard_map/ppermute | solution.py:268
  55.4 4.6 %collective-permute-start.7 = (bf16[96,512]{1,0:T(8,128)(2,1)S(1)}, bf16[96,512]{1,0:T(8,128)(2,1)S(1)}, u32[]{:S(2)}, u32[]{:S(2)}) collective-permute-start(bf16[96,512]{1,0:T(8,128)(2,1)S(1)} %collective-permute-done.3.refs_2_), channel_id=1, source_target_pairs={{0,2},{1,3},{2,0},{3,1},{4,6},{5,7},{6,4},{7,5},{8,10},{9,11},{10,... | collective-permute-start | bytes 294920 | tf_op jit(solution)/shard_map/ppermute | solution.py:268
  56.0 5.1 %collective-permute-start.8 = (bf16[96,512]{1,0:T(8,128)(2,1)S(1)}, bf16[96,512]{1,0:T(8,128)(2,1)S(1)}, u32[]{:S(2)}, u32[]{:S(2)}) collective-permute-start(bf16[96,512]{1,0:T(8,128)(2,1)S(1)} %collective-permute-done.4.refs_3_), channel_id=1, source_target_pairs={{0,2},{1,3},{2,0},{3,1},{4,6},{5,7},{6,4},{7,5},{8,10},{9,11},{10,... | collective-permute-start | bytes 294920 | tf_op jit(solution)/shard_map/ppermute | solution.py:268
  57.4 3.6 %collective-permute-start.10 = (bf16[96,512]{1,0:T(8,128)(2,1)S(1)}, bf16[96,512]{1,0:T(8,128)(2,1)S(1)}, u32[]{:S(2)}, u32[]{:S(2)}) collective-permute-start(bf16[96,512]{1,0:T(8,128)(2,1)S(1)} %collective-permute-done.2.refs_1_), channel_id=1, source_target_pairs={{0,1},{1,0},{2,3},{3,2},{4,5},{5,4},{6,7},{7,6},{8,9},{9,8},{10,11... | collective-permute-start | bytes 294920 | tf_op jit(solution)/shard_map/ppermute | solution.py:268
  57.4 4.1 %collective-permute-start.11 = (bf16[96,512]{1,0:T(8,128)(2,1)S(1)}, bf16[96,512]{1,0:T(8,128)(2,1)S(1)}, u32[]{:S(2)}, u32[]{:S(2)}) collective-permute-start(bf16[96,512]{1,0:T(8,128)(2,1)S(1)} %collective-permute-done.3.refs_2_), channel_id=1, source_target_pairs={{0,1},{1,0},{2,3},{3,2},{4,5},{5,4},{6,7},{7,6},{8,9},{9,8},{10,11... | collective-permute-start | bytes 294920 | tf_op jit(solution)/shard_map/ppermute | solution.py:268
  57.9 3.7 %collective-permute-start.12 = (bf16[96,512]{1,0:T(8,128)(2,1)S(1)}, bf16[96,512]{1,0:T(8,128)(2,1)S(1)}, u32[]{:S(2)}, u32[]{:S(2)}) collective-permute-start(bf16[96,512]{1,0:T(8,128)(2,1)S(1)} %collective-permute-done.4.refs_3_), channel_id=1, source_target_pairs={{0,1},{1,0},{2,3},{3,2},{4,5},{5,4},{6,7},{7,6},{8,9},{9,8},{10,11... | collective-permute-start | bytes 294920 | tf_op jit(solution)/shard_map/ppermute | solution.py:268
  60.0 1.6 %collective-permute-start.13 = (bf16[96,512]{1,0:T(8,128)(2,1)S(1)}, bf16[96,512]{1,0:T(8,128)(2,1)S(1)}, u32[]{:S(2)}, u32[]{:S(2)}) collective-permute-start(bf16[96,512]{1,0:T(8,128)(2,1)S(1)} %collective-permute-done.5.refs_4_), channel_id=1, source_target_pairs={{0,1},{1,0},{2,3},{3,2},{4,5},{5,4},{6,7},{7,6},{8,9},{9,8},{10,11... | collective-permute-start | bytes 294920 | tf_op jit(solution)/shard_map/ppermute | solution.py:268
  61.0 1.3 %collective-permute-start.14 = (bf16[96,512]{1,0:T(8,128)(2,1)S(1)}, bf16[96,512]{1,0:T(8,128)(2,1)S(1)}, u32[]{:S(2)}, u32[]{:S(2)}) collective-permute-start(bf16[96,512]{1,0:T(8,128)(2,1)S(1)} %collective-permute-done.6.refs_5_), channel_id=1, source_target_pairs={{0,1},{1,0},{2,3},{3,2},{4,5},{5,4},{6,7},{7,6},{8,9},{9,8},{10,11... | collective-permute-start | bytes 294920 | tf_op jit(solution)/shard_map/ppermute | solution.py:268
  61.0 1.5 %collective-permute-start.15 = (bf16[96,512]{1,0:T(8,128)(2,1)S(1)}, bf16[96,512]{1,0:T(8,128)(2,1)S(1)}, u32[]{:S(2)}, u32[]{:S(2)}) collective-permute-start(bf16[96,512]{1,0:T(8,128)(2,1)S(1)} %collective-permute-done.7.refs_6_), channel_id=1, source_target_pairs={{0,1},{1,0},{2,3},{3,2},{4,5},{5,4},{6,7},{7,6},{8,9},{9,8},{10,11... | collective-permute-start | bytes 294920 | tf_op jit(solution)/shard_map/ppermute | solution.py:268
  61.6 1.3 %collective-permute-start.16 = (bf16[96,512]{1,0:T(8,128)(2,1)S(1)}, bf16[96,512]{1,0:T(8,128)(2,1)S(1)}, u32[]{:S(2)}, u32[]{:S(2)}) collective-permute-start(bf16[96,512]{1,0:T(8,128)(2,1)S(1)} %collective-permute-done.8.refs_7_), channel_id=1, source_target_pairs={{0,1},{1,0},{2,3},{3,2},{4,5},{5,4},{6,7},{7,6},{8,9},{9,8},{10,11... | collective-permute-start | bytes 294920 | tf_op jit(solution)/shard_map/ppermute | solution.py:268

commit v4 on v3

--- a/solution.py
+++ b/solution.py
@@ -15,6 +15,7 @@
 LANES = 128
 GAIN, BIAS, CONV_BIAS, PROJ_BIAS = 0, 3, 6, 8
 VMEM_BYTES = 52 * 1024 * 1024
+SHADOW_BYTES = 256 * 1024 * 1024
 FAR = pl.BlockSpec(memory_space=pltpu.HBM)
 NEAR = pl.BlockSpec(memory_space=pltpu.VMEM)
 
@@ -23,17 +24,25 @@
 skip_gain = 0.7071067811865476
 
 
-def noise_terms(noise_index, sigma_table, affine_weight):
-    levels_count = sigma_table.shape[0]
-    chosen = (noise_index[:, None] == jnp.arange(levels_count, dtype=jnp.int32)[None, :]).astype(
-        jnp.float32
-    )
-    sigmas = jnp.sum(chosen * sigma_table[None, :], axis=1)
-    log_level = jnp.log(sigmas) / 4.0
-    frequency = jnp.exp(-math.log(10000.0) * jnp.arange(FREQS, dtype=jnp.float32) / FREQS)
-    angles = log_level[:, None] * frequency[None, :]
-    fourier = jnp.concatenate([jnp.cos(angles), jnp.sin(angles)], axis=1).astype(jnp.bfloat16)
-    return jnp.dot(fourier, affine_weight, preferred_element_type=jnp.float32)
+def film_kernel(noise_index, sigma_table, affine_weight, after, out):
+    del after
+    level = lax.broadcasted_iota(jnp.int32, sigma_table.shape, 1)
+    chosen = jnp.where(level == noise_index[0], sigma_table[...], 0.0)
+    log_level = jnp.log(jnp.sum(chosen, axis=1, keepdims=True)) / 4.0
+    lane = lax.broadcasted_iota(jnp.int32, (1, 2 * FREQS), 1)
+    order = (lane % FREQS).astype(jnp.float32)
+    angles = log_level * jnp.exp(-math.log(10000.0) * order / FREQS)
+    fourier = jnp.where(lane < FREQS, jnp.cos(angles), jnp.sin(angles)).astype(jnp.bfloat16)
+    out[...] = jnp.dot(fourier, affine_weight[...], preferred_element_type=jnp.float32)
+
+
+def film_terms(noise_index, sigma_table, affine_weight, after):
+    return pl.pallas_call(
+        film_kernel,
+        in_specs=[pl.BlockSpec(memory_space=pltpu.SMEM), NEAR, NEAR, FAR],
+        out_shape=jax.ShapeDtypeStruct((1, affine_weight.shape[1]), jnp.float32),
+        compiler_params=pltpu.CompilerParams(vmem_limit_bytes=VMEM_BYTES),
+    )(noise_index, sigma_table[None], affine_weight, after)
 
 
 def group_total(rows):
@@ -130,105 +139,150 @@
     spread[:, 2 * channels :] = lines[9 : 9 + breadth, :].astype(jnp.bfloat16)
 
 
-def convolved(spread, weight, copies, rows, breadth):
+def affine_kernel(which, entries, sums, table, *refs):
+    film, out = (None, *refs)[-2:]
+    channels = table.shape[1]
+    center, variance = unpacked_moments(sums[...], entries, channels)
+    factor = lax.rsqrt(variance + eps) * table[GAIN + which : GAIN + which + 1]
+    offset = table[BIAS + which : BIAS + which + 1]
+    if film is not None:
+        scale = 1.0 + film[:, :channels]
+        factor = factor * scale
+        offset = offset * scale + film[:, channels:]
+    out[0:1, :] = center
+    out[1:2, :] = factor
+    out[2:3, :] = offset
+
+
+def affine(which, cells, sums, table, *film):
+    channels = table.shape[1]
+    entries = sums.shape[0] * cells * (channels // GROUPS)
+    return pl.pallas_call(
+        functools.partial(affine_kernel, which, entries),
+        out_shape=jax.ShapeDtypeStruct((3, channels), jnp.float32),
+        cost_estimate=pl.CostEstimate(flops=0, bytes_accessed=SHADOW_BYTES, transcendentals=0),
+        compiler_params=pltpu.CompilerParams(vmem_limit_bytes=VMEM_BYTES),
+    )(sums, table, *film)
+
+
+def tap_copies(source, target, sems):
+    return [pltpu.make_async_copy(source.at[tap], target.at[tap], sems.at[tap]) for tap in range(3)]
+
+
+def convolved(patches, weight, copies):
     total = None
     for tap, copy in enumerate(copies):
         copy.wait()
-        patch = spread[tap * breadth : (tap + rows) * breadth, :]
-        part = jnp.dot(patch, weight[tap], preferred_element_type=jnp.float32)
+        part = jnp.dot(patches(tap), weight[tap], preferred_element_type=jnp.float32)
         total = part if total is None else total + part
     return total
 
 
-def first_kernel(
-    height, breadth, below, own, above, sums, table, taps, out, packed, weight, spread, lines, result, sems
+def first_kernel(height, breadth, outer, own, norm, table, taps, mate, other, *refs):
+    refs = list(refs)
+    if outer:
+        refs.pop(0)
+    result = refs.pop(0)
+    packed = None if outer else refs.pop(0)
+    weight, spread, lines, sems = refs
+    count = lax.axis_size("lat")
+    place = lax.axis_index("lat")
+    odd = place % 2 == 1
+    channels = own.shape[1]
+    copies = tap_copies(taps, weight, sems)
+    copies[0].start()
+    lines[...] = jnp.zeros_like(lines)
+    center, factor, offset = norm[0:1, :], norm[1:2, :], norm[2:3, :]
+    if outer:
+        needed = [-2, -1, 0, height - 1, height, height + 1]
+    else:
+        needed = list(range(-1, height + 1))
+    for i, row in enumerate(needed):
+        if row < 0:
+            span = slice((row + height) * breadth, (row + height + 1) * breadth)
+            values = jnp.where(odd, mate[span, :], other[span, :])
+        elif row < height:
+            values = own[row * breadth : (row + 1) * breadth, :]
+        else:
+            span = slice((row - height) * breadth, (row - height + 1) * breadth)
+            values = jnp.where(odd, other[span, :], mate[span, :])
+        values = silu((values.astype(jnp.float32) - center) * factor + offset)
+        if row < 0:
+            values = jnp.where(place > 0, values, 0.0)
+        elif row >= height:
+            values = jnp.where(place < count - 1, values, 0.0)
+        shifted(values, breadth, lines, spread.at[i * breadth : (i + 1) * breadth, :])
+        if i in (1, 3):
+            copies[(i + 1) // 2].start()
+
+    def patches(tap):
+        if outer:
+            pair = [spread[(tap + at) * breadth : (tap + at + 1) * breadth, :] for at in (0, 3)]
+            return jnp.concatenate(pair, axis=0)
+        return spread[tap * breadth : (tap + height) * breadth, :]
+
+    result[...] = convolved(patches, weight, copies) + table[CONV_BIAS : CONV_BIAS + 1]
+    if not outer:
+        total, squares = column_sums(result[...])
+        packed[...] = jnp.broadcast_to(packed_moments(total, squares), packed.shape)
+
+
+def first_convolution(height, breadth, own, norm, table, weight, mate, other, after=()):
+    channels = own.shape[1]
+    count = lax.axis_size("lat")
+    outer = len(after) > 0
+    rows, needed = (2, 6) if outer else (height, height + 2)
+    shape = jax.ShapeDtypeStruct((rows * breadth, channels), jnp.float32)
+    return pl.pallas_call(
+        functools.partial(first_kernel, height, breadth, outer),
+        in_specs=[NEAR] * 3 + [FAR] + [NEAR] * 2 + [FAR] * len(after),
+        out_shape=shape if outer else (shape, jax.ShapeDtypeStruct((count, LANES), jnp.float32)),
+        scratch_shapes=[
+            pltpu.VMEM((3, 3 * channels, channels), jnp.bfloat16),
+            pltpu.VMEM((needed * breadth, 3 * channels), jnp.bfloat16),
+            pltpu.VMEM((breadth + 16, channels), jnp.float32),
+            pltpu.SemaphoreType.DMA((3,)),
+        ],
+        compiler_params=pltpu.CompilerParams(vmem_limit_bytes=VMEM_BYTES),
+    )(own, norm, table, weight.reshape(3, 3 * channels, channels), mate, other, *after)
+
+
+def second_kernel(
+    height, breadth, first, outer, own, norm, table, taps, pooled, sent, rows, weight, spread, lines, pairs, sems, weight_sems
 ):
     count = lax.axis_size("lat")
     place = lax.axis_index("lat")
     channels = own.shape[1]
-    copies = fetched([(taps.at[tap], weight.at[tap]) for tap in range(3)], sems)
-    lines[...] = jnp.zeros_like(lines)
-    center, variance = unpacked_moments(
-        sums[...], count * height * breadth * (channels // GROUPS), channels
-    )
-    factor = lax.rsqrt(variance + eps) * table[GAIN : GAIN + 1]
-    offset = table[BIAS : BIAS + 1]
-    for row in range(height + 4):
-        if row < 2:
-            values = below[row * breadth : (row + 1) * breadth, :]
-        elif row < height + 2:
-            values = own[(row - 2) * breadth : (row - 1) * breadth, :]
-        else:
-            values = above[(row - height - 2) * breadth : (row - height - 1) * breadth, :]
-        values = values.astype(jnp.float32)
-        values = silu((values - center) * factor + offset)
-        if row < 2:
-            values = jnp.where(place > 0, values, 0.0)
-        elif row >= height + 2:
-            values = jnp.where(place < count - 1, values, 0.0)
-        shifted(values, breadth, lines, spread.at[row * breadth : (row + 1) * breadth, :])
-    result[...] = convolved(spread, weight, copies, height + 2, breadth) + table[CONV_BIAS : CONV_BIAS + 1]
-    away = pltpu.make_async_copy(result, out, sems.at[3])
-    away.start()
-    total, squares = column_sums(result[breadth : (1 + height) * breadth, :])
-    packed[...] = jnp.broadcast_to(packed_moments(total, squares), packed.shape)
-    away.wait()
-
-
-def first_convolution(height, breadth, below, own, above, sums, table, weight):
-    channels = own.shape[1]
-    count = sums.shape[0]
-    return pl.pallas_call(
-        functools.partial(first_kernel, height, breadth),
-        in_specs=[NEAR] * 5 + [FAR],
-        out_specs=(FAR, NEAR),
-        out_shape=(
-            jax.ShapeDtypeStruct(((height + 2) * breadth, channels), jnp.float32),
-            jax.ShapeDtypeStruct((count, LANES), jnp.float32),
-        ),
-        scratch_shapes=[
-            pltpu.VMEM((3, 3 * channels, channels), jnp.bfloat16),
-            pltpu.VMEM(((height + 4) * breadth, 3 * channels), jnp.bfloat16),
-            pltpu.VMEM((breadth + 16, channels), jnp.float32),
-            pltpu.VMEM(((height + 2) * breadth, channels), jnp.float32),
-            pltpu.SemaphoreType.DMA((4,)),
+    low, high = rows.at[pl.ds(0, breadth)], rows.at[pl.ds((height + 1) * breadth, breadth)]
+    copies = fetched(
+        [
+            (first, rows.at[pl.ds(breadth, height * breadth)]),
+            (outer.at[pl.ds(0, breadth)], low),
+            (outer.at[pl.ds(breadth, breadth)], high),
         ],
-        compiler_params=pltpu.CompilerParams(vmem_limit_bytes=VMEM_BYTES),
-    )(below, own, above, sums, table, weight.reshape(3, 3 * channels, channels))
-
-
-def second_kernel(
-    height, breadth, first, own, sums, table, film, taps, pooled, sent, rows, weight, spread, lines, pairs, sems
-):
-    count = lax.axis_size("lat")
-    place = lax.axis_index("lat")
-    channels = own.shape[1]
-    spans = [pl.ds(row * breadth, breadth) for row in range(height + 2)]
-    copies = fetched(
-        [(first.at[span], rows.at[span]) for span in spans]
-        + [(taps.at[tap], weight.at[tap]) for tap in range(3)],
         sems,
     )
+    weights = tap_copies(taps, weight, weight_sems)
+    weights[0].start()
     lines[...] = jnp.zeros_like(lines)
-    center, variance = unpacked_moments(
-        sums[...], count * height * breadth * (channels // GROUPS), channels
-    )
-    factor = lax.rsqrt(variance + eps) * table[GAIN + 1 : GAIN + 2]
-    offset = table[BIAS + 1 : BIAS + 2]
-    scale = 1.0 + film[:, :channels]
-    shift = film[:, channels:]
-    for row in range(height + 2):
-        copies[row].wait()
+    center, factor, offset = norm[0:1, :], norm[1:2, :], norm[2:3, :]
+    for row in [*range(1, height + 1), 0, height + 1]:
+        if row in (0, 1, height + 1):
+            copies[{1: 0, 0: 1}.get(row, 2)].wait()
         values = rows[row * breadth : (row + 1) * breadth, :]
-        values = silu(((values - center) * factor + offset) * scale + shift)
+        values = silu((values - center) * factor + offset)
         if row == 0:
             values = jnp.where(place > 0, values, 0.0)
         elif row == height + 1:
             values = jnp.where(place < count - 1, values, 0.0)
         shifted(values, breadth, lines, spread.at[row * breadth : (row + 1) * breadth, :])
-    result = convolved(spread, weight, copies[height + 2 :], height, breadth)
-    level = ((own[...].astype(jnp.float32) + result + table[CONV_BIAS + 1 : CONV_BIAS + 2]) * skip_gain).astype(jnp.bfloat16)
-    level = level.astype(jnp.float32)
+        if row in (2, height + 1):
+            weights[1 if row == 2 else 2].start()
+    result = convolved(
+        lambda tap: spread[tap * breadth : (tap + height) * breadth, :], weight, weights
+    )
+    level = own[...].astype(jnp.float32) + result + table[CONV_BIAS + 1 : CONV_BIAS + 2]
+    level = (level * skip_gain).astype(jnp.bfloat16).astype(jnp.float32)
     half = breadth // 2
     for row in range(height // 2):
         start = 2 * row * breadth
@@ -241,26 +295,27 @@
             sent[row * half : (row + 1) * half, lanes] = mean.astype(jnp.bfloat16)
 
 
-def second_convolution(height, breadth, first, own, sums, table, film, weight):
+def second_convolution(height, breadth, first, outer, own, norm, table, weight):
     channels = own.shape[1]
     tokens = (height // 2) * (breadth // 2)
     return pl.pallas_call(
         functools.partial(second_kernel, height, breadth),
-        in_specs=[FAR] + [NEAR] * 4 + [FAR],
+        in_specs=[FAR] * 2 + [NEAR] * 3 + [FAR],
         out_shape=(
             jax.ShapeDtypeStruct((tokens, channels), jnp.float32),
             jax.ShapeDtypeStruct((tokens, channels), jnp.bfloat16),
         ),
         scratch_shapes=[
-            pltpu.VMEM(first.shape, jnp.float32),
+            pltpu.VMEM(((height + 2) * breadth, channels), jnp.float32),
             pltpu.VMEM((3, 3 * channels, channels), jnp.bfloat16),
             pltpu.VMEM(((height + 2) * breadth, 3 * channels), jnp.bfloat16),
             pltpu.VMEM((breadth + 16, channels), jnp.float32),
             pltpu.VMEM((breadth, LANES), jnp.float32),
-            pltpu.SemaphoreType.DMA((height + 5,)),
+            pltpu.SemaphoreType.DMA((3,)),
+            pltpu.SemaphoreType.DMA((3,)),
         ],
         compiler_params=pltpu.CompilerParams(vmem_limit_bytes=VMEM_BYTES),
-    )(first, own, sums, table, film, weight.reshape(3, 3 * channels, channels))
+    )(first, outer, own, norm, table, weight.reshape(3, 3 * channels, channels))
 
 
 def exchange(block, stride):
@@ -366,18 +421,17 @@
 ):
     members, height, breadth, channels = features.shape
     count = lax.axis_size("lat")
-    below = lax.ppermute(features[:, -2:], "lat", [(i, i + 1) for i in range(count - 1)])
-    above = lax.ppermute(features[:, :2], "lat", [(i + 1, i) for i in range(count - 1)])
-    film = noise_terms(noise_index, sigma_table, affine_weight)
-    own = features.reshape(height * breadth, channels)
-    below = below.reshape(2 * breadth, channels)
-    above = above.reshape(2 * breadth, channels)
     table = jnp.concatenate([norm_gain, norm_bias, conv_bias, proj_bias[None]], axis=0)
-    packed, own = moments(own)
-    first, packed = first_convolution(height, breadth, below, own, above, shared(packed), table, conv1_weight)
-    pooled, sent = second_convolution(
-        height, breadth, first, own, shared(packed), table, film, conv2_weight
-    )
+    packed, own = moments(features.reshape(height * breadth, channels))
+    mate = lax.ppermute(own, "lat", [(i, i ^ 1) for i in range(count)])
+    other = lax.ppermute(own, "lat", [(i, (i - 1 ^ 1) + 1) for i in range(1, count - 1)])
+    norm = affine(0, height * breadth, shared(packed), table)
+    known = (own, norm, table, conv1_weight, mate, other)
+    first, packed = first_convolution(height, breadth, *known)
+    outer = first_convolution(height, breadth, *known, [packed])
+    film = film_terms(noise_index, sigma_table, affine_weight, packed)
+    norm = affine(1, height * breadth, shared(packed), table, film)
+    pooled, sent = second_convolution(height, breadth, first, outer, own, norm, table, conv2_weight)
     out = attention(gather_blocks(sent), pooled, table, qkv_weight, proj_weight)
     return out.reshape(members, height // 2, breadth // 2, channels)
 

time: 69.7 us -> 66.5 us (0.954)
  starting transfers between devices: 25.8 us -> 23.9 us
  Pallas kernels: 20.4 us -> 22.2 us
  waiting for transfers between devices: 18.2 us -> 16.6 us
  other arithmetic: 2.14 us -> 0.76 us
  local copies, waits for them, and re-layouts: 1.01 us -> 1.91 us
  between operations: 1.48 us -> 0.78 us
    all_to_all x2, waiting for transfers between devices: 8.72 us -> 6.05 us  [shared(): lax.all_to_all(rows.reshape(count, 1, lanes), 'lat', 0, 0)]
    ppermute x2, starting transfers between devices: 3.79 us -> 1.19 us  [the longest x1 0.67 us: local(): lax.ppermute(own, 'lat', [(i, (i - 1 ^ 1) + 1) for i in range(1, count -...]
    pallas_call x1 -> x5, Pallas kernels: 7.76 us -> 9.75 us  [the longest x2 8.9 us: first_convolution(): pl.pallas_call(functools.partial(first_kernel, height, breadth, outer), i...]
    reduce_sum x1 -> x0, other arithmetic: 1.33 us -> none  [noise_terms(): sigmas = jnp.sum(chosen * sigma_table[None, :], axis=1)]
    ppermute x15, waiting for transfers between devices: 9.52 us -> 10.6 us  [exchange(): return lax.ppermute(block, 'lat', [(i, i ^ stride) for i in range(count)])]
    unnamed x8 -> x12, local copies, waits for them, and re-layouts: 1.01 us -> 1.91 us
    ppermute x15, starting transfers between devices: 8.96 us -> 9.71 us  [exchange(): return lax.ppermute(block, 'lat', [(i, i ^ stride) for i in range(count)])]
  transfers between devices with their start and end apart: 19 -> 19, of which waited for: 9 -> 8; matrix products, arithmetic and copies ran while one was open for 3% -> 1% of each run, Pallas kernels for 2% -> 7%
where the time goes in v4:
time: 66.5 us; the launch traced here: 66.2 us
  starting transfers between devices  23.9 us (36%)
  Pallas kernels  22.2 us (33%)
  waiting for transfers between devices  16.6 us (25%)
  local copies, waits for them, and re-layouts  1.91 us (3%)
  between operations  0.78 us (1%)
  other arithmetic  0.76 us (1%)
    all_to_all x2, starting transfers between devices, shared(): lax.all_to_all(rows.reshape(count, 1, lanes), 'lat', 0, 0)  13 us
    ppermute x15, waiting for transfers between devices, exchange(): return lax.ppermute(block, 'lat', [(i, i ^ stride) for i in range(count)])  10.6 us
    ppermute x15, starting transfers between devices, exchange(): return lax.ppermute(block, 'lat', [(i, i ^ stride) for i in range(count)])  9.71 us
    pallas_call x2, Pallas kernels, first_convolution(): pl.pallas_call(functools.partial(first_kernel, height, breadth, outer), i...  8.9 us
    pallas_call x1, Pallas kernels, attention(): pl.pallas_call(functools.partial(attention_kernel, count), out_shape=jax....  6.51 us
    all_to_all x2, waiting for transfers between devices, shared(): lax.all_to_all(rows.reshape(count, 1, lanes), 'lat', 0, 0)  6.05 us
    pallas_call x1, Pallas kernels, second_convolution(): pl.pallas_call(functools.partial(second_kernel, height, breadth), in_spec...  4.43 us
    unnamed x12, local copies, waits for them, and re-layouts  1.91 us
  transfers between devices with their start and end apart: 19, of which 8 were waited for; matrix products, arithmetic and copies ran while one was open for 1% of the time, Pallas kernels for 7%

profile of v4, /device:TPU:0, one launch (start us, length us, event | category | flops | bytes accessed | tf_op | source)
XLA Modules:
  0.0 66.2 jit_solution(3485803674337810803)
XLA Ops:
  0.0 0.0 copy-start.5
  0.0 0.0 copy-start.3
  0.0 1.0 %copy-done.3 = bf16[1,2,192,512]{3,2,1,0:T(8,128)(2,1)S(1)} copy-done((bf16[1,2,192,512]{3,2,1,0:T(8,128)(2,1)S(1)}, bf16[1,2,192,512]{3,2,1,0:T(8,128)(2,1)}, u32[]{:S(2)}) %copy-start.3) | copy-done | bytes 393240
  1.0 0.0 copy-start.4
  1.0 1.5 %shard_map.118 = (f32[16,128]{1,0:T(8,128)}, bf16[384,512]{1,0:T(8,128)(2,1)S(1)}) custom-call(bf16[384,512]{1,0:T(8,128)(2,1)S(1)} %bitcast.14), custom_call_target="tpu_custom_call" | custom-call | tf_op jit(solution)/shard_map/pallas_call | solution.py:122
  2.6 0.5 collective-permute-start
  3.1 0.7 %collective-permute-start.1 = (bf16[384,512]{1,0:T(8,128)(2,1)S(1)}, bf16[384,512]{1,0:T(8,128)(2,1)S(1)}, u32[]{:S(2)}, u32[]{:S(2)}) collective-permute-start(bf16[384,512]{1,0:T(8,128)(2,1)S(1)} %get-tuple-element.11.own), channel_id=1, source_target_pairs={{1,2},{2,1},{3,4},{4,3},{5,6},{6,5},{7,8},{8,7},{9,10},{10,9},{11,... | collective-permute-start | bytes 1179656 | tf_op jit(solution)/shard_map/ppermute | solution.py:427
  3.8 8.8 %all-to-all-start = ((f32[16,1,128]{2,1,0:T(1,128)}), f32[16,1,128]{2,1,0:T(1,128)S(1)}, u32[]{:S(2)}, u32[]{:S(2)}) async-start(f32[16,1,128]{2,1,0:T(1,128)} %bitcast.2), calls=%async_computation | async-start | bytes 16384 | tf_op jit(solution)/shard_map/all_to_all | solution.py:98
  12.6 0.8 %pad_maximum_fusion.table.refs_17_ = f32[9,512]{1,0:T(8,128)S(1)} fusion(f32[1,512]{1,0:T(1,128)} %bitcast.21, f32[2,512]{1,0:T(2,128)} %param.20, f32[3,512]{1,0:T(4,128)} %param.17, f32[3,512]{1,0:T(4,128)} %param.16), kind=kLoop, calls=%fused_computation | loop fusion | flops 13824 | bytes 36864 | tf_op jit(solution)/shard_map/concatenate | solution.py:424
  13.3 5.6 %all-to-all-done = f32[16,1,128]{2,1,0:T(1,128)S(1)} async-done(((f32[16,1,128]{2,1,0:T(1,128)}), f32[16,1,128]{2,1,0:T(1,128)S(1)}, u32[]{:S(2)}, u32[]{:S(2)}) %all-to-all-start) | async-done | bytes 8224 | tf_op jit(solution)/shard_map/all_to_all | solution.py:98
  18.9 0.3 shard_map.119.norm
  19.2 0.0 collective-permute-done.mate
  19.2 0.0 collective-permute-done.1.other
  19.2 4.9 %shard_map.120 = (f32[384,512]{1,0:T(8,128)S(1)}, f32[16,128]{1,0:T(8,128)}) custom-call(bf16[384,512]{1,0:T(8,128)(2,1)S(1)} %get-tuple-element.11.own, f32[3,512]{1,0:T(4,128)S(1)} %shard_map.119.norm, f32[9,512]{1,0:T(8,128)S(1)} %pad_maximum_fusion.table.refs_17_, bf16[3,1536,512]{2,1,0:T(8,128)(2,1)} %bitcast.18, ...), custom_call_target="tpu_custom_call" | custom-call | tf_op jit(solution)/shard_map/pallas_call | solution.py:236
  24.1 4.2 %all-to-all-start.1 = ((f32[16,1,128]{2,1,0:T(1,128)}), f32[16,1,128]{2,1,0:T(1,128)S(1)}, u32[]{:S(2)}, u32[]{:S(2)}) async-start(f32[16,1,128]{2,1,0:T(1,128)} %bitcast.7), calls=%async_computation.1 | async-start | bytes 16384 | tf_op jit(solution)/shard_map/all_to_all | solution.py:98
  29.0 0.0 copy-done.5
  29.0 0.0 copy-done.4
  29.0 0.3 shard_map.122.refs_0_
  29.3 4.0 %shard_map.121.outer = f32[384,512]{1,0:T(8,128)S(1)} custom-call(bf16[384,512]{1,0:T(8,128)(2,1)S(1)} %get-tuple-element.11.own, f32[3,512]{1,0:T(4,128)S(1)} %shard_map.119.norm, f32[9,512]{1,0:T(8,128)S(1)} %pad_maximum_fusion.table.refs_17_, bf16[3,1536,512]{2,1,0:T(8,128)(2,1)} %bitcast.19, bf16[384,512]{1,0:T(8,128)(2,1)S(1)} %collective-permute-done.mate, ...), custom_call_target="tpu_custom_call" | custom-call | tf_op jit(solution)/shard_map/pallas_call | solution.py:236
  33.3 0.0 copy-start
  33.3 0.9 %copy-done = f32[384,512]{1,0:T(8,128)} copy-done((f32[384,512]{1,0:T(8,128)}, f32[384,512]{1,0:T(8,128)S(1)}, u32[]{:S(2)}) %copy-start) | copy-done | bytes 786456
  34.2 0.0 copy-start.1
  34.2 0.0 copy-start.2
  34.2 0.5 all-to-all-done.1
  34.7 0.3 shard_map.123.norm
  35.0 4.4 %shard_map.124 = (f32[96,512]{1,0:T(8,128)S(1)}, bf16[96,512]{1,0:T(8,128)(2,1)S(1)}) custom-call(f32[384,512]{1,0:T(8,128)S(1)} %get-tuple-element.13.first, f32[384,512]{1,0:T(8,128)} %copy-done, bf16[384,512]{1,0:T(8,128)(2,1)S(1)} %get-tuple-element.11.own, f32[3,512]{1,0:T(4,128)S(1)} %shard_map.123.norm, f32[9,512]{1,0:T(8,128)S(1)} %pad_maximum_fusion.table.refs_17_, ...), custom_call_target="tpu_custom_call" | custom-call | tf_op jit(solution)/shard_map/pallas_call | solution.py:301
  39.4 1.7 %collective-permute-start.2 = (bf16[96,512]{1,0:T(8,128)(2,1)S(1)}, bf16[96,512]{1,0:T(8,128)(2,1)S(1)}, u32[]{:S(2)}, u32[]{:S(2)}) collective-permute-start(bf16[96,512]{1,0:T(8,128)(2,1)S(1)} %get-tuple-element.15.refs_0_), channel_id=1, source_target_pairs={{0,4},{1,5},{2,6},{3,7},{4,0},{5,1},{6,2},{7,3},{8,12},{9,13},{10,... | collective-permute-start | bytes 294920 | tf_op jit(solution)/shard_map/ppermute | solution.py:323
  41.1 2.4 %collective-permute-start.3 = (bf16[96,512]{1,0:T(8,128)(2,1)S(1)}, bf16[96,512]{1,0:T(8,128)(2,1)S(1)}, u32[]{:S(2)}, u32[]{:S(2)}) collective-permute-start(bf16[96,512]{1,0:T(8,128)(2,1)S(1)} %get-tuple-element.15.refs_0_), channel_id=1, source_target_pairs={{0,8},{1,9},{2,10},{3,11},{4,12},{5,13},{6,14},{7,15},{8,0},{9,1},... | collective-permute-start | bytes 294920 | tf_op jit(solution)/shard_map/ppermute | solution.py:323
  43.5 0.4 collective-permute-start.4
  43.9 1.6 %collective-permute-start.5 = (bf16[96,512]{1,0:T(8,128)(2,1)S(1)}, bf16[96,512]{1,0:T(8,128)(2,1)S(1)}, u32[]{:S(2)}, u32[]{:S(2)}) collective-permute-start(bf16[96,512]{1,0:T(8,128)(2,1)S(1)} %get-tuple-element.15.refs_0_), channel_id=1, source_target_pairs={{0,2},{1,3},{2,0},{3,1},{4,6},{5,7},{6,4},{7,5},{8,10},{9,11},{10,... | collective-permute-start | bytes 294920 | tf_op jit(solution)/shard_map/ppermute | solution.py:323
  45.5 0.0 collective-permute-start.9
  45.5 0.0 collective-permute-done.2.refs_1_
  45.5 0.5 collective-permute-start.6
  46.0 5.8 %collective-permute-done.3.refs_2_ = bf16[96,512]{1,0:T(8,128)(2,1)S(1)} collective-permute-done((bf16[96,512]{1,0:T(8,128)(2,1)S(1)}, bf16[96,512]{1,0:T(8,128)(2,1)S(1)}, u32[]{:S(2)}, u32[]{:S(2)}) %collective-permute-start.3) | collective-permute-done | bytes 98336 | tf_op jit(solution)/shard_map/ppermute | solution.py:323
  51.8 1.5 %collective-permute-start.7 = (bf16[96,512]{1,0:T(8,128)(2,1)S(1)}, bf16[96,512]{1,0:T(8,128)(2,1)S(1)}, u32[]{:S(2)}, u32[]{:S(2)}) collective-permute-start(bf16[96,512]{1,0:T(8,128)(2,1)S(1)} %collective-permute-done.3.refs_2_), channel_id=1, source_target_pairs={{0,2},{1,3},{2,0},{3,1},{4,6},{5,7},{6,4},{7,5},{8,10},{9,11},{10,... | collective-permute-start | bytes 294920 | tf_op jit(solution)/shard_map/ppermute | solution.py:323
  53.3 0.0 collective-permute-done.4.refs_3_
  53.3 0.6 collective-permute-start.8
  53.8 0.0 collective-permute-done.5.refs_4_
  53.8 0.0 collective-permute-start.10
  53.8 0.0 collective-permute-done.9.refs_8_
  53.8 0.5 collective-permute-start.11
  54.3 0.0 collective-permute-done.6.refs_5_
  54.3 0.1 collective-permute-start.12
  54.4 2.0 %collective-permute-done.7.refs_6_ = bf16[96,512]{1,0:T(8,128)(2,1)S(1)} collective-permute-done((bf16[96,512]{1,0:T(8,128)(2,1)S(1)}, bf16[96,512]{1,0:T(8,128)(2,1)S(1)}, u32[]{:S(2)}, u32[]{:S(2)}) %collective-permute-start.7) | collective-permute-done | bytes 98336 | tf_op jit(solution)/shard_map/ppermute | solution.py:323
  56.4 0.0 collective-permute-start.13
  56.4 1.5 %collective-permute-done.8.refs_7_ = bf16[96,512]{1,0:T(8,128)(2,1)S(1)} collective-permute-done((bf16[96,512]{1,0:T(8,128)(2,1)S(1)}, bf16[96,512]{1,0:T(8,128)(2,1)S(1)}, u32[]{:S(2)}, u32[]{:S(2)}) %collective-permute-start.8) | collective-permute-done | bytes 98336 | tf_op jit(solution)/shard_map/ppermute | solution.py:323
  57.9 0.0 collective-permute-start.14
  57.9 0.0 collective-permute-done.10.refs_9_
  57.9 0.5 collective-permute-start.15
  58.4 0.0 collective-permute-done.11.refs_10_
  58.4 0.1 collective-permute-start.16
  58.5 0.0 collective-permute-done.12.refs_11_
  58.5 0.0 collective-permute-done.13.refs_12_
  58.5 0.7 %collective-permute-done.14.refs_13_ = bf16[96,512]{1,0:T(8,128)(2,1)S(1)} collective-permute-done((bf16[96,512]{1,0:T(8,128)(2,1)S(1)}, bf16[96,512]{1,0:T(8,128)(2,1)S(1)}, u32[]{:S(2)}, u32[]{:S(2)}) %collective-permute-start.14) | collective-permute-done | bytes 98336 | tf_op jit(solution)/shard_map/ppermute | solution.py:323
  59.2 0.2 collective-permute-done.15.refs_14_
  59.3 0.4 collective-permute-done.16.refs_15_
  59.7 0.0 copy-done.1
  59.7 0.0 copy-done.2
  59.7 6.5 %shard_map.125 = bf16[96,512]{1,0:T(8,128)(2,1)} custom-call(bf16[96,512]{1,0:T(8,128)(2,1)S(1)} %get-tuple-element.15.refs_0_, bf16[96,512]{1,0:T(8,128)(2,1)S(1)} %collective-permute-done.2.refs_1_, bf16[96,512]{1,0:T(8,128)(2,1)S(1)} %collective-permute-done.3.refs_2_, bf16[96,512]{1,0:T(8,128)(2,1)S(1)} %collective-permute-done.4.refs_3_, ...), custom_call_target="tpu_custom_call" | custom-call | tf_op jit(solution)/shard_map/pallas_call | solution.py:391
Async XLA Ops:
  0.0 29.0 %copy-start.5 = (f32[18]{0:T(128)S(1)}, f32[18]{0:T(128)}, u32[]{:S(2)}) copy-start(f32[18]{0:T(128)} %param.14) | copy-start | bytes 220
  0.0 1.0 %copy-start.3 = (bf16[1,2,192,512]{3,2,1,0:T(8,128)(2,1)S(1)}, bf16[1,2,192,512]{3,2,1,0:T(8,128)(2,1)}, u32[]{:S(2)}) copy-start(bf16[1,2,192,512]{3,2,1,0:T(8,128)(2,1)} %param.12) | copy-start | bytes 1179652
  1.0 28.0 %copy-start.4 = (bf16[128,1024]{1,0:T(8,128)(2,1)S(1)}, bf16[128,1024]{1,0:T(8,128)(2,1)}, u32[]{:S(2)}) copy-start(bf16[128,1024]{1,0:T(8,128)(2,1)} %affine_weight.1) | copy-start | bytes 786436
  2.6 16.6 %collective-permute-start = (bf16[384,512]{1,0:T(8,128)(2,1)S(1)}, bf16[384,512]{1,0:T(8,128)(2,1)S(1)}, u32[]{:S(2)}, u32[]{:S(2)}) collective-permute-start(bf16[384,512]{1,0:T(8,128)(2,1)S(1)} %get-tuple-element.11.own), channel_id=1, source_target_pairs={{0,1},{1,0},{2,3},{3,2},{4,5},{5,4},{6,7},{7,6},{8,9},{9,8},{10,11... | collective-permute-start | bytes 1179656 | tf_op jit(solution)/shard_map/ppermute | solution.py:426
  3.1 16.1 %collective-permute-start.1 = (bf16[384,512]{1,0:T(8,128)(2,1)S(1)}, bf16[384,512]{1,0:T(8,128)(2,1)S(1)}, u32[]{:S(2)}, u32[]{:S(2)}) collective-permute-start(bf16[384,512]{1,0:T(8,128)(2,1)S(1)} %get-tuple-element.11.own), channel_id=1, source_target_pairs={{1,2},{2,1},{3,4},{4,3},{5,6},{6,5},{7,8},{8,7},{9,10},{10,9},{11,... | collective-permute-start | bytes 1179656 | tf_op jit(solution)/shard_map/ppermute | solution.py:427
  3.8 15.1 %all-to-all-start = ((f32[16,1,128]{2,1,0:T(1,128)}), f32[16,1,128]{2,1,0:T(1,128)S(1)}, u32[]{:S(2)}, u32[]{:S(2)}) async-start(f32[16,1,128]{2,1,0:T(1,128)} %bitcast.2), calls=%async_computation | async-start | bytes 16384 | tf_op jit(solution)/shard_map/all_to_all | solution.py:98
  24.1 10.6 %all-to-all-start.1 = ((f32[16,1,128]{2,1,0:T(1,128)}), f32[16,1,128]{2,1,0:T(1,128)S(1)}, u32[]{:S(2)}, u32[]{:S(2)}) async-start(f32[16,1,128]{2,1,0:T(1,128)} %bitcast.7), calls=%async_computation.1 | async-start | bytes 16384 | tf_op jit(solution)/shard_map/all_to_all | solution.py:98
  33.3 0.9 %copy-start = (f32[384,512]{1,0:T(8,128)}, f32[384,512]{1,0:T(8,128)S(1)}, u32[]{:S(2)}) copy-start(f32[384,512]{1,0:T(8,128)S(1)} %shard_map.121.outer) | copy-start | bytes 2359300
  34.2 25.5 %copy-start.1 = (bf16[512,1536]{1,0:T(8,128)(2,1)S(1)}, bf16[512,1536]{1,0:T(8,128)(2,1)}, u32[]{:S(2)}) copy-start(bf16[512,1536]{1,0:T(8,128)(2,1)} %refs_18_.1) | copy-start | bytes 4718596
  34.2 25.5 %copy-start.2 = (bf16[512,512]{1,0:T(8,128)(2,1)S(1)}, bf16[512,512]{1,0:T(8,128)(2,1)}, u32[]{:S(2)}) copy-start(bf16[512,512]{1,0:T(8,128)(2,1)} %refs_19_.1) | copy-start | bytes 1572868
  39.4 6.1 %collective-permute-start.2 = (bf16[96,512]{1,0:T(8,128)(2,1)S(1)}, bf16[96,512]{1,0:T(8,128)(2,1)S(1)}, u32[]{:S(2)}, u32[]{:S(2)}) collective-permute-start(bf16[96,512]{1,0:T(8,128)(2,1)S(1)} %get-tuple-element.15.refs_0_), channel_id=1, source_target_pairs={{0,4},{1,5},{2,6},{3,7},{4,0},{5,1},{6,2},{7,3},{8,12},{9,13},{10,... | collective-permute-start | bytes 294920 | tf_op jit(solution)/shard_map/ppermute | solution.py:323
  41.1 10.7 %collective-permute-start.3 = (bf16[96,512]{1,0:T(8,128)(2,1)S(1)}, bf16[96,512]{1,0:T(8,128)(2,1)S(1)}, u32[]{:S(2)}, u32[]{:S(2)}) collective-permute-start(bf16[96,512]{1,0:T(8,128)(2,1)S(1)} %get-tuple-element.15.refs_0_), channel_id=1, source_target_pairs={{0,8},{1,9},{2,10},{3,11},{4,12},{5,13},{6,14},{7,15},{8,0},{9,1},... | collective-permute-start | bytes 294920 | tf_op jit(solution)/shard_map/ppermute | solution.py:323
  43.5 9.8 %collective-permute-start.4 = (bf16[96,512]{1,0:T(8,128)(2,1)S(1)}, bf16[96,512]{1,0:T(8,128)(2,1)S(1)}, u32[]{:S(2)}, u32[]{:S(2)}) collective-permute-start(bf16[96,512]{1,0:T(8,128)(2,1)S(1)} %get-tuple-element.15.refs_0_), channel_id=1, source_target_pairs={{0,12},{1,13},{2,14},{3,15},{4,8},{5,9},{6,10},{7,11},{8,4},{9,5},... | collective-permute-start | bytes 294920 | tf_op jit(solution)/shard_map/ppermute | solution.py:323
  43.9 10.0 %collective-permute-start.5 = (bf16[96,512]{1,0:T(8,128)(2,1)S(1)}, bf16[96,512]{1,0:T(8,128)(2,1)S(1)}, u32[]{:S(2)}, u32[]{:S(2)}) collective-permute-start(bf16[96,512]{1,0:T(8,128)(2,1)S(1)} %get-tuple-element.15.refs_0_), channel_id=1, source_target_pairs={{0,2},{1,3},{2,0},{3,1},{4,6},{5,7},{6,4},{7,5},{8,10},{9,11},{10,... | collective-permute-start | bytes 294920 | tf_op jit(solution)/shard_map/ppermute | solution.py:323
  45.5 8.4 %collective-permute-start.9 = (bf16[96,512]{1,0:T(8,128)(2,1)S(1)}, bf16[96,512]{1,0:T(8,128)(2,1)S(1)}, u32[]{:S(2)}, u32[]{:S(2)}) collective-permute-start(bf16[96,512]{1,0:T(8,128)(2,1)S(1)} %get-tuple-element.15.refs_0_), channel_id=1, source_target_pairs={{0,1},{1,0},{2,3},{3,2},{4,5},{5,4},{6,7},{7,6},{8,9},{9,8},{10,11... | collective-permute-start | bytes 294920 | tf_op jit(solution)/shard_map/ppermute | solution.py:323
  45.5 8.9 %collective-permute-start.6 = (bf16[96,512]{1,0:T(8,128)(2,1)S(1)}, bf16[96,512]{1,0:T(8,128)(2,1)S(1)}, u32[]{:S(2)}, u32[]{:S(2)}) collective-permute-start(bf16[96,512]{1,0:T(8,128)(2,1)S(1)} %collective-permute-done.2.refs_1_), channel_id=1, source_target_pairs={{0,2},{1,3},{2,0},{3,1},{4,6},{5,7},{6,4},{7,5},{8,10},{9,11},{10,... | collective-permute-start | bytes 294920 | tf_op jit(solution)/shard_map/ppermute | solution.py:323
  51.8 4.6 %collective-permute-start.7 = (bf16[96,512]{1,0:T(8,128)(2,1)S(1)}, bf16[96,512]{1,0:T(8,128)(2,1)S(1)}, u32[]{:S(2)}, u32[]{:S(2)}) collective-permute-start(bf16[96,512]{1,0:T(8,128)(2,1)S(1)} %collective-permute-done.3.refs_2_), channel_id=1, source_target_pairs={{0,2},{1,3},{2,0},{3,1},{4,6},{5,7},{6,4},{7,5},{8,10},{9,11},{10,... | collective-permute-start | bytes 294920 | tf_op jit(solution)/shard_map/ppermute | solution.py:323
  53.3 4.6 %collective-permute-start.8 = (bf16[96,512]{1,0:T(8,128)(2,1)S(1)}, bf16[96,512]{1,0:T(8,128)(2,1)S(1)}, u32[]{:S(2)}, u32[]{:S(2)}) collective-permute-start(bf16[96,512]{1,0:T(8,128)(2,1)S(1)} %collective-permute-done.4.refs_3_), channel_id=1, source_target_pairs={{0,2},{1,3},{2,0},{3,1},{4,6},{5,7},{6,4},{7,5},{8,10},{9,11},{10,... | collective-permute-start | bytes 294920 | tf_op jit(solution)/shard_map/ppermute | solution.py:323
  53.8 4.1 %collective-permute-start.10 = (bf16[96,512]{1,0:T(8,128)(2,1)S(1)}, bf16[96,512]{1,0:T(8,128)(2,1)S(1)}, u32[]{:S(2)}, u32[]{:S(2)}) collective-permute-start(bf16[96,512]{1,0:T(8,128)(2,1)S(1)} %collective-permute-done.2.refs_1_), channel_id=1, source_target_pairs={{0,1},{1,0},{2,3},{3,2},{4,5},{5,4},{6,7},{7,6},{8,9},{9,8},{10,11... | collective-permute-start | bytes 294920 | tf_op jit(solution)/shard_map/ppermute | solution.py:323
  53.8 4.6 %collective-permute-start.11 = (bf16[96,512]{1,0:T(8,128)(2,1)S(1)}, bf16[96,512]{1,0:T(8,128)(2,1)S(1)}, u32[]{:S(2)}, u32[]{:S(2)}) collective-permute-start(bf16[96,512]{1,0:T(8,128)(2,1)S(1)} %collective-permute-done.3.refs_2_), channel_id=1, source_target_pairs={{0,1},{1,0},{2,3},{3,2},{4,5},{5,4},{6,7},{7,6},{8,9},{9,8},{10,11... | collective-permute-start | bytes 294920 | tf_op jit(solution)/shard_map/ppermute | solution.py:323
  54.3 4.1 %collective-permute-start.12 = (bf16[96,512]{1,0:T(8,128)(2,1)S(1)}, bf16[96,512]{1,0:T(8,128)(2,1)S(1)}, u32[]{:S(2)}, u32[]{:S(2)}) collective-permute-start(bf16[96,512]{1,0:T(8,128)(2,1)S(1)} %collective-permute-done.4.refs_3_), channel_id=1, source_target_pairs={{0,1},{1,0},{2,3},{3,2},{4,5},{5,4},{6,7},{7,6},{8,9},{9,8},{10,11... | collective-permute-start | bytes 294920 | tf_op jit(solution)/shard_map/ppermute | solution.py:323
  56.4 2.1 %collective-permute-start.13 = (bf16[96,512]{1,0:T(8,128)(2,1)S(1)}, bf16[96,512]{1,0:T(8,128)(2,1)S(1)}, u32[]{:S(2)}, u32[]{:S(2)}) collective-permute-start(bf16[96,512]{1,0:T(8,128)(2,1)S(1)} %collective-permute-done.5.refs_4_), channel_id=1, source_target_pairs={{0,1},{1,0},{2,3},{3,2},{4,5},{5,4},{6,7},{7,6},{8,9},{9,8},{10,11... | collective-permute-start | bytes 294920 | tf_op jit(solution)/shard_map/ppermute | solution.py:323
  57.9 1.3 %collective-permute-start.14 = (bf16[96,512]{1,0:T(8,128)(2,1)S(1)}, bf16[96,512]{1,0:T(8,128)(2,1)S(1)}, u32[]{:S(2)}, u32[]{:S(2)}) collective-permute-start(bf16[96,512]{1,0:T(8,128)(2,1)S(1)} %collective-permute-done.6.refs_5_), channel_id=1, source_target_pairs={{0,1},{1,0},{2,3},{3,2},{4,5},{5,4},{6,7},{7,6},{8,9},{9,8},{10,11... | collective-permute-start | bytes 294920 | tf_op jit(solution)/shard_map/ppermute | solution.py:323
  57.9 1.5 %collective-permute-start.15 = (bf16[96,512]{1,0:T(8,128)(2,1)S(1)}, bf16[96,512]{1,0:T(8,128)(2,1)S(1)}, u32[]{:S(2)}, u32[]{:S(2)}) collective-permute-start(bf16[96,512]{1,0:T(8,128)(2,1)S(1)} %collective-permute-done.7.refs_6_), channel_id=1, source_target_pairs={{0,1},{1,0},{2,3},{3,2},{4,5},{5,4},{6,7},{7,6},{8,9},{9,8},{10,11... | collective-permute-start | bytes 294920 | tf_op jit(solution)/shard_map/ppermute | solution.py:323
  58.4 1.3 %collective-permute-start.16 = (bf16[96,512]{1,0:T(8,128)(2,1)S(1)}, bf16[96,512]{1,0:T(8,128)(2,1)S(1)}, u32[]{:S(2)}, u32[]{:S(2)}) collective-permute-start(bf16[96,512]{1,0:T(8,128)(2,1)S(1)} %collective-permute-done.8.refs_7_), channel_id=1, source_target_pairs={{0,1},{1,0},{2,3},{3,2},{4,5},{5,4},{6,7},{7,6},{8,9},{9,8},{10,11... | collective-permute-start | bytes 294920 | tf_op jit(solution)/shard_map/ppermute | solution.py:323

commit v5 on v4

--- a/solution.py
+++ b/solution.py
@@ -105,28 +105,24 @@
     return copies
 
 
-def moments_kernel(parts, features, out, held, sems):
-    rows = features.shape[0] // parts
-    spans = [pl.ds(part * rows, rows) for part in range(parts)]
-    copies = fetched([(features.at[span], held.at[span]) for span in spans], sems)
+def moments_kernel(features, out, held):
+    rows = features.shape[0] // 4
     sums, squares = 0.0, 0.0
-    for part, copy in enumerate(copies):
-        copy.wait()
-        more = column_sums(held[part * rows : (part + 1) * rows, :].astype(jnp.float32))
+    for part in range(4):
+        values = features[part * rows : (part + 1) * rows, :]
+        held[part * rows : (part + 1) * rows, :] = values
+        more = column_sums(values.astype(jnp.float32))
         sums, squares = sums + more[0], squares + more[1]
     out[...] = jnp.broadcast_to(packed_moments(sums, squares), out.shape)
 
 
 def moments(features):
-    parts = 4
-    return pl.pallas_call(
-        functools.partial(moments_kernel, parts),
-        in_specs=[FAR],
+    return pl.pallas_call(
+        moments_kernel,
         out_shape=(
             jax.ShapeDtypeStruct((lax.axis_size("lat"), LANES), jnp.float32),
             jax.ShapeDtypeStruct(features.shape, features.dtype),
         ),
-        scratch_shapes=[pltpu.SemaphoreType.DMA((parts,))],
         compiler_params=pltpu.CompilerParams(vmem_limit_bytes=VMEM_BYTES),
     )(features)
 
@@ -332,57 +328,54 @@
 
 def attention_kernel(count, *refs):
     blocks = refs[:count]
-    pooled, table, qkv_weight, proj_weight, out, keys, values = refs[count:]
+    pooled, table, qkv_weight, proj_weight, out, normed, projected = refs[count:]
     tokens, channels = pooled.shape
-    group_width = channels // GROUPS
-    sums = jnp.zeros((8, channels), jnp.float32)
-    squares = jnp.zeros((8, channels), jnp.float32)
+    sums, squares = 0.0, 0.0
     for block in blocks:
-        entry = block[...].astype(jnp.float32).reshape(tokens // 8, 8, channels)
-        sums = sums + jnp.sum(entry, axis=0)
-        squares = squares + jnp.sum(entry * entry, axis=0)
-    sums = jnp.sum(sums, axis=0, keepdims=True)
-    squares = jnp.sum(squares, axis=0, keepdims=True)
+        more = column_sums(block[...].astype(jnp.float32))
+        sums, squares = sums + more[0], squares + more[1]
     row = lax.broadcasted_iota(jnp.int32, (8, channels), 0)
-    moments = group_total(jnp.where(row == 0, sums, squares)) / (count * tokens * group_width)
+    entries = count * tokens * (channels // GROUPS)
+    moments = group_total(jnp.where(row == 0, sums, squares)) / entries
     center = moments[0:1]
-    spread = moments[1:2] - center * center
-    factor = lax.rsqrt(spread + eps) * table[GAIN + 2 : GAIN + 3]
+    factor = lax.rsqrt(moments[1:2] - center * center + eps) * table[GAIN + 2 : GAIN + 3]
     offset = table[BIAS + 2 : BIAS + 3]
 
-    def normed(entry):
-        return ((entry.astype(jnp.float32) - center) * factor + offset).astype(jnp.bfloat16)
+    def norm(values):
+        return ((values.astype(jnp.float32) - center) * factor + offset).astype(jnp.bfloat16)
 
     for i, block in enumerate(blocks):
-        projected = jnp.dot(
-            normed(block[...]), qkv_weight[:, channels:], preferred_element_type=jnp.float32
-        ).astype(jnp.bfloat16)
-        keys[i * tokens : (i + 1) * tokens, :] = projected[:, :channels]
-        values[i * tokens : (i + 1) * tokens, :] = projected[:, channels:]
+        normed[i * tokens : (i + 1) * tokens, :] = norm(block[...])
+    projected[...] = jnp.dot(
+        normed[...], qkv_weight[:, channels:], preferred_element_type=jnp.float32
+    ).astype(jnp.bfloat16)
     queries = jnp.dot(
-        normed(pooled[...]), qkv_weight[:, :channels], preferred_element_type=jnp.float32
+        norm(pooled[...]), qkv_weight[:, :channels], preferred_element_type=jnp.float32
     ).astype(jnp.bfloat16) * jnp.bfloat16(HEAD_DIM ** (-0.5))
     first = lax.broadcasted_iota(jnp.int32, (tokens, 2 * HEAD_DIM), 1) < HEAD_DIM
-    attended = []
-    for start in range(0, channels, 2 * HEAD_DIM):
-        pair = slice(start, start + 2 * HEAD_DIM)
-        query = queries[:, pair]
+    starts = range(0, channels, 2 * HEAD_DIM)
+
+    def scored(start):
+        query = queries[:, start : start + 2 * HEAD_DIM]
         zero = jnp.zeros_like(query)
         both = jnp.concatenate([jnp.where(first, query, zero), jnp.where(first, zero, query)], axis=0)
-        scores = lax.dot_general(
-            both, keys[:, pair], (((1,), (1,)), ((), ())), preferred_element_type=jnp.float32
-        )
+        keys = projected[:, start : start + 2 * HEAD_DIM]
+        return lax.dot_general(both, keys, (((1,), (1,)), ((), ())), preferred_element_type=jnp.float32)
+
+    attended = []
+    later = scored(0)
+    for start in starts:
+        scores = later
+        if start + 2 * HEAD_DIM < channels:
+            later = scored(start + 2 * HEAD_DIM)
         weights = jnp.exp(scores - jnp.max(scores, axis=1, keepdims=True))
         totals = jnp.sum(weights, axis=1, keepdims=True)
-        blended = (
-            jnp.dot(weights.astype(jnp.bfloat16), values[:, pair], preferred_element_type=jnp.float32)
-            / totals
-        )
+        values = projected[:, channels + start : channels + start + 2 * HEAD_DIM]
+        blended = jnp.dot(weights.astype(jnp.bfloat16), values, preferred_element_type=jnp.float32) / totals
         attended.append(jnp.where(first, blended[:tokens], blended[tokens:]).astype(jnp.bfloat16))
-    projected = jnp.dot(
-        jnp.concatenate(attended, axis=1), proj_weight[...], preferred_element_type=jnp.float32
-    )
-    out[...] = ((pooled[...] + projected + table[PROJ_BIAS : PROJ_BIAS + 1]) * skip_gain).astype(jnp.bfloat16)
+    result = jnp.dot(jnp.concatenate(attended, axis=1), proj_weight[...], preferred_element_type=jnp.float32)
+    result = pooled[...] + result + table[PROJ_BIAS : PROJ_BIAS + 1]
+    out[...] = (result * skip_gain).astype(jnp.bfloat16)
 
 
 def attention(blocks, pooled, table, qkv_weight, proj_weight):
@@ -393,16 +386,10 @@
         out_shape=jax.ShapeDtypeStruct((tokens, channels), jnp.bfloat16),
         scratch_shapes=[
             pltpu.VMEM((count * tokens, channels), jnp.bfloat16),
-            pltpu.VMEM((count * tokens, channels), jnp.bfloat16),
+            pltpu.VMEM((count * tokens, 2 * channels), jnp.bfloat16),
         ],
         compiler_params=pltpu.CompilerParams(vmem_limit_bytes=(12 + count) * 1024 * 1024),
-    )(
-        *blocks,
-        pooled,
-        table,
-        qkv_weight,
-        proj_weight,
-    )
+    )(*blocks, pooled, table, qkv_weight, proj_weight)
 
 
 def local(

time: 66.5 us -> 64.7 us (0.973)
  Pallas kernels: 22.2 us -> 20.5 us
    pallas_call x1, Pallas kernels: 6.51 us -> 5.29 us  [attention(): pl.pallas_call(functools.partial(attention_kernel, count), out_shape=jax....]
where the time goes in v5:
time: 64.7 us; the launch traced here: 64.4 us
  starting transfers between devices  23.9 us (37%)
  Pallas kernels  20.5 us (32%)
  waiting for transfers between devices  16.6 us (26%)
  local copies, waits for them, and re-layouts  1.91 us (3%)
  between operations  0.78 us (1%)
  other arithmetic  0.76 us (1%)
    all_to_all x2, starting transfers between devices, shared(): lax.all_to_all(rows.reshape(count, 1, lanes), 'lat', 0, 0)  13 us
    ppermute x15, waiting for transfers between devices, exchange(): return lax.ppermute(block, 'lat', [(i, i ^ stride) for i in range(count)])  10.5 us
    ppermute x15, starting transfers between devices, exchange(): return lax.ppermute(block, 'lat', [(i, i ^ stride) for i in range(count)])  9.71 us
    pallas_call x2, Pallas kernels, first_convolution(): pl.pallas_call(functools.partial(first_kernel, height, breadth, outer), i...  8.9 us
    all_to_all x2, waiting for transfers between devices, shared(): lax.all_to_all(rows.reshape(count, 1, lanes), 'lat', 0, 0)  6.05 us
    pallas_call x1, Pallas kernels, attention(): pl.pallas_call(functools.partial(attention_kernel, count), out_shape=jax....  5.29 us
    pallas_call x1, Pallas kernels, second_convolution(): pl.pallas_call(functools.partial(second_kernel, height, breadth), in_spec...  4.43 us
    unnamed x12, local copies, waits for them, and re-layouts  1.91 us
  transfers between devices with their start and end apart: 19, of which 8 were waited for; matrix products, arithmetic and copies ran while one was open for 1% of the time, Pallas kernels for 7%

profile of v5, /device:TPU:0, one launch (start us, length us, event | category | flops | bytes accessed | tf_op | source)
XLA Modules:
  0.0 64.4 jit_solution(8904735655075665700)
XLA Ops:
  0.0 0.0 copy-start.5
  0.0 0.0 copy-start.3
  0.0 1.0 %copy-done.3 = bf16[1,2,192,512]{3,2,1,0:T(8,128)(2,1)S(1)} copy-done((bf16[1,2,192,512]{3,2,1,0:T(8,128)(2,1)S(1)}, bf16[1,2,192,512]{3,2,1,0:T(8,128)(2,1)}, u32[]{:S(2)}) %copy-start.3) | copy-done | bytes 393240
  1.0 0.0 copy-start.4
  1.0 1.0 %shard_map.118 = (f32[16,128]{1,0:T(8,128)}, bf16[384,512]{1,0:T(8,128)(2,1)S(1)}) custom-call(bf16[384,512]{1,0:T(8,128)(2,1)S(1)} %bitcast.14), custom_call_target="tpu_custom_call" | custom-call | tf_op jit(solution)/shard_map/pallas_call | solution.py:120
  2.0 0.5 collective-permute-start
  2.5 0.7 %collective-permute-start.1 = (bf16[384,512]{1,0:T(8,128)(2,1)S(1)}, bf16[384,512]{1,0:T(8,128)(2,1)S(1)}, u32[]{:S(2)}, u32[]{:S(2)}) collective-permute-start(bf16[384,512]{1,0:T(8,128)(2,1)S(1)} %get-tuple-element.11.own), channel_id=1, source_target_pairs={{1,2},{2,1},{3,4},{4,3},{5,6},{6,5},{7,8},{8,7},{9,10},{10,9},{11,... | collective-permute-start | bytes 1179656 | tf_op jit(solution)/shard_map/ppermute | solution.py:414
  3.2 8.8 %all-to-all-start = ((f32[16,1,128]{2,1,0:T(1,128)}), f32[16,1,128]{2,1,0:T(1,128)S(1)}, u32[]{:S(2)}, u32[]{:S(2)}) async-start(f32[16,1,128]{2,1,0:T(1,128)} %bitcast.2), calls=%async_computation | async-start | bytes 16384 | tf_op jit(solution)/shard_map/all_to_all | solution.py:98
  12.0 0.8 %pad_maximum_fusion.table.refs_17_ = f32[9,512]{1,0:T(8,128)S(1)} fusion(f32[1,512]{1,0:T(1,128)} %bitcast.21, f32[2,512]{1,0:T(2,128)} %param.20, f32[3,512]{1,0:T(4,128)} %param.17, f32[3,512]{1,0:T(4,128)} %param.16), kind=kLoop, calls=%fused_computation | loop fusion | flops 13824 | bytes 36864 | tf_op jit(solution)/shard_map/concatenate | solution.py:411
  12.7 5.6 %all-to-all-done = f32[16,1,128]{2,1,0:T(1,128)S(1)} async-done(((f32[16,1,128]{2,1,0:T(1,128)}), f32[16,1,128]{2,1,0:T(1,128)S(1)}, u32[]{:S(2)}, u32[]{:S(2)}) %all-to-all-start) | async-done | bytes 8224 | tf_op jit(solution)/shard_map/all_to_all | solution.py:98
  18.3 0.3 shard_map.119.norm
  18.6 0.0 collective-permute-done.mate
  18.6 0.0 collective-permute-done.1.other
  18.6 4.9 %shard_map.120 = (f32[384,512]{1,0:T(8,128)S(1)}, f32[16,128]{1,0:T(8,128)}) custom-call(bf16[384,512]{1,0:T(8,128)(2,1)S(1)} %get-tuple-element.11.own, f32[3,512]{1,0:T(4,128)S(1)} %shard_map.119.norm, f32[9,512]{1,0:T(8,128)S(1)} %pad_maximum_fusion.table.refs_17_, bf16[3,1536,512]{2,1,0:T(8,128)(2,1)} %bitcast.18, ...), custom_call_target="tpu_custom_call" | custom-call | tf_op jit(solution)/shard_map/pallas_call | solution.py:232
  23.5 4.2 %all-to-all-start.1 = ((f32[16,1,128]{2,1,0:T(1,128)}), f32[16,1,128]{2,1,0:T(1,128)S(1)}, u32[]{:S(2)}, u32[]{:S(2)}) async-start(f32[16,1,128]{2,1,0:T(1,128)} %bitcast.7), calls=%async_computation.1 | async-start | bytes 16384 | tf_op jit(solution)/shard_map/all_to_all | solution.py:98
  28.4 0.0 copy-done.5
  28.4 0.0 copy-done.4
  28.4 0.3 shard_map.122.refs_0_
  28.7 4.0 %shard_map.121.outer = f32[384,512]{1,0:T(8,128)S(1)} custom-call(bf16[384,512]{1,0:T(8,128)(2,1)S(1)} %get-tuple-element.11.own, f32[3,512]{1,0:T(4,128)S(1)} %shard_map.119.norm, f32[9,512]{1,0:T(8,128)S(1)} %pad_maximum_fusion.table.refs_17_, bf16[3,1536,512]{2,1,0:T(8,128)(2,1)} %bitcast.19, bf16[384,512]{1,0:T(8,128)(2,1)S(1)} %collective-permute-done.mate, ...), custom_call_target="tpu_custom_call" | custom-call | tf_op jit(solution)/shard_map/pallas_call | solution.py:232
  32.7 0.0 copy-start
  32.7 0.9 %copy-done = f32[384,512]{1,0:T(8,128)} copy-done((f32[384,512]{1,0:T(8,128)}, f32[384,512]{1,0:T(8,128)S(1)}, u32[]{:S(2)}) %copy-start) | copy-done | bytes 786456
  33.6 0.0 copy-start.1
  33.6 0.0 copy-start.2
  33.6 0.5 all-to-all-done.1
  34.1 0.3 shard_map.123.norm
  34.4 4.4 %shard_map.124 = (f32[96,512]{1,0:T(8,128)S(1)}, bf16[96,512]{1,0:T(8,128)(2,1)S(1)}) custom-call(f32[384,512]{1,0:T(8,128)S(1)} %get-tuple-element.13.first, f32[384,512]{1,0:T(8,128)} %copy-done, bf16[384,512]{1,0:T(8,128)(2,1)S(1)} %get-tuple-element.11.own, f32[3,512]{1,0:T(4,128)S(1)} %shard_map.123.norm, f32[9,512]{1,0:T(8,128)S(1)} %pad_maximum_fusion.table.refs_17_, ...), custom_call_target="tpu_custom_call" | custom-call | tf_op jit(solution)/shard_map/pallas_call | solution.py:297
  38.8 1.7 %collective-permute-start.2 = (bf16[96,512]{1,0:T(8,128)(2,1)S(1)}, bf16[96,512]{1,0:T(8,128)(2,1)S(1)}, u32[]{:S(2)}, u32[]{:S(2)}) collective-permute-start(bf16[96,512]{1,0:T(8,128)(2,1)S(1)} %get-tuple-element.15.refs_0_), channel_id=1, source_target_pairs={{0,4},{1,5},{2,6},{3,7},{4,0},{5,1},{6,2},{7,3},{8,12},{9,13},{10,... | collective-permute-start | bytes 294920 | tf_op jit(solution)/shard_map/ppermute | solution.py:319
  40.5 2.4 %collective-permute-start.3 = (bf16[96,512]{1,0:T(8,128)(2,1)S(1)}, bf16[96,512]{1,0:T(8,128)(2,1)S(1)}, u32[]{:S(2)}, u32[]{:S(2)}) collective-permute-start(bf16[96,512]{1,0:T(8,128)(2,1)S(1)} %get-tuple-element.15.refs_0_), channel_id=1, source_target_pairs={{0,8},{1,9},{2,10},{3,11},{4,12},{5,13},{6,14},{7,15},{8,0},{9,1},... | collective-permute-start | bytes 294920 | tf_op jit(solution)/shard_map/ppermute | solution.py:319
  42.9 0.4 collective-permute-start.4
  43.3 1.6 %collective-permute-start.5 = (bf16[96,512]{1,0:T(8,128)(2,1)S(1)}, bf16[96,512]{1,0:T(8,128)(2,1)S(1)}, u32[]{:S(2)}, u32[]{:S(2)}) collective-permute-start(bf16[96,512]{1,0:T(8,128)(2,1)S(1)} %get-tuple-element.15.refs_0_), channel_id=1, source_target_pairs={{0,2},{1,3},{2,0},{3,1},{4,6},{5,7},{6,4},{7,5},{8,10},{9,11},{10,... | collective-permute-start | bytes 294920 | tf_op jit(solution)/shard_map/ppermute | solution.py:319
  44.9 0.0 collective-permute-start.9
  44.9 0.0 collective-permute-done.2.refs_1_
  44.9 0.5 collective-permute-start.6
  45.4 5.8 %collective-permute-done.3.refs_2_ = bf16[96,512]{1,0:T(8,128)(2,1)S(1)} collective-permute-done((bf16[96,512]{1,0:T(8,128)(2,1)S(1)}, bf16[96,512]{1,0:T(8,128)(2,1)S(1)}, u32[]{:S(2)}, u32[]{:S(2)}) %collective-permute-start.3) | collective-permute-done | bytes 98336 | tf_op jit(solution)/shard_map/ppermute | solution.py:319
  51.2 1.5 %collective-permute-start.7 = (bf16[96,512]{1,0:T(8,128)(2,1)S(1)}, bf16[96,512]{1,0:T(8,128)(2,1)S(1)}, u32[]{:S(2)}, u32[]{:S(2)}) collective-permute-start(bf16[96,512]{1,0:T(8,128)(2,1)S(1)} %collective-permute-done.3.refs_2_), channel_id=1, source_target_pairs={{0,2},{1,3},{2,0},{3,1},{4,6},{5,7},{6,4},{7,5},{8,10},{9,11},{10,... | collective-permute-start | bytes 294920 | tf_op jit(solution)/shard_map/ppermute | solution.py:319
  52.7 0.0 collective-permute-done.4.refs_3_
  52.7 0.6 collective-permute-start.8
  53.2 0.0 collective-permute-done.5.refs_4_
  53.2 0.0 collective-permute-start.10
  53.2 0.0 collective-permute-done.9.refs_8_
  53.2 0.5 collective-permute-start.11
  53.8 0.0 collective-permute-done.6.refs_5_
  53.8 0.1 collective-permute-start.12
  53.8 2.0 %collective-permute-done.7.refs_6_ = bf16[96,512]{1,0:T(8,128)(2,1)S(1)} collective-permute-done((bf16[96,512]{1,0:T(8,128)(2,1)S(1)}, bf16[96,512]{1,0:T(8,128)(2,1)S(1)}, u32[]{:S(2)}, u32[]{:S(2)}) %collective-permute-start.7) | collective-permute-done | bytes 98336 | tf_op jit(solution)/shard_map/ppermute | solution.py:319
  55.8 0.0 collective-permute-start.13
  55.8 1.5 %collective-permute-done.8.refs_7_ = bf16[96,512]{1,0:T(8,128)(2,1)S(1)} collective-permute-done((bf16[96,512]{1,0:T(8,128)(2,1)S(1)}, bf16[96,512]{1,0:T(8,128)(2,1)S(1)}, u32[]{:S(2)}, u32[]{:S(2)}) %collective-permute-start.8) | collective-permute-done | bytes 98336 | tf_op jit(solution)/shard_map/ppermute | solution.py:319
  57.3 0.0 collective-permute-start.14
  57.3 0.0 collective-permute-done.10.refs_9_
  57.3 0.5 collective-permute-start.15
  57.8 0.0 collective-permute-done.11.refs_10_
  57.8 0.1 collective-permute-start.16
  57.9 0.0 collective-permute-done.12.refs_11_
  57.9 0.0 collective-permute-done.13.refs_12_
  57.9 0.7 %collective-permute-done.14.refs_13_ = bf16[96,512]{1,0:T(8,128)(2,1)S(1)} collective-permute-done((bf16[96,512]{1,0:T(8,128)(2,1)S(1)}, bf16[96,512]{1,0:T(8,128)(2,1)S(1)}, u32[]{:S(2)}, u32[]{:S(2)}) %collective-permute-start.14) | collective-permute-done | bytes 98336 | tf_op jit(solution)/shard_map/ppermute | solution.py:319
  58.6 0.2 collective-permute-done.15.refs_14_
  58.7 0.4 collective-permute-done.16.refs_15_
  59.1 0.0 copy-done.1
  59.1 0.0 copy-done.2
  59.1 5.3 %shard_map.125 = bf16[96,512]{1,0:T(8,128)(2,1)} custom-call(bf16[96,512]{1,0:T(8,128)(2,1)S(1)} %get-tuple-element.15.refs_0_, bf16[96,512]{1,0:T(8,128)(2,1)S(1)} %collective-permute-done.2.refs_1_, bf16[96,512]{1,0:T(8,128)(2,1)S(1)} %collective-permute-done.3.refs_2_, bf16[96,512]{1,0:T(8,128)(2,1)S(1)} %collective-permute-done.4.refs_3_, ...), custom_call_target="tpu_custom_call" | custom-call | tf_op jit(solution)/shard_map/pallas_call | solution.py:384
Async XLA Ops:
  0.0 28.4 %copy-start.5 = (f32[18]{0:T(128)S(1)}, f32[18]{0:T(128)}, u32[]{:S(2)}) copy-start(f32[18]{0:T(128)} %param.14) | copy-start | bytes 220
  0.0 1.0 %copy-start.3 = (bf16[1,2,192,512]{3,2,1,0:T(8,128)(2,1)S(1)}, bf16[1,2,192,512]{3,2,1,0:T(8,128)(2,1)}, u32[]{:S(2)}) copy-start(bf16[1,2,192,512]{3,2,1,0:T(8,128)(2,1)} %param.12) | copy-start | bytes 1179652
  1.0 27.4 %copy-start.4 = (bf16[128,1024]{1,0:T(8,128)(2,1)S(1)}, bf16[128,1024]{1,0:T(8,128)(2,1)}, u32[]{:S(2)}) copy-start(bf16[128,1024]{1,0:T(8,128)(2,1)} %affine_weight.1) | copy-start | bytes 786436
  2.0 16.6 %collective-permute-start = (bf16[384,512]{1,0:T(8,128)(2,1)S(1)}, bf16[384,512]{1,0:T(8,128)(2,1)S(1)}, u32[]{:S(2)}, u32[]{:S(2)}) collective-permute-start(bf16[384,512]{1,0:T(8,128)(2,1)S(1)} %get-tuple-element.11.own), channel_id=1, source_target_pairs={{0,1},{1,0},{2,3},{3,2},{4,5},{5,4},{6,7},{7,6},{8,9},{9,8},{10,11... | collective-permute-start | bytes 1179656 | tf_op jit(solution)/shard_map/ppermute | solution.py:413
  2.5 16.1 %collective-permute-start.1 = (bf16[384,512]{1,0:T(8,128)(2,1)S(1)}, bf16[384,512]{1,0:T(8,128)(2,1)S(1)}, u32[]{:S(2)}, u32[]{:S(2)}) collective-permute-start(bf16[384,512]{1,0:T(8,128)(2,1)S(1)} %get-tuple-element.11.own), channel_id=1, source_target_pairs={{1,2},{2,1},{3,4},{4,3},{5,6},{6,5},{7,8},{8,7},{9,10},{10,9},{11,... | collective-permute-start | bytes 1179656 | tf_op jit(solution)/shard_map/ppermute | solution.py:414
  3.2 15.1 %all-to-all-start = ((f32[16,1,128]{2,1,0:T(1,128)}), f32[16,1,128]{2,1,0:T(1,128)S(1)}, u32[]{:S(2)}, u32[]{:S(2)}) async-start(f32[16,1,128]{2,1,0:T(1,128)} %bitcast.2), calls=%async_computation | async-start | bytes 16384 | tf_op jit(solution)/shard_map/all_to_all | solution.py:98
  23.5 10.6 %all-to-all-start.1 = ((f32[16,1,128]{2,1,0:T(1,128)}), f32[16,1,128]{2,1,0:T(1,128)S(1)}, u32[]{:S(2)}, u32[]{:S(2)}) async-start(f32[16,1,128]{2,1,0:T(1,128)} %bitcast.7), calls=%async_computation.1 | async-start | bytes 16384 | tf_op jit(solution)/shard_map/all_to_all | solution.py:98
  32.7 0.9 %copy-start = (f32[384,512]{1,0:T(8,128)}, f32[384,512]{1,0:T(8,128)S(1)}, u32[]{:S(2)}) copy-start(f32[384,512]{1,0:T(8,128)S(1)} %shard_map.121.outer) | copy-start | bytes 2359300
  33.6 25.5 %copy-start.1 = (bf16[512,1536]{1,0:T(8,128)(2,1)S(1)}, bf16[512,1536]{1,0:T(8,128)(2,1)}, u32[]{:S(2)}) copy-start(bf16[512,1536]{1,0:T(8,128)(2,1)} %refs_18_.1) | copy-start | bytes 4718596
  33.6 25.5 %copy-start.2 = (bf16[512,512]{1,0:T(8,128)(2,1)S(1)}, bf16[512,512]{1,0:T(8,128)(2,1)}, u32[]{:S(2)}) copy-start(bf16[512,512]{1,0:T(8,128)(2,1)} %refs_19_.1) | copy-start | bytes 1572868
  38.8 6.1 %collective-permute-start.2 = (bf16[96,512]{1,0:T(8,128)(2,1)S(1)}, bf16[96,512]{1,0:T(8,128)(2,1)S(1)}, u32[]{:S(2)}, u32[]{:S(2)}) collective-permute-start(bf16[96,512]{1,0:T(8,128)(2,1)S(1)} %get-tuple-element.15.refs_0_), channel_id=1, source_target_pairs={{0,4},{1,5},{2,6},{3,7},{4,0},{5,1},{6,2},{7,3},{8,12},{9,13},{10,... | collective-permute-start | bytes 294920 | tf_op jit(solution)/shard_map/ppermute | solution.py:319
  40.5 10.7 %collective-permute-start.3 = (bf16[96,512]{1,0:T(8,128)(2,1)S(1)}, bf16[96,512]{1,0:T(8,128)(2,1)S(1)}, u32[]{:S(2)}, u32[]{:S(2)}) collective-permute-start(bf16[96,512]{1,0:T(8,128)(2,1)S(1)} %get-tuple-element.15.refs_0_), channel_id=1, source_target_pairs={{0,8},{1,9},{2,10},{3,11},{4,12},{5,13},{6,14},{7,15},{8,0},{9,1},... | collective-permute-start | bytes 294920 | tf_op jit(solution)/shard_map/ppermute | solution.py:319
  42.9 9.8 %collective-permute-start.4 = (bf16[96,512]{1,0:T(8,128)(2,1)S(1)}, bf16[96,512]{1,0:T(8,128)(2,1)S(1)}, u32[]{:S(2)}, u32[]{:S(2)}) collective-permute-start(bf16[96,512]{1,0:T(8,128)(2,1)S(1)} %get-tuple-element.15.refs_0_), channel_id=1, source_target_pairs={{0,12},{1,13},{2,14},{3,15},{4,8},{5,9},{6,10},{7,11},{8,4},{9,5},... | collective-permute-start | bytes 294920 | tf_op jit(solution)/shard_map/ppermute | solution.py:319
  43.3 10.0 %collective-permute-start.5 = (bf16[96,512]{1,0:T(8,128)(2,1)S(1)}, bf16[96,512]{1,0:T(8,128)(2,1)S(1)}, u32[]{:S(2)}, u32[]{:S(2)}) collective-permute-start(bf16[96,512]{1,0:T(8,128)(2,1)S(1)} %get-tuple-element.15.refs_0_), channel_id=1, source_target_pairs={{0,2},{1,3},{2,0},{3,1},{4,6},{5,7},{6,4},{7,5},{8,10},{9,11},{10,... | collective-permute-start | bytes 294920 | tf_op jit(solution)/shard_map/ppermute | solution.py:319
  44.9 8.4 %collective-permute-start.9 = (bf16[96,512]{1,0:T(8,128)(2,1)S(1)}, bf16[96,512]{1,0:T(8,128)(2,1)S(1)}, u32[]{:S(2)}, u32[]{:S(2)}) collective-permute-start(bf16[96,512]{1,0:T(8,128)(2,1)S(1)} %get-tuple-element.15.refs_0_), channel_id=1, source_target_pairs={{0,1},{1,0},{2,3},{3,2},{4,5},{5,4},{6,7},{7,6},{8,9},{9,8},{10,11... | collective-permute-start | bytes 294920 | tf_op jit(solution)/shard_map/ppermute | solution.py:319
  44.9 8.9 %collective-permute-start.6 = (bf16[96,512]{1,0:T(8,128)(2,1)S(1)}, bf16[96,512]{1,0:T(8,128)(2,1)S(1)}, u32[]{:S(2)}, u32[]{:S(2)}) collective-permute-start(bf16[96,512]{1,0:T(8,128)(2,1)S(1)} %collective-permute-done.2.refs_1_), channel_id=1, source_target_pairs={{0,2},{1,3},{2,0},{3,1},{4,6},{5,7},{6,4},{7,5},{8,10},{9,11},{10,... | collective-permute-start | bytes 294920 | tf_op jit(solution)/shard_map/ppermute | solution.py:319
  51.2 4.6 %collective-permute-start.7 = (bf16[96,512]{1,0:T(8,128)(2,1)S(1)}, bf16[96,512]{1,0:T(8,128)(2,1)S(1)}, u32[]{:S(2)}, u32[]{:S(2)}) collective-permute-start(bf16[96,512]{1,0:T(8,128)(2,1)S(1)} %collective-permute-done.3.refs_2_), channel_id=1, source_target_pairs={{0,2},{1,3},{2,0},{3,1},{4,6},{5,7},{6,4},{7,5},{8,10},{9,11},{10,... | collective-permute-start | bytes 294920 | tf_op jit(solution)/shard_map/ppermute | solution.py:319
  52.7 4.6 %collective-permute-start.8 = (bf16[96,512]{1,0:T(8,128)(2,1)S(1)}, bf16[96,512]{1,0:T(8,128)(2,1)S(1)}, u32[]{:S(2)}, u32[]{:S(2)}) collective-permute-start(bf16[96,512]{1,0:T(8,128)(2,1)S(1)} %collective-permute-done.4.refs_3_), channel_id=1, source_target_pairs={{0,2},{1,3},{2,0},{3,1},{4,6},{5,7},{6,4},{7,5},{8,10},{9,11},{10,... | collective-permute-start | bytes 294920 | tf_op jit(solution)/shard_map/ppermute | solution.py:319
  53.2 4.1 %collective-permute-start.10 = (bf16[96,512]{1,0:T(8,128)(2,1)S(1)}, bf16[96,512]{1,0:T(8,128)(2,1)S(1)}, u32[]{:S(2)}, u32[]{:S(2)}) collective-permute-start(bf16[96,512]{1,0:T(8,128)(2,1)S(1)} %collective-permute-done.2.refs_1_), channel_id=1, source_target_pairs={{0,1},{1,0},{2,3},{3,2},{4,5},{5,4},{6,7},{7,6},{8,9},{9,8},{10,11... | collective-permute-start | bytes 294920 | tf_op jit(solution)/shard_map/ppermute | solution.py:319
  53.2 4.6 %collective-permute-start.11 = (bf16[96,512]{1,0:T(8,128)(2,1)S(1)}, bf16[96,512]{1,0:T(8,128)(2,1)S(1)}, u32[]{:S(2)}, u32[]{:S(2)}) collective-permute-start(bf16[96,512]{1,0:T(8,128)(2,1)S(1)} %collective-permute-done.3.refs_2_), channel_id=1, source_target_pairs={{0,1},{1,0},{2,3},{3,2},{4,5},{5,4},{6,7},{7,6},{8,9},{9,8},{10,11... | collective-permute-start | bytes 294920 | tf_op jit(solution)/shard_map/ppermute | solution.py:319
  53.8 4.1 %collective-permute-start.12 = (bf16[96,512]{1,0:T(8,128)(2,1)S(1)}, bf16[96,512]{1,0:T(8,128)(2,1)S(1)}, u32[]{:S(2)}, u32[]{:S(2)}) collective-permute-start(bf16[96,512]{1,0:T(8,128)(2,1)S(1)} %collective-permute-done.4.refs_3_), channel_id=1, source_target_pairs={{0,1},{1,0},{2,3},{3,2},{4,5},{5,4},{6,7},{7,6},{8,9},{9,8},{10,11... | collective-permute-start | bytes 294920 | tf_op jit(solution)/shard_map/ppermute | solution.py:319
  55.8 2.1 %collective-permute-start.13 = (bf16[96,512]{1,0:T(8,128)(2,1)S(1)}, bf16[96,512]{1,0:T(8,128)(2,1)S(1)}, u32[]{:S(2)}, u32[]{:S(2)}) collective-permute-start(bf16[96,512]{1,0:T(8,128)(2,1)S(1)} %collective-permute-done.5.refs_4_), channel_id=1, source_target_pairs={{0,1},{1,0},{2,3},{3,2},{4,5},{5,4},{6,7},{7,6},{8,9},{9,8},{10,11... | collective-permute-start | bytes 294920 | tf_op jit(solution)/shard_map/ppermute | solution.py:319
  57.3 1.3 %collective-permute-start.14 = (bf16[96,512]{1,0:T(8,128)(2,1)S(1)}, bf16[96,512]{1,0:T(8,128)(2,1)S(1)}, u32[]{:S(2)}, u32[]{:S(2)}) collective-permute-start(bf16[96,512]{1,0:T(8,128)(2,1)S(1)} %collective-permute-done.6.refs_5_), channel_id=1, source_target_pairs={{0,1},{1,0},{2,3},{3,2},{4,5},{5,4},{6,7},{7,6},{8,9},{9,8},{10,11... | collective-permute-start | bytes 294920 | tf_op jit(solution)/shard_map/ppermute | solution.py:319
  57.3 1.5 %collective-permute-start.15 = (bf16[96,512]{1,0:T(8,128)(2,1)S(1)}, bf16[96,512]{1,0:T(8,128)(2,1)S(1)}, u32[]{:S(2)}, u32[]{:S(2)}) collective-permute-start(bf16[96,512]{1,0:T(8,128)(2,1)S(1)} %collective-permute-done.7.refs_6_), channel_id=1, source_target_pairs={{0,1},{1,0},{2,3},{3,2},{4,5},{5,4},{6,7},{7,6},{8,9},{9,8},{10,11... | collective-permute-start | bytes 294920 | tf_op jit(solution)/shard_map/ppermute | solution.py:319
  57.8 1.3 %collective-permute-start.16 = (bf16[96,512]{1,0:T(8,128)(2,1)S(1)}, bf16[96,512]{1,0:T(8,128)(2,1)S(1)}, u32[]{:S(2)}, u32[]{:S(2)}) collective-permute-start(bf16[96,512]{1,0:T(8,128)(2,1)S(1)} %collective-permute-done.8.refs_7_), channel_id=1, source_target_pairs={{0,1},{1,0},{2,3},{3,2},{4,5},{5,4},{6,7},{7,6},{8,9},{9,8},{10,11... | collective-permute-start | bytes 294920 | tf_op jit(solution)/shard_map/ppermute | solution.py:319

commit v6 on v5

--- a/solution.py
+++ b/solution.py
@@ -16,6 +16,8 @@
 GAIN, BIAS, CONV_BIAS, PROJ_BIAS = 0, 3, 6, 8
 VMEM_BYTES = 52 * 1024 * 1024
 SHADOW_BYTES = 256 * 1024 * 1024
+OUTER_BYTES = 52 * 1024 * 1024
+SECOND_BYTES = 51 * 1024 * 1024
 FAR = pl.BlockSpec(memory_space=pltpu.HBM)
 NEAR = pl.BlockSpec(memory_space=pltpu.VMEM)
 
@@ -127,12 +129,14 @@
     )(features)
 
 
-def shifted(line, breadth, lines, spread):
-    channels = line.shape[1]
-    lines[8 : 8 + breadth, :] = line
+def shifted(line, spread):
+    breadth, channels = line.shape
+    column = lax.broadcasted_iota(jnp.int32, line.shape, 0)
+    before = jnp.where(column == 0, 0.0, pltpu.roll(line, 1, 0))
+    after = jnp.where(column == breadth - 1, 0.0, pltpu.roll(line, breadth - 1, 0))
+    spread[:, :channels] = before.astype(jnp.bfloat16)
     spread[:, channels : 2 * channels] = line.astype(jnp.bfloat16)
-    spread[:, :channels] = lines[7 : 7 + breadth, :].astype(jnp.bfloat16)
-    spread[:, 2 * channels :] = lines[9 : 9 + breadth, :].astype(jnp.bfloat16)
+    spread[:, 2 * channels :] = after.astype(jnp.bfloat16)
 
 
 def affine_kernel(which, entries, sums, table, *refs):
@@ -180,14 +184,13 @@
         refs.pop(0)
     result = refs.pop(0)
     packed = None if outer else refs.pop(0)
-    weight, spread, lines, sems = refs
+    weight, spread, sems = refs
     count = lax.axis_size("lat")
     place = lax.axis_index("lat")
     odd = place % 2 == 1
     channels = own.shape[1]
     copies = tap_copies(taps, weight, sems)
     copies[0].start()
-    lines[...] = jnp.zeros_like(lines)
     center, factor, offset = norm[0:1, :], norm[1:2, :], norm[2:3, :]
     if outer:
         needed = [-2, -1, 0, height - 1, height, height + 1]
@@ -207,7 +210,7 @@
             values = jnp.where(place > 0, values, 0.0)
         elif row >= height:
             values = jnp.where(place < count - 1, values, 0.0)
-        shifted(values, breadth, lines, spread.at[i * breadth : (i + 1) * breadth, :])
+        shifted(values, spread.at[i * breadth : (i + 1) * breadth, :])
         if i in (1, 3):
             copies[(i + 1) // 2].start()
 
@@ -236,42 +239,33 @@
         scratch_shapes=[
             pltpu.VMEM((3, 3 * channels, channels), jnp.bfloat16),
             pltpu.VMEM((needed * breadth, 3 * channels), jnp.bfloat16),
-            pltpu.VMEM((breadth + 16, channels), jnp.float32),
             pltpu.SemaphoreType.DMA((3,)),
         ],
-        compiler_params=pltpu.CompilerParams(vmem_limit_bytes=VMEM_BYTES),
+        compiler_params=pltpu.CompilerParams(vmem_limit_bytes=OUTER_BYTES if outer else VMEM_BYTES),
     )(own, norm, table, weight.reshape(3, 3 * channels, channels), mate, other, *after)
 
 
 def second_kernel(
-    height, breadth, first, outer, own, norm, table, taps, pooled, sent, rows, weight, spread, lines, pairs, sems, weight_sems
+    height, breadth, first, outer, own, norm, table, taps, pooled, sent, weight, spread, pairs, sems
 ):
     count = lax.axis_size("lat")
     place = lax.axis_index("lat")
     channels = own.shape[1]
-    low, high = rows.at[pl.ds(0, breadth)], rows.at[pl.ds((height + 1) * breadth, breadth)]
-    copies = fetched(
-        [
-            (first, rows.at[pl.ds(breadth, height * breadth)]),
-            (outer.at[pl.ds(0, breadth)], low),
-            (outer.at[pl.ds(breadth, breadth)], high),
-        ],
-        sems,
-    )
-    weights = tap_copies(taps, weight, weight_sems)
+    weights = tap_copies(taps, weight, sems)
     weights[0].start()
-    lines[...] = jnp.zeros_like(lines)
     center, factor, offset = norm[0:1, :], norm[1:2, :], norm[2:3, :]
     for row in [*range(1, height + 1), 0, height + 1]:
-        if row in (0, 1, height + 1):
-            copies[{1: 0, 0: 1}.get(row, 2)].wait()
-        values = rows[row * breadth : (row + 1) * breadth, :]
+        if 0 < row <= height:
+            values = first[(row - 1) * breadth : row * breadth, :]
+        else:
+            at = 0 if row == 0 else breadth
+            values = outer[at : at + breadth, :]
         values = silu((values - center) * factor + offset)
         if row == 0:
             values = jnp.where(place > 0, values, 0.0)
         elif row == height + 1:
             values = jnp.where(place < count - 1, values, 0.0)
-        shifted(values, breadth, lines, spread.at[row * breadth : (row + 1) * breadth, :])
+        shifted(values, spread.at[row * breadth : (row + 1) * breadth, :])
         if row in (2, height + 1):
             weights[1 if row == 2 else 2].start()
     result = convolved(
@@ -296,21 +290,18 @@
     tokens = (height // 2) * (breadth // 2)
     return pl.pallas_call(
         functools.partial(second_kernel, height, breadth),
-        in_specs=[FAR] * 2 + [NEAR] * 3 + [FAR],
+        in_specs=[NEAR] * 5 + [FAR],
         out_shape=(
             jax.ShapeDtypeStruct((tokens, channels), jnp.float32),
             jax.ShapeDtypeStruct((tokens, channels), jnp.bfloat16),
         ),
         scratch_shapes=[
-            pltpu.VMEM(((height + 2) * breadth, channels), jnp.float32),
             pltpu.VMEM((3, 3 * channels, channels), jnp.bfloat16),
             pltpu.VMEM(((height + 2) * breadth, 3 * channels), jnp.bfloat16),
-            pltpu.VMEM((breadth + 16, channels), jnp.float32),
             pltpu.VMEM((breadth, LANES), jnp.float32),
             pltpu.SemaphoreType.DMA((3,)),
-            pltpu.SemaphoreType.DMA((3,)),
         ],
-        compiler_params=pltpu.CompilerParams(vmem_limit_bytes=VMEM_BYTES),
+        compiler_params=pltpu.CompilerParams(vmem_limit_bytes=SECOND_BYTES),
     )(first, outer, own, norm, table, weight.reshape(3, 3 * channels, channels))
 
 
@@ -418,7 +409,9 @@
     outer = first_convolution(height, breadth, *known, [packed])
     film = film_terms(noise_index, sigma_table, affine_weight, packed)
     norm = affine(1, height * breadth, shared(packed), table, film)
-    pooled, sent = second_convolution(height, breadth, first, outer, own, norm, table, conv2_weight)
+    pooled, sent = second_convolution(
+        height, breadth, first, outer, features.reshape(height * breadth, channels), norm, table, conv2_weight
+    )
     out = attention(gather_blocks(sent), pooled, table, qkv_weight, proj_weight)
     return out.reshape(members, height // 2, breadth // 2, channels)
 

time: 64.7 us -> 63.6 us (0.983)
  starting transfers between devices: 23.9 us -> 23 us
  local copies, waits for them, and re-layouts: 1.91 us -> 1.03 us
  waiting for transfers between devices: 16.6 us -> 17.4 us
    ppermute x15, starting transfers between devices: 9.71 us -> 8.74 us  [exchange(): return lax.ppermute(block, 'lat', [(i, i ^ stride) for i in range(count)])]
    all_to_all x2, waiting for transfers between devices: 6.05 us -> 6.97 us  [shared(): lax.all_to_all(rows.reshape(count, 1, lanes), 'lat', 0, 0)]
    unnamed x12, local copies, waits for them, and re-layouts: 1.91 us -> 1.03 us
  transfers between devices with their start and end apart: 19 -> 19, of which waited for: 8 -> 9; matrix products, arithmetic and copies ran while one was open for 1% -> 1% of each run, Pallas kernels for 7% -> 7%
where the time goes in v6:
time: 63.6 us; the launch traced here: 63.3 us
  starting transfers between devices  23 us (36%)
  Pallas kernels  20.3 us (32%)
  waiting for transfers between devices  17.4 us (27%)
  local copies, waits for them, and re-layouts  1.03 us (2%)
  between operations  0.79 us (1%)
  other arithmetic  0.76 us (1%)
    all_to_all x2, starting transfers between devices, shared(): lax.all_to_all(rows.reshape(count, 1, lanes), 'lat', 0, 0)  13.1 us
    ppermute x15, waiting for transfers between devices, exchange(): return lax.ppermute(block, 'lat', [(i, i ^ stride) for i in range(count)])  10.5 us
    pallas_call x2, Pallas kernels, first_convolution(): pl.pallas_call(functools.partial(first_kernel, height, breadth, outer), i...  8.86 us
    ppermute x15, starting transfers between devices, exchange(): return lax.ppermute(block, 'lat', [(i, i ^ stride) for i in range(count)])  8.74 us
    all_to_all x2, waiting for transfers between devices, shared(): lax.all_to_all(rows.reshape(count, 1, lanes), 'lat', 0, 0)  6.97 us
    pallas_call x1, Pallas kernels, attention(): pl.pallas_call(functools.partial(attention_kernel, count), out_shape=jax....  5.29 us
    pallas_call x1, Pallas kernels, second_convolution(): pl.pallas_call(functools.partial(second_kernel, height, breadth), in_spec...  4.24 us
  transfers between devices with their start and end apart: 19, of which 9 were waited for; matrix products, arithmetic and copies ran while one was open for 1% of the time, Pallas kernels for 7%

profile of v6, /device:TPU:0, one launch (start us, length us, event | category | flops | bytes accessed | tf_op | source)
XLA Modules:
  0.0 63.3 jit_solution(15606664767844550204)
XLA Ops:
  0.0 0.0 copy-start.5
  0.0 0.0 copy-start
  0.0 1.0 %copy-done = bf16[1,2,192,512]{3,2,1,0:T(8,128)(2,1)S(1)} copy-done((bf16[1,2,192,512]{3,2,1,0:T(8,128)(2,1)S(1)}, bf16[1,2,192,512]{3,2,1,0:T(8,128)(2,1)}, u32[]{:S(2)}) %copy-start) | copy-done | bytes 393240
  1.0 0.0 copy-start.4
  1.0 1.0 %shard_map.118 = (f32[16,128]{1,0:T(8,128)}, bf16[384,512]{1,0:T(8,128)(2,1)S(1)}) custom-call(bf16[384,512]{1,0:T(8,128)(2,1)S(1)} %bitcast.14), custom_call_target="tpu_custom_call" | custom-call | tf_op jit(solution)/shard_map/pallas_call | solution.py:122
  2.0 0.5 collective-permute-start
  2.5 0.7 %collective-permute-start.1 = (bf16[384,512]{1,0:T(8,128)(2,1)S(1)}, bf16[384,512]{1,0:T(8,128)(2,1)S(1)}, u32[]{:S(2)}, u32[]{:S(2)}) collective-permute-start(bf16[384,512]{1,0:T(8,128)(2,1)S(1)} %get-tuple-element.11.own), channel_id=1, source_target_pairs={{1,2},{2,1},{3,4},{4,3},{5,6},{6,5},{7,8},{8,7},{9,10},{10,9},{11,... | collective-permute-start | bytes 1179656 | tf_op jit(solution)/shard_map/ppermute | solution.py:405
  3.2 8.8 %all-to-all-start = ((f32[16,1,128]{2,1,0:T(1,128)}), f32[16,1,128]{2,1,0:T(1,128)S(1)}, u32[]{:S(2)}, u32[]{:S(2)}) async-start(f32[16,1,128]{2,1,0:T(1,128)} %bitcast.2), calls=%async_computation | async-start | bytes 16384 | tf_op jit(solution)/shard_map/all_to_all | solution.py:100
  12.0 0.8 %pad_maximum_fusion.table.refs_17_ = f32[9,512]{1,0:T(8,128)S(1)} fusion(f32[1,512]{1,0:T(1,128)} %bitcast.22, f32[2,512]{1,0:T(2,128)} %param.20, f32[3,512]{1,0:T(4,128)} %param.17, f32[3,512]{1,0:T(4,128)} %param.16), kind=kLoop, calls=%fused_computation | loop fusion | flops 13824 | bytes 36864 | tf_op jit(solution)/shard_map/concatenate | solution.py:402
  12.7 5.6 %all-to-all-done = f32[16,1,128]{2,1,0:T(1,128)S(1)} async-done(((f32[16,1,128]{2,1,0:T(1,128)}), f32[16,1,128]{2,1,0:T(1,128)S(1)}, u32[]{:S(2)}, u32[]{:S(2)}) %all-to-all-start) | async-done | bytes 8224 | tf_op jit(solution)/shard_map/all_to_all | solution.py:100
  18.3 0.3 shard_map.119.norm
  18.6 0.0 collective-permute-done.mate
  18.6 0.0 collective-permute-done.1.other
  18.6 4.9 %shard_map.120 = (f32[384,512]{1,0:T(8,128)S(1)}, f32[16,128]{1,0:T(8,128)}) custom-call(bf16[384,512]{1,0:T(8,128)(2,1)S(1)} %get-tuple-element.11.own, f32[3,512]{1,0:T(4,128)S(1)} %shard_map.119.norm, f32[9,512]{1,0:T(8,128)S(1)} %pad_maximum_fusion.table.refs_17_, bf16[3,1536,512]{2,1,0:T(8,128)(2,1)} %bitcast.19, ...), custom_call_target="tpu_custom_call" | custom-call | tf_op jit(solution)/shard_map/pallas_call | solution.py:235
  23.5 0.0 copy-start.1
  23.5 4.4 %all-to-all-start.1 = ((f32[16,1,128]{2,1,0:T(1,128)}), f32[16,1,128]{2,1,0:T(1,128)S(1)}, u32[]{:S(2)}, u32[]{:S(2)}) async-start(f32[16,1,128]{2,1,0:T(1,128)} %bitcast.7), calls=%async_computation.1 | async-start | bytes 16384 | tf_op jit(solution)/shard_map/all_to_all | solution.py:100
  28.6 0.0 copy-done.5
  28.6 0.0 copy-done.4
  28.6 0.3 shard_map.122.refs_0_
  28.8 4.0 %shard_map.121.outer = f32[384,512]{1,0:T(8,128)S(1)} custom-call(bf16[384,512]{1,0:T(8,128)(2,1)S(1)} %get-tuple-element.11.own, f32[3,512]{1,0:T(4,128)S(1)} %shard_map.119.norm, f32[9,512]{1,0:T(8,128)S(1)} %pad_maximum_fusion.table.refs_17_, bf16[3,1536,512]{2,1,0:T(8,128)(2,1)} %bitcast.20, bf16[384,512]{1,0:T(8,128)(2,1)S(1)} %collective-permute-done.mate, ...), custom_call_target="tpu_custom_call" | custom-call | tf_op jit(solution)/shard_map/pallas_call | solution.py:235
  32.8 0.0 copy-start.3
  32.8 1.4 %all-to-all-done.1 = f32[16,1,128]{2,1,0:T(1,128)S(1)} async-done(((f32[16,1,128]{2,1,0:T(1,128)}), f32[16,1,128]{2,1,0:T(1,128)S(1)}, u32[]{:S(2)}, u32[]{:S(2)}) %all-to-all-start.1) | async-done | bytes 8224 | tf_op jit(solution)/shard_map/all_to_all | solution.py:100
  34.2 0.0 copy-start.2
  34.2 0.3 shard_map.123.norm
  34.5 0.0 copy-done.1
  34.5 4.2 %shard_map.124 = (f32[96,512]{1,0:T(8,128)S(1)}, bf16[96,512]{1,0:T(8,128)(2,1)S(1)}) custom-call(f32[384,512]{1,0:T(8,128)S(1)} %get-tuple-element.13.first, f32[384,512]{1,0:T(8,128)S(1)} %shard_map.121.outer, bf16[384,512]{1,0:T(8,128)(2,1)S(1)} %bitcast.15, f32[3,512]{1,0:T(4,128)S(1)} %shard_map.123.norm, f32[9,512]{1,0:T(8,128)S(1)} %pad_maximum_fusion.table.refs_17_, ...), custom_call_target="tpu_custom_call" | custom-call | tf_op jit(solution)/shard_map/pallas_call | solution.py:291
  38.8 0.6 collective-permute-start.2
  39.4 2.4 %collective-permute-start.3 = (bf16[96,512]{1,0:T(8,128)(2,1)S(1)}, bf16[96,512]{1,0:T(8,128)(2,1)S(1)}, u32[]{:S(2)}, u32[]{:S(2)}) collective-permute-start(bf16[96,512]{1,0:T(8,128)(2,1)S(1)} %get-tuple-element.15.refs_0_), channel_id=1, source_target_pairs={{0,8},{1,9},{2,10},{3,11},{4,12},{5,13},{6,14},{7,15},{8,0},{9,1},... | collective-permute-start | bytes 294920 | tf_op jit(solution)/shard_map/ppermute | solution.py:310
  41.8 1.5 %collective-permute-start.4 = (bf16[96,512]{1,0:T(8,128)(2,1)S(1)}, bf16[96,512]{1,0:T(8,128)(2,1)S(1)}, u32[]{:S(2)}, u32[]{:S(2)}) collective-permute-start(bf16[96,512]{1,0:T(8,128)(2,1)S(1)} %get-tuple-element.15.refs_0_), channel_id=1, source_target_pairs={{0,12},{1,13},{2,14},{3,15},{4,8},{5,9},{6,10},{7,11},{8,4},{9,5},... | collective-permute-start | bytes 294920 | tf_op jit(solution)/shard_map/ppermute | solution.py:310
  43.3 0.6 collective-permute-start.5
  43.8 0.0 collective-permute-start.9
  43.8 0.9 %collective-permute-done.2.refs_1_ = bf16[96,512]{1,0:T(8,128)(2,1)S(1)} collective-permute-done((bf16[96,512]{1,0:T(8,128)(2,1)S(1)}, bf16[96,512]{1,0:T(8,128)(2,1)S(1)}, u32[]{:S(2)}, u32[]{:S(2)}) %collective-permute-start.2) | collective-permute-done | bytes 98336 | tf_op jit(solution)/shard_map/ppermute | solution.py:310
  44.7 0.5 collective-permute-start.6
  45.3 4.9 %collective-permute-done.3.refs_2_ = bf16[96,512]{1,0:T(8,128)(2,1)S(1)} collective-permute-done((bf16[96,512]{1,0:T(8,128)(2,1)S(1)}, bf16[96,512]{1,0:T(8,128)(2,1)S(1)}, u32[]{:S(2)}, u32[]{:S(2)}) %collective-permute-start.3) | collective-permute-done | bytes 98336 | tf_op jit(solution)/shard_map/ppermute | solution.py:310
  50.2 1.4 %collective-permute-start.7 = (bf16[96,512]{1,0:T(8,128)(2,1)S(1)}, bf16[96,512]{1,0:T(8,128)(2,1)S(1)}, u32[]{:S(2)}, u32[]{:S(2)}) collective-permute-start(bf16[96,512]{1,0:T(8,128)(2,1)S(1)} %collective-permute-done.3.refs_2_), channel_id=1, source_target_pairs={{0,2},{1,3},{2,0},{3,1},{4,6},{5,7},{6,4},{7,5},{8,10},{9,11},{10,... | collective-permute-start | bytes 294920 | tf_op jit(solution)/shard_map/ppermute | solution.py:310
  51.6 0.0 collective-permute-done.4.refs_3_
  51.6 0.6 collective-permute-start.8
  52.2 0.0 collective-permute-done.5.refs_4_
  52.2 0.0 collective-permute-start.10
  52.2 0.0 collective-permute-done.9.refs_8_
  52.2 0.5 collective-permute-start.11
  52.7 0.0 collective-permute-done.6.refs_5_
  52.7 0.1 collective-permute-start.12
  52.8 2.0 %collective-permute-done.7.refs_6_ = bf16[96,512]{1,0:T(8,128)(2,1)S(1)} collective-permute-done((bf16[96,512]{1,0:T(8,128)(2,1)S(1)}, bf16[96,512]{1,0:T(8,128)(2,1)S(1)}, u32[]{:S(2)}, u32[]{:S(2)}) %collective-permute-start.7) | collective-permute-done | bytes 98336 | tf_op jit(solution)/shard_map/ppermute | solution.py:310
  54.8 0.0 collective-permute-start.13
  54.8 1.4 %collective-permute-done.8.refs_7_ = bf16[96,512]{1,0:T(8,128)(2,1)S(1)} collective-permute-done((bf16[96,512]{1,0:T(8,128)(2,1)S(1)}, bf16[96,512]{1,0:T(8,128)(2,1)S(1)}, u32[]{:S(2)}, u32[]{:S(2)}) %collective-permute-start.8) | collective-permute-done | bytes 98336 | tf_op jit(solution)/shard_map/ppermute | solution.py:310
  56.2 0.0 collective-permute-start.14
  56.2 0.0 collective-permute-done.10.refs_9_
  56.2 0.5 collective-permute-start.15
  56.7 0.0 collective-permute-done.11.refs_10_
  56.7 0.1 collective-permute-start.16
  56.8 0.0 collective-permute-done.12.refs_11_
  56.8 0.0 collective-permute-done.13.refs_12_
  56.8 0.7 %collective-permute-done.14.refs_13_ = bf16[96,512]{1,0:T(8,128)(2,1)S(1)} collective-permute-done((bf16[96,512]{1,0:T(8,128)(2,1)S(1)}, bf16[96,512]{1,0:T(8,128)(2,1)S(1)}, u32[]{:S(2)}, u32[]{:S(2)}) %collective-permute-start.14) | collective-permute-done | bytes 98336 | tf_op jit(solution)/shard_map/ppermute | solution.py:310
  57.5 0.2 collective-permute-done.15.refs_14_
  57.7 0.4 collective-permute-done.16.refs_15_
  58.0 0.0 copy-done.3
  58.0 0.0 copy-done.2
  58.0 5.3 %shard_map.125 = bf16[96,512]{1,0:T(8,128)(2,1)} custom-call(bf16[96,512]{1,0:T(8,128)(2,1)S(1)} %get-tuple-element.15.refs_0_, bf16[96,512]{1,0:T(8,128)(2,1)S(1)} %collective-permute-done.2.refs_1_, bf16[96,512]{1,0:T(8,128)(2,1)S(1)} %collective-permute-done.3.refs_2_, bf16[96,512]{1,0:T(8,128)(2,1)S(1)} %collective-permute-done.4.refs_3_, ...), custom_call_target="tpu_custom_call" | custom-call | tf_op jit(solution)/shard_map/pallas_call | solution.py:375
Async XLA Ops:
  0.0 28.6 %copy-start.5 = (f32[18]{0:T(128)S(1)}, f32[18]{0:T(128)}, u32[]{:S(2)}) copy-start(f32[18]{0:T(128)} %param.14) | copy-start | bytes 220
  0.0 1.0 %copy-start = (bf16[1,2,192,512]{3,2,1,0:T(8,128)(2,1)S(1)}, bf16[1,2,192,512]{3,2,1,0:T(8,128)(2,1)}, u32[]{:S(2)}) copy-start(bf16[1,2,192,512]{3,2,1,0:T(8,128)(2,1)} %param.12) | copy-start | bytes 1179652
  1.0 27.6 %copy-start.4 = (bf16[128,1024]{1,0:T(8,128)(2,1)S(1)}, bf16[128,1024]{1,0:T(8,128)(2,1)}, u32[]{:S(2)}) copy-start(bf16[128,1024]{1,0:T(8,128)(2,1)} %affine_weight.1) | copy-start | bytes 786436
  2.0 16.6 %collective-permute-start = (bf16[384,512]{1,0:T(8,128)(2,1)S(1)}, bf16[384,512]{1,0:T(8,128)(2,1)S(1)}, u32[]{:S(2)}, u32[]{:S(2)}) collective-permute-start(bf16[384,512]{1,0:T(8,128)(2,1)S(1)} %get-tuple-element.11.own), channel_id=1, source_target_pairs={{0,1},{1,0},{2,3},{3,2},{4,5},{5,4},{6,7},{7,6},{8,9},{9,8},{10,11... | collective-permute-start | bytes 1179656 | tf_op jit(solution)/shard_map/ppermute | solution.py:404
  2.5 16.1 %collective-permute-start.1 = (bf16[384,512]{1,0:T(8,128)(2,1)S(1)}, bf16[384,512]{1,0:T(8,128)(2,1)S(1)}, u32[]{:S(2)}, u32[]{:S(2)}) collective-permute-start(bf16[384,512]{1,0:T(8,128)(2,1)S(1)} %get-tuple-element.11.own), channel_id=1, source_target_pairs={{1,2},{2,1},{3,4},{4,3},{5,6},{6,5},{7,8},{8,7},{9,10},{10,9},{11,... | collective-permute-start | bytes 1179656 | tf_op jit(solution)/shard_map/ppermute | solution.py:405
  3.2 15.1 %all-to-all-start = ((f32[16,1,128]{2,1,0:T(1,128)}), f32[16,1,128]{2,1,0:T(1,128)S(1)}, u32[]{:S(2)}, u32[]{:S(2)}) async-start(f32[16,1,128]{2,1,0:T(1,128)} %bitcast.2), calls=%async_computation | async-start | bytes 16384 | tf_op jit(solution)/shard_map/all_to_all | solution.py:100
  23.5 11.0 %copy-start.1 = (bf16[1,2,192,512]{3,2,1,0:T(8,128)(2,1)S(1)}, bf16[1,2,192,512]{3,2,1,0:T(8,128)(2,1)}, u32[]{:S(2)}) copy-start(bf16[1,2,192,512]{3,2,1,0:T(8,128)(2,1)} %param.12) | copy-start | bytes 1179652
  23.5 10.7 %all-to-all-start.1 = ((f32[16,1,128]{2,1,0:T(1,128)}), f32[16,1,128]{2,1,0:T(1,128)S(1)}, u32[]{:S(2)}, u32[]{:S(2)}) async-start(f32[16,1,128]{2,1,0:T(1,128)} %bitcast.7), calls=%async_computation.1 | async-start | bytes 16384 | tf_op jit(solution)/shard_map/all_to_all | solution.py:100
  32.8 25.2 %copy-start.3 = (bf16[512,512]{1,0:T(8,128)(2,1)S(1)}, bf16[512,512]{1,0:T(8,128)(2,1)}, u32[]{:S(2)}) copy-start(bf16[512,512]{1,0:T(8,128)(2,1)} %refs_19_.1) | copy-start | bytes 1572868
  34.2 23.8 %copy-start.2 = (bf16[512,1536]{1,0:T(8,128)(2,1)S(1)}, bf16[512,1536]{1,0:T(8,128)(2,1)}, u32[]{:S(2)}) copy-start(bf16[512,1536]{1,0:T(8,128)(2,1)} %refs_18_.1) | copy-start | bytes 4718596
  38.8 5.9 %collective-permute-start.2 = (bf16[96,512]{1,0:T(8,128)(2,1)S(1)}, bf16[96,512]{1,0:T(8,128)(2,1)S(1)}, u32[]{:S(2)}, u32[]{:S(2)}) collective-permute-start(bf16[96,512]{1,0:T(8,128)(2,1)S(1)} %get-tuple-element.15.refs_0_), channel_id=1, source_target_pairs={{0,4},{1,5},{2,6},{3,7},{4,0},{5,1},{6,2},{7,3},{8,12},{9,13},{10,... | collective-permute-start | bytes 294920 | tf_op jit(solution)/shard_map/ppermute | solution.py:310
  39.4 10.8 %collective-permute-start.3 = (bf16[96,512]{1,0:T(8,128)(2,1)S(1)}, bf16[96,512]{1,0:T(8,128)(2,1)S(1)}, u32[]{:S(2)}, u32[]{:S(2)}) collective-permute-start(bf16[96,512]{1,0:T(8,128)(2,1)S(1)} %get-tuple-element.15.refs_0_), channel_id=1, source_target_pairs={{0,8},{1,9},{2,10},{3,11},{4,12},{5,13},{6,14},{7,15},{8,0},{9,1},... | collective-permute-start | bytes 294920 | tf_op jit(solution)/shard_map/ppermute | solution.py:310
  41.8 9.8 %collective-permute-start.4 = (bf16[96,512]{1,0:T(8,128)(2,1)S(1)}, bf16[96,512]{1,0:T(8,128)(2,1)S(1)}, u32[]{:S(2)}, u32[]{:S(2)}) collective-permute-start(bf16[96,512]{1,0:T(8,128)(2,1)S(1)} %get-tuple-element.15.refs_0_), channel_id=1, source_target_pairs={{0,12},{1,13},{2,14},{3,15},{4,8},{5,9},{6,10},{7,11},{8,4},{9,5},... | collective-permute-start | bytes 294920 | tf_op jit(solution)/shard_map/ppermute | solution.py:310
  43.3 9.0 %collective-permute-start.5 = (bf16[96,512]{1,0:T(8,128)(2,1)S(1)}, bf16[96,512]{1,0:T(8,128)(2,1)S(1)}, u32[]{:S(2)}, u32[]{:S(2)}) collective-permute-start(bf16[96,512]{1,0:T(8,128)(2,1)S(1)} %get-tuple-element.15.refs_0_), channel_id=1, source_target_pairs={{0,2},{1,3},{2,0},{3,1},{4,6},{5,7},{6,4},{7,5},{8,10},{9,11},{10,... | collective-permute-start | bytes 294920 | tf_op jit(solution)/shard_map/ppermute | solution.py:310
  43.8 8.4 %collective-permute-start.9 = (bf16[96,512]{1,0:T(8,128)(2,1)S(1)}, bf16[96,512]{1,0:T(8,128)(2,1)S(1)}, u32[]{:S(2)}, u32[]{:S(2)}) collective-permute-start(bf16[96,512]{1,0:T(8,128)(2,1)S(1)} %get-tuple-element.15.refs_0_), channel_id=1, source_target_pairs={{0,1},{1,0},{2,3},{3,2},{4,5},{5,4},{6,7},{7,6},{8,9},{9,8},{10,11... | collective-permute-start | bytes 294920 | tf_op jit(solution)/shard_map/ppermute | solution.py:310
  44.7 8.0 %collective-permute-start.6 = (bf16[96,512]{1,0:T(8,128)(2,1)S(1)}, bf16[96,512]{1,0:T(8,128)(2,1)S(1)}, u32[]{:S(2)}, u32[]{:S(2)}) collective-permute-start(bf16[96,512]{1,0:T(8,128)(2,1)S(1)} %collective-permute-done.2.refs_1_), channel_id=1, source_target_pairs={{0,2},{1,3},{2,0},{3,1},{4,6},{5,7},{6,4},{7,5},{8,10},{9,11},{10,... | collective-permute-start | bytes 294920 | tf_op jit(solution)/shard_map/ppermute | solution.py:310
  50.2 4.6 %collective-permute-start.7 = (bf16[96,512]{1,0:T(8,128)(2,1)S(1)}, bf16[96,512]{1,0:T(8,128)(2,1)S(1)}, u32[]{:S(2)}, u32[]{:S(2)}) collective-permute-start(bf16[96,512]{1,0:T(8,128)(2,1)S(1)} %collective-permute-done.3.refs_2_), channel_id=1, source_target_pairs={{0,2},{1,3},{2,0},{3,1},{4,6},{5,7},{6,4},{7,5},{8,10},{9,11},{10,... | collective-permute-start | bytes 294920 | tf_op jit(solution)/shard_map/ppermute | solution.py:310
  51.6 4.6 %collective-permute-start.8 = (bf16[96,512]{1,0:T(8,128)(2,1)S(1)}, bf16[96,512]{1,0:T(8,128)(2,1)S(1)}, u32[]{:S(2)}, u32[]{:S(2)}) collective-permute-start(bf16[96,512]{1,0:T(8,128)(2,1)S(1)} %collective-permute-done.4.refs_3_), channel_id=1, source_target_pairs={{0,2},{1,3},{2,0},{3,1},{4,6},{5,7},{6,4},{7,5},{8,10},{9,11},{10,... | collective-permute-start | bytes 294920 | tf_op jit(solution)/shard_map/ppermute | solution.py:310
  52.2 4.0 %collective-permute-start.10 = (bf16[96,512]{1,0:T(8,128)(2,1)S(1)}, bf16[96,512]{1,0:T(8,128)(2,1)S(1)}, u32[]{:S(2)}, u32[]{:S(2)}) collective-permute-start(bf16[96,512]{1,0:T(8,128)(2,1)S(1)} %collective-permute-done.2.refs_1_), channel_id=1, source_target_pairs={{0,1},{1,0},{2,3},{3,2},{4,5},{5,4},{6,7},{7,6},{8,9},{9,8},{10,11... | collective-permute-start | bytes 294920 | tf_op jit(solution)/shard_map/ppermute | solution.py:310
  52.2 4.5 %collective-permute-start.11 = (bf16[96,512]{1,0:T(8,128)(2,1)S(1)}, bf16[96,512]{1,0:T(8,128)(2,1)S(1)}, u32[]{:S(2)}, u32[]{:S(2)}) collective-permute-start(bf16[96,512]{1,0:T(8,128)(2,1)S(1)} %collective-permute-done.3.refs_2_), channel_id=1, source_target_pairs={{0,1},{1,0},{2,3},{3,2},{4,5},{5,4},{6,7},{7,6},{8,9},{9,8},{10,11... | collective-permute-start | bytes 294920 | tf_op jit(solution)/shard_map/ppermute | solution.py:310
  52.7 4.1 %collective-permute-start.12 = (bf16[96,512]{1,0:T(8,128)(2,1)S(1)}, bf16[96,512]{1,0:T(8,128)(2,1)S(1)}, u32[]{:S(2)}, u32[]{:S(2)}) collective-permute-start(bf16[96,512]{1,0:T(8,128)(2,1)S(1)} %collective-permute-done.4.refs_3_), channel_id=1, source_target_pairs={{0,1},{1,0},{2,3},{3,2},{4,5},{5,4},{6,7},{7,6},{8,9},{9,8},{10,11... | collective-permute-start | bytes 294920 | tf_op jit(solution)/shard_map/ppermute | solution.py:310
  54.8 2.0 %collective-permute-start.13 = (bf16[96,512]{1,0:T(8,128)(2,1)S(1)}, bf16[96,512]{1,0:T(8,128)(2,1)S(1)}, u32[]{:S(2)}, u32[]{:S(2)}) collective-permute-start(bf16[96,512]{1,0:T(8,128)(2,1)S(1)} %collective-permute-done.5.refs_4_), channel_id=1, source_target_pairs={{0,1},{1,0},{2,3},{3,2},{4,5},{5,4},{6,7},{7,6},{8,9},{9,8},{10,11... | collective-permute-start | bytes 294920 | tf_op jit(solution)/shard_map/ppermute | solution.py:310
  56.2 1.3 %collective-permute-start.14 = (bf16[96,512]{1,0:T(8,128)(2,1)S(1)}, bf16[96,512]{1,0:T(8,128)(2,1)S(1)}, u32[]{:S(2)}, u32[]{:S(2)}) collective-permute-start(bf16[96,512]{1,0:T(8,128)(2,1)S(1)} %collective-permute-done.6.refs_5_), channel_id=1, source_target_pairs={{0,1},{1,0},{2,3},{3,2},{4,5},{5,4},{6,7},{7,6},{8,9},{9,8},{10,11... | collective-permute-start | bytes 294920 | tf_op jit(solution)/shard_map/ppermute | solution.py:310
  56.2 1.5 %collective-permute-start.15 = (bf16[96,512]{1,0:T(8,128)(2,1)S(1)}, bf16[96,512]{1,0:T(8,128)(2,1)S(1)}, u32[]{:S(2)}, u32[]{:S(2)}) collective-permute-start(bf16[96,512]{1,0:T(8,128)(2,1)S(1)} %collective-permute-done.7.refs_6_), channel_id=1, source_target_pairs={{0,1},{1,0},{2,3},{3,2},{4,5},{5,4},{6,7},{7,6},{8,9},{9,8},{10,11... | collective-permute-start | bytes 294920 | tf_op jit(solution)/shard_map/ppermute | solution.py:310
  56.7 1.3 %collective-permute-start.16 = (bf16[96,512]{1,0:T(8,128)(2,1)S(1)}, bf16[96,512]{1,0:T(8,128)(2,1)S(1)}, u32[]{:S(2)}, u32[]{:S(2)}) collective-permute-start(bf16[96,512]{1,0:T(8,128)(2,1)S(1)} %collective-permute-done.8.refs_7_), channel_id=1, source_target_pairs={{0,1},{1,0},{2,3},{3,2},{4,5},{5,4},{6,7},{7,6},{8,9},{9,8},{10,11... | collective-permute-start | bytes 294920 | tf_op jit(solution)/shard_map/ppermute | solution.py:310

commit v7 on v6

--- a/solution.py
+++ b/solution.py
@@ -400,9 +400,10 @@
     members, height, breadth, channels = features.shape
     count = lax.axis_size("lat")
     table = jnp.concatenate([norm_gain, norm_bias, conv_bias, proj_bias[None]], axis=0)
-    packed, own = moments(features.reshape(height * breadth, channels))
-    mate = lax.ppermute(own, "lat", [(i, i ^ 1) for i in range(count)])
-    other = lax.ppermute(own, "lat", [(i, (i - 1 ^ 1) + 1) for i in range(1, count - 1)])
+    cells = features.reshape(height * breadth, channels)
+    packed, own = moments(cells)
+    mate = lax.ppermute(cells, "lat", [(i, i ^ 1) for i in range(count)])
+    other = lax.ppermute(cells, "lat", [(i, (i - 1 ^ 1) + 1) for i in range(1, count - 1)])
     norm = affine(0, height * breadth, shared(packed), table)
     known = (own, norm, table, conv1_weight, mate, other)
     first, packed = first_convolution(height, breadth, *known)
@@ -410,7 +411,7 @@
     film = film_terms(noise_index, sigma_table, affine_weight, packed)
     norm = affine(1, height * breadth, shared(packed), table, film)
     pooled, sent = second_convolution(
-        height, breadth, first, outer, features.reshape(height * breadth, channels), norm, table, conv2_weight
+        height, breadth, first, outer, cells, norm, table, conv2_weight
     )
     out = attention(gather_blocks(sent), pooled, table, qkv_weight, proj_weight)
     return out.reshape(members, height // 2, breadth // 2, channels)

time: 63.6 us -> 62.8 us (0.987)
  transfers between devices with their start and end apart: 19 -> 19, of which waited for: 9 -> 9; matrix products, arithmetic and copies ran while one was open for 1% -> 1% of each run, Pallas kernels for 7% -> 9%
where the time goes in v7:
time: 62.8 us; the launch traced here: 62.5 us
  starting transfers between devices  22.4 us (36%)
  Pallas kernels  20.3 us (32%)
  waiting for transfers between devices  17.2 us (27%)
  local copies, waits for them, and re-layouts  1.01 us (2%)
  between operations  0.8 us (1%)
  other arithmetic  0.76 us (1%)
    all_to_all x2, starting transfers between devices, shared(): lax.all_to_all(rows.reshape(count, 1, lanes), 'lat', 0, 0)  12.6 us
    ppermute x15, waiting for transfers between devices, exchange(): return lax.ppermute(block, 'lat', [(i, i ^ stride) for i in range(count)])  10.4 us
    pallas_call x2, Pallas kernels, first_convolution(): pl.pallas_call(functools.partial(first_kernel, height, breadth, outer), i...  8.85 us
    ppermute x15, starting transfers between devices, exchange(): return lax.ppermute(block, 'lat', [(i, i ^ stride) for i in range(count)])  8.69 us
    all_to_all x2, waiting for transfers between devices, shared(): lax.all_to_all(rows.reshape(count, 1, lanes), 'lat', 0, 0)  6.77 us
    pallas_call x1, Pallas kernels, attention(): pl.pallas_call(functools.partial(attention_kernel, count), out_shape=jax....  5.29 us
    pallas_call x1, Pallas kernels, second_convolution(): pl.pallas_call(functools.partial(second_kernel, height, breadth), in_spec...  4.27 us
  transfers between devices with their start and end apart: 19, of which 9 were waited for; matrix products, arithmetic and copies ran while one was open for 1% of the time, Pallas kernels for 9%

profile of v7, /device:TPU:0, one launch (start us, length us, event | category | flops | bytes accessed | tf_op | source)
XLA Modules:
  0.0 62.5 jit_solution(15652536071987294101)
XLA Ops:
  0.0 0.0 copy-start.5
  0.0 0.5 collective-permute-start
  0.5 0.7 %collective-permute-start.1 = (bf16[384,512]{1,0:T(8,128)(2,1)}, bf16[384,512]{1,0:T(8,128)(2,1)S(1)}, u32[]{:S(2)}, u32[]{:S(2)}) collective-permute-start(bf16[384,512]{1,0:T(8,128)(2,1)} %bitcast.15), channel_id=1, source_target_pairs={{1,2},{2,1},{3,4},{4,3},{5,6},{6,5},{7,8},{8,7},{9,10},{10,9},{11,... | collective-permute-start | bytes 1179656 | tf_op jit(solution)/shard_map/ppermute | solution.py:406
  1.1 0.0 copy-start
  1.1 1.0 %copy-done = bf16[1,2,192,512]{3,2,1,0:T(8,128)(2,1)S(1)} copy-done((bf16[1,2,192,512]{3,2,1,0:T(8,128)(2,1)S(1)}, bf16[1,2,192,512]{3,2,1,0:T(8,128)(2,1)}, u32[]{:S(2)}) %copy-start) | copy-done | bytes 393240
  2.1 0.0 copy-start.4
  2.1 1.0 %shard_map.118 = (f32[16,128]{1,0:T(8,128)}, bf16[384,512]{1,0:T(8,128)(2,1)S(1)}) custom-call(bf16[384,512]{1,0:T(8,128)(2,1)S(1)} %bitcast.16), custom_call_target="tpu_custom_call" | custom-call | tf_op jit(solution)/shard_map/pallas_call | solution.py:122
  3.2 8.8 %all-to-all-start = ((f32[16,1,128]{2,1,0:T(1,128)}), f32[16,1,128]{2,1,0:T(1,128)S(1)}, u32[]{:S(2)}, u32[]{:S(2)}) async-start(f32[16,1,128]{2,1,0:T(1,128)} %bitcast.2), calls=%async_computation | async-start | bytes 16384 | tf_op jit(solution)/shard_map/all_to_all | solution.py:100
  12.0 0.8 %pad_maximum_fusion.table.refs_17_ = f32[9,512]{1,0:T(8,128)S(1)} fusion(f32[1,512]{1,0:T(1,128)} %bitcast.24, f32[2,512]{1,0:T(2,128)} %param.20, f32[3,512]{1,0:T(4,128)} %param.17, f32[3,512]{1,0:T(4,128)} %param.16), kind=kLoop, calls=%fused_computation | loop fusion | flops 13824 | bytes 36864 | tf_op jit(solution)/shard_map/concatenate | solution.py:402
  12.7 5.6 %all-to-all-done = f32[16,1,128]{2,1,0:T(1,128)S(1)} async-done(((f32[16,1,128]{2,1,0:T(1,128)}), f32[16,1,128]{2,1,0:T(1,128)S(1)}, u32[]{:S(2)}, u32[]{:S(2)}) %all-to-all-start) | async-done | bytes 8224 | tf_op jit(solution)/shard_map/all_to_all | solution.py:100
  18.3 0.3 shard_map.119.norm
  18.6 0.0 collective-permute-done.mate
  18.6 0.0 collective-permute-done.1.other
  18.6 4.9 %shard_map.120 = (f32[384,512]{1,0:T(8,128)S(1)}, f32[16,128]{1,0:T(8,128)}) custom-call(bf16[384,512]{1,0:T(8,128)(2,1)S(1)} %get-tuple-element.11.own, f32[3,512]{1,0:T(4,128)S(1)} %shard_map.119.norm, f32[9,512]{1,0:T(8,128)S(1)} %pad_maximum_fusion.table.refs_17_, bf16[3,1536,512]{2,1,0:T(8,128)(2,1)} %bitcast.21, ...), custom_call_target="tpu_custom_call" | custom-call | tf_op jit(solution)/shard_map/pallas_call | solution.py:235
  23.5 0.0 copy-start.1
  23.5 3.8 %all-to-all-start.1 = ((f32[16,1,128]{2,1,0:T(1,128)}), f32[16,1,128]{2,1,0:T(1,128)S(1)}, u32[]{:S(2)}, u32[]{:S(2)}) async-start(f32[16,1,128]{2,1,0:T(1,128)} %bitcast.7), calls=%async_computation.1 | async-start | bytes 16384 | tf_op jit(solution)/shard_map/all_to_all | solution.py:100
  28.0 0.0 copy-done.5
  28.0 0.0 copy-done.4
  28.0 0.3 shard_map.122.refs_0_
  28.3 4.0 %shard_map.121.outer = f32[384,512]{1,0:T(8,128)S(1)} custom-call(bf16[384,512]{1,0:T(8,128)(2,1)S(1)} %get-tuple-element.11.own, f32[3,512]{1,0:T(4,128)S(1)} %shard_map.119.norm, f32[9,512]{1,0:T(8,128)S(1)} %pad_maximum_fusion.table.refs_17_, bf16[3,1536,512]{2,1,0:T(8,128)(2,1)} %bitcast.22, bf16[384,512]{1,0:T(8,128)(2,1)S(1)} %collective-permute-done.mate, ...), custom_call_target="tpu_custom_call" | custom-call | tf_op jit(solution)/shard_map/pallas_call | solution.py:235
  32.2 0.0 copy-start.3
  32.2 1.2 %all-to-all-done.1 = f32[16,1,128]{2,1,0:T(1,128)S(1)} async-done(((f32[16,1,128]{2,1,0:T(1,128)}), f32[16,1,128]{2,1,0:T(1,128)S(1)}, u32[]{:S(2)}, u32[]{:S(2)}) %all-to-all-start.1) | async-done | bytes 8224 | tf_op jit(solution)/shard_map/all_to_all | solution.py:100
  33.4 0.0 copy-start.2
  33.4 0.3 shard_map.123.norm
  33.8 0.0 copy-done.1
  33.8 4.3 %shard_map.124 = (f32[96,512]{1,0:T(8,128)S(1)}, bf16[96,512]{1,0:T(8,128)(2,1)S(1)}) custom-call(f32[384,512]{1,0:T(8,128)S(1)} %get-tuple-element.13.first, f32[384,512]{1,0:T(8,128)S(1)} %shard_map.121.outer, bf16[384,512]{1,0:T(8,128)(2,1)S(1)} %bitcast.17, f32[3,512]{1,0:T(4,128)S(1)} %shard_map.123.norm, f32[9,512]{1,0:T(8,128)S(1)} %pad_maximum_fusion.table.refs_17_, ...), custom_call_target="tpu_custom_call" | custom-call | tf_op jit(solution)/shard_map/pallas_call | solution.py:291
  38.0 0.6 collective-permute-start.2
  38.6 2.4 %collective-permute-start.3 = (bf16[96,512]{1,0:T(8,128)(2,1)S(1)}, bf16[96,512]{1,0:T(8,128)(2,1)S(1)}, u32[]{:S(2)}, u32[]{:S(2)}) collective-permute-start(bf16[96,512]{1,0:T(8,128)(2,1)S(1)} %get-tuple-element.15.refs_0_), channel_id=1, source_target_pairs={{0,8},{1,9},{2,10},{3,11},{4,12},{5,13},{6,14},{7,15},{8,0},{9,1},... | collective-permute-start | bytes 294920 | tf_op jit(solution)/shard_map/ppermute | solution.py:310
  41.0 1.5 %collective-permute-start.4 = (bf16[96,512]{1,0:T(8,128)(2,1)S(1)}, bf16[96,512]{1,0:T(8,128)(2,1)S(1)}, u32[]{:S(2)}, u32[]{:S(2)}) collective-permute-start(bf16[96,512]{1,0:T(8,128)(2,1)S(1)} %get-tuple-element.15.refs_0_), channel_id=1, source_target_pairs={{0,12},{1,13},{2,14},{3,15},{4,8},{5,9},{6,10},{7,11},{8,4},{9,5},... | collective-permute-start | bytes 294920 | tf_op jit(solution)/shard_map/ppermute | solution.py:310
  42.5 0.5 collective-permute-start.5
  43.0 0.0 collective-permute-start.9
  43.0 1.0 %collective-permute-done.2.refs_1_ = bf16[96,512]{1,0:T(8,128)(2,1)S(1)} collective-permute-done((bf16[96,512]{1,0:T(8,128)(2,1)S(1)}, bf16[96,512]{1,0:T(8,128)(2,1)S(1)}, u32[]{:S(2)}, u32[]{:S(2)}) %collective-permute-start.2) | collective-permute-done | bytes 98336 | tf_op jit(solution)/shard_map/ppermute | solution.py:310
  44.0 0.5 collective-permute-start.6
  44.5 4.8 %collective-permute-done.3.refs_2_ = bf16[96,512]{1,0:T(8,128)(2,1)S(1)} collective-permute-done((bf16[96,512]{1,0:T(8,128)(2,1)S(1)}, bf16[96,512]{1,0:T(8,128)(2,1)S(1)}, u32[]{:S(2)}, u32[]{:S(2)}) %collective-permute-start.3) | collective-permute-done | bytes 98336 | tf_op jit(solution)/shard_map/ppermute | solution.py:310
  49.3 1.4 %collective-permute-start.7 = (bf16[96,512]{1,0:T(8,128)(2,1)S(1)}, bf16[96,512]{1,0:T(8,128)(2,1)S(1)}, u32[]{:S(2)}, u32[]{:S(2)}) collective-permute-start(bf16[96,512]{1,0:T(8,128)(2,1)S(1)} %collective-permute-done.3.refs_2_), channel_id=1, source_target_pairs={{0,2},{1,3},{2,0},{3,1},{4,6},{5,7},{6,4},{7,5},{8,10},{9,11},{10,... | collective-permute-start | bytes 294920 | tf_op jit(solution)/shard_map/ppermute | solution.py:310
  50.7 0.0 collective-permute-done.4.refs_3_
  50.8 0.6 collective-permute-start.8
  51.4 0.0 collective-permute-done.5.refs_4_
  51.4 0.0 collective-permute-start.10
  51.4 0.0 collective-permute-done.9.refs_8_
  51.4 0.5 collective-permute-start.11
  51.9 0.0 collective-permute-done.6.refs_5_
  51.9 0.1 collective-permute-start.12
  52.0 2.0 %collective-permute-done.7.refs_6_ = bf16[96,512]{1,0:T(8,128)(2,1)S(1)} collective-permute-done((bf16[96,512]{1,0:T(8,128)(2,1)S(1)}, bf16[96,512]{1,0:T(8,128)(2,1)S(1)}, u32[]{:S(2)}, u32[]{:S(2)}) %collective-permute-start.7) | collective-permute-done | bytes 98336 | tf_op jit(solution)/shard_map/ppermute | solution.py:310
  54.0 0.0 collective-permute-start.13
  54.0 1.4 %collective-permute-done.8.refs_7_ = bf16[96,512]{1,0:T(8,128)(2,1)S(1)} collective-permute-done((bf16[96,512]{1,0:T(8,128)(2,1)S(1)}, bf16[96,512]{1,0:T(8,128)(2,1)S(1)}, u32[]{:S(2)}, u32[]{:S(2)}) %collective-permute-start.8) | collective-permute-done | bytes 98336 | tf_op jit(solution)/shard_map/ppermute | solution.py:310
  55.4 0.0 collective-permute-start.14
  55.4 0.0 collective-permute-done.10.refs_9_
  55.4 0.5 collective-permute-start.15
  55.9 0.0 collective-permute-done.11.refs_10_
  55.9 0.1 collective-permute-start.16
  56.0 0.0 collective-permute-done.12.refs_11_
  56.0 0.0 collective-permute-done.13.refs_12_
  56.0 0.7 %collective-permute-done.14.refs_13_ = bf16[96,512]{1,0:T(8,128)(2,1)S(1)} collective-permute-done((bf16[96,512]{1,0:T(8,128)(2,1)S(1)}, bf16[96,512]{1,0:T(8,128)(2,1)S(1)}, u32[]{:S(2)}, u32[]{:S(2)}) %collective-permute-start.14) | collective-permute-done | bytes 98336 | tf_op jit(solution)/shard_map/ppermute | solution.py:310
  56.7 0.2 collective-permute-done.15.refs_14_
  56.8 0.4 collective-permute-done.16.refs_15_
  57.2 0.0 copy-done.3
  57.2 0.0 copy-done.2
  57.2 5.3 %shard_map.125 = bf16[96,512]{1,0:T(8,128)(2,1)} custom-call(bf16[96,512]{1,0:T(8,128)(2,1)S(1)} %get-tuple-element.15.refs_0_, bf16[96,512]{1,0:T(8,128)(2,1)S(1)} %collective-permute-done.2.refs_1_, bf16[96,512]{1,0:T(8,128)(2,1)S(1)} %collective-permute-done.3.refs_2_, bf16[96,512]{1,0:T(8,128)(2,1)S(1)} %collective-permute-done.4.refs_3_, ...), custom_call_target="tpu_custom_call" | custom-call | tf_op jit(solution)/shard_map/pallas_call | solution.py:375
Async XLA Ops:
  0.0 28.0 %copy-start.5 = (f32[18]{0:T(128)S(1)}, f32[18]{0:T(128)}, u32[]{:S(2)}) copy-start(f32[18]{0:T(128)} %param.14) | copy-start | bytes 220
  0.0 18.6 %collective-permute-start = (bf16[384,512]{1,0:T(8,128)(2,1)}, bf16[384,512]{1,0:T(8,128)(2,1)S(1)}, u32[]{:S(2)}, u32[]{:S(2)}) collective-permute-start(bf16[384,512]{1,0:T(8,128)(2,1)} %bitcast.14), channel_id=1, source_target_pairs={{0,1},{1,0},{2,3},{3,2},{4,5},{5,4},{6,7},{7,6},{8,9},{9,8},{10,11... | collective-permute-start | bytes 1179656 | tf_op jit(solution)/shard_map/ppermute | solution.py:405
  0.5 18.2 %collective-permute-start.1 = (bf16[384,512]{1,0:T(8,128)(2,1)}, bf16[384,512]{1,0:T(8,128)(2,1)S(1)}, u32[]{:S(2)}, u32[]{:S(2)}) collective-permute-start(bf16[384,512]{1,0:T(8,128)(2,1)} %bitcast.15), channel_id=1, source_target_pairs={{1,2},{2,1},{3,4},{4,3},{5,6},{6,5},{7,8},{8,7},{9,10},{10,9},{11,... | collective-permute-start | bytes 1179656 | tf_op jit(solution)/shard_map/ppermute | solution.py:406
  1.1 1.0 %copy-start = (bf16[1,2,192,512]{3,2,1,0:T(8,128)(2,1)S(1)}, bf16[1,2,192,512]{3,2,1,0:T(8,128)(2,1)}, u32[]{:S(2)}) copy-start(bf16[1,2,192,512]{3,2,1,0:T(8,128)(2,1)} %param.12) | copy-start | bytes 1179652
  2.1 25.9 %copy-start.4 = (bf16[128,1024]{1,0:T(8,128)(2,1)S(1)}, bf16[128,1024]{1,0:T(8,128)(2,1)}, u32[]{:S(2)}) copy-start(bf16[128,1024]{1,0:T(8,128)(2,1)} %affine_weight.1) | copy-start | bytes 786436
  3.2 15.1 %all-to-all-start = ((f32[16,1,128]{2,1,0:T(1,128)}), f32[16,1,128]{2,1,0:T(1,128)S(1)}, u32[]{:S(2)}, u32[]{:S(2)}) async-start(f32[16,1,128]{2,1,0:T(1,128)} %bitcast.2), calls=%async_computation | async-start | bytes 16384 | tf_op jit(solution)/shard_map/all_to_all | solution.py:100
  23.5 10.2 %copy-start.1 = (bf16[1,2,192,512]{3,2,1,0:T(8,128)(2,1)S(1)}, bf16[1,2,192,512]{3,2,1,0:T(8,128)(2,1)}, u32[]{:S(2)}) copy-start(bf16[1,2,192,512]{3,2,1,0:T(8,128)(2,1)} %param.12) | copy-start | bytes 1179652
  23.5 9.9 %all-to-all-start.1 = ((f32[16,1,128]{2,1,0:T(1,128)}), f32[16,1,128]{2,1,0:T(1,128)S(1)}, u32[]{:S(2)}, u32[]{:S(2)}) async-start(f32[16,1,128]{2,1,0:T(1,128)} %bitcast.7), calls=%async_computation.1 | async-start | bytes 16384 | tf_op jit(solution)/shard_map/all_to_all | solution.py:100
  32.2 25.0 %copy-start.3 = (bf16[512,512]{1,0:T(8,128)(2,1)S(1)}, bf16[512,512]{1,0:T(8,128)(2,1)}, u32[]{:S(2)}) copy-start(bf16[512,512]{1,0:T(8,128)(2,1)} %refs_19_.1) | copy-start | bytes 1572868
  33.4 23.7 %copy-start.2 = (bf16[512,1536]{1,0:T(8,128)(2,1)S(1)}, bf16[512,1536]{1,0:T(8,128)(2,1)}, u32[]{:S(2)}) copy-start(bf16[512,1536]{1,0:T(8,128)(2,1)} %refs_18_.1) | copy-start | bytes 4718596
  38.0 6.0 %collective-permute-start.2 = (bf16[96,512]{1,0:T(8,128)(2,1)S(1)}, bf16[96,512]{1,0:T(8,128)(2,1)S(1)}, u32[]{:S(2)}, u32[]{:S(2)}) collective-permute-start(bf16[96,512]{1,0:T(8,128)(2,1)S(1)} %get-tuple-element.15.refs_0_), channel_id=1, source_target_pairs={{0,4},{1,5},{2,6},{3,7},{4,0},{5,1},{6,2},{7,3},{8,12},{9,13},{10,... | collective-permute-start | bytes 294920 | tf_op jit(solution)/shard_map/ppermute | solution.py:310
  38.6 10.7 %collective-permute-start.3 = (bf16[96,512]{1,0:T(8,128)(2,1)S(1)}, bf16[96,512]{1,0:T(8,128)(2,1)S(1)}, u32[]{:S(2)}, u32[]{:S(2)}) collective-permute-start(bf16[96,512]{1,0:T(8,128)(2,1)S(1)} %get-tuple-element.15.refs_0_), channel_id=1, source_target_pairs={{0,8},{1,9},{2,10},{3,11},{4,12},{5,13},{6,14},{7,15},{8,0},{9,1},... | collective-permute-start | bytes 294920 | tf_op jit(solution)/shard_map/ppermute | solution.py:310
  41.0 9.8 %collective-permute-start.4 = (bf16[96,512]{1,0:T(8,128)(2,1)S(1)}, bf16[96,512]{1,0:T(8,128)(2,1)S(1)}, u32[]{:S(2)}, u32[]{:S(2)}) collective-permute-start(bf16[96,512]{1,0:T(8,128)(2,1)S(1)} %get-tuple-element.15.refs_0_), channel_id=1, source_target_pairs={{0,12},{1,13},{2,14},{3,15},{4,8},{5,9},{6,10},{7,11},{8,4},{9,5},... | collective-permute-start | bytes 294920 | tf_op jit(solution)/shard_map/ppermute | solution.py:310
  42.5 8.9 %collective-permute-start.5 = (bf16[96,512]{1,0:T(8,128)(2,1)S(1)}, bf16[96,512]{1,0:T(8,128)(2,1)S(1)}, u32[]{:S(2)}, u32[]{:S(2)}) collective-permute-start(bf16[96,512]{1,0:T(8,128)(2,1)S(1)} %get-tuple-element.15.refs_0_), channel_id=1, source_target_pairs={{0,2},{1,3},{2,0},{3,1},{4,6},{5,7},{6,4},{7,5},{8,10},{9,11},{10,... | collective-permute-start | bytes 294920 | tf_op jit(solution)/shard_map/ppermute | solution.py:310
  43.0 8.3 %collective-permute-start.9 = (bf16[96,512]{1,0:T(8,128)(2,1)S(1)}, bf16[96,512]{1,0:T(8,128)(2,1)S(1)}, u32[]{:S(2)}, u32[]{:S(2)}) collective-permute-start(bf16[96,512]{1,0:T(8,128)(2,1)S(1)} %get-tuple-element.15.refs_0_), channel_id=1, source_target_pairs={{0,1},{1,0},{2,3},{3,2},{4,5},{5,4},{6,7},{7,6},{8,9},{9,8},{10,11... | collective-permute-start | bytes 294920 | tf_op jit(solution)/shard_map/ppermute | solution.py:310
  44.0 7.9 %collective-permute-start.6 = (bf16[96,512]{1,0:T(8,128)(2,1)S(1)}, bf16[96,512]{1,0:T(8,128)(2,1)S(1)}, u32[]{:S(2)}, u32[]{:S(2)}) collective-permute-start(bf16[96,512]{1,0:T(8,128)(2,1)S(1)} %collective-permute-done.2.refs_1_), channel_id=1, source_target_pairs={{0,2},{1,3},{2,0},{3,1},{4,6},{5,7},{6,4},{7,5},{8,10},{9,11},{10,... | collective-permute-start | bytes 294920 | tf_op jit(solution)/shard_map/ppermute | solution.py:310
  49.3 4.6 %collective-permute-start.7 = (bf16[96,512]{1,0:T(8,128)(2,1)S(1)}, bf16[96,512]{1,0:T(8,128)(2,1)S(1)}, u32[]{:S(2)}, u32[]{:S(2)}) collective-permute-start(bf16[96,512]{1,0:T(8,128)(2,1)S(1)} %collective-permute-done.3.refs_2_), channel_id=1, source_target_pairs={{0,2},{1,3},{2,0},{3,1},{4,6},{5,7},{6,4},{7,5},{8,10},{9,11},{10,... | collective-permute-start | bytes 294920 | tf_op jit(solution)/shard_map/ppermute | solution.py:310
  50.8 4.6 %collective-permute-start.8 = (bf16[96,512]{1,0:T(8,128)(2,1)S(1)}, bf16[96,512]{1,0:T(8,128)(2,1)S(1)}, u32[]{:S(2)}, u32[]{:S(2)}) collective-permute-start(bf16[96,512]{1,0:T(8,128)(2,1)S(1)} %collective-permute-done.4.refs_3_), channel_id=1, source_target_pairs={{0,2},{1,3},{2,0},{3,1},{4,6},{5,7},{6,4},{7,5},{8,10},{9,11},{10,... | collective-permute-start | bytes 294920 | tf_op jit(solution)/shard_map/ppermute | solution.py:310
  51.4 4.0 %collective-permute-start.10 = (bf16[96,512]{1,0:T(8,128)(2,1)S(1)}, bf16[96,512]{1,0:T(8,128)(2,1)S(1)}, u32[]{:S(2)}, u32[]{:S(2)}) collective-permute-start(bf16[96,512]{1,0:T(8,128)(2,1)S(1)} %collective-permute-done.2.refs_1_), channel_id=1, source_target_pairs={{0,1},{1,0},{2,3},{3,2},{4,5},{5,4},{6,7},{7,6},{8,9},{9,8},{10,11... | collective-permute-start | bytes 294920 | tf_op jit(solution)/shard_map/ppermute | solution.py:310
  51.4 4.5 %collective-permute-start.11 = (bf16[96,512]{1,0:T(8,128)(2,1)S(1)}, bf16[96,512]{1,0:T(8,128)(2,1)S(1)}, u32[]{:S(2)}, u32[]{:S(2)}) collective-permute-start(bf16[96,512]{1,0:T(8,128)(2,1)S(1)} %collective-permute-done.3.refs_2_), channel_id=1, source_target_pairs={{0,1},{1,0},{2,3},{3,2},{4,5},{5,4},{6,7},{7,6},{8,9},{9,8},{10,11... | collective-permute-start | bytes 294920 | tf_op jit(solution)/shard_map/ppermute | solution.py:310
  51.9 4.1 %collective-permute-start.12 = (bf16[96,512]{1,0:T(8,128)(2,1)S(1)}, bf16[96,512]{1,0:T(8,128)(2,1)S(1)}, u32[]{:S(2)}, u32[]{:S(2)}) collective-permute-start(bf16[96,512]{1,0:T(8,128)(2,1)S(1)} %collective-permute-done.4.refs_3_), channel_id=1, source_target_pairs={{0,1},{1,0},{2,3},{3,2},{4,5},{5,4},{6,7},{7,6},{8,9},{9,8},{10,11... | collective-permute-start | bytes 294920 | tf_op jit(solution)/shard_map/ppermute | solution.py:310
  54.0 2.0 %collective-permute-start.13 = (bf16[96,512]{1,0:T(8,128)(2,1)S(1)}, bf16[96,512]{1,0:T(8,128)(2,1)S(1)}, u32[]{:S(2)}, u32[]{:S(2)}) collective-permute-start(bf16[96,512]{1,0:T(8,128)(2,1)S(1)} %collective-permute-done.5.refs_4_), channel_id=1, source_target_pairs={{0,1},{1,0},{2,3},{3,2},{4,5},{5,4},{6,7},{7,6},{8,9},{9,8},{10,11... | collective-permute-start | bytes 294920 | tf_op jit(solution)/shard_map/ppermute | solution.py:310
  55.4 1.3 %collective-permute-start.14 = (bf16[96,512]{1,0:T(8,128)(2,1)S(1)}, bf16[96,512]{1,0:T(8,128)(2,1)S(1)}, u32[]{:S(2)}, u32[]{:S(2)}) collective-permute-start(bf16[96,512]{1,0:T(8,128)(2,1)S(1)} %collective-permute-done.6.refs_5_), channel_id=1, source_target_pairs={{0,1},{1,0},{2,3},{3,2},{4,5},{5,4},{6,7},{7,6},{8,9},{9,8},{10,11... | collective-permute-start | bytes 294920 | tf_op jit(solution)/shard_map/ppermute | solution.py:310
  55.4 1.5 %collective-permute-start.15 = (bf16[96,512]{1,0:T(8,128)(2,1)S(1)}, bf16[96,512]{1,0:T(8,128)(2,1)S(1)}, u32[]{:S(2)}, u32[]{:S(2)}) collective-permute-start(bf16[96,512]{1,0:T(8,128)(2,1)S(1)} %collective-permute-done.7.refs_6_), channel_id=1, source_target_pairs={{0,1},{1,0},{2,3},{3,2},{4,5},{5,4},{6,7},{7,6},{8,9},{9,8},{10,11... | collective-permute-start | bytes 294920 | tf_op jit(solution)/shard_map/ppermute | solution.py:310
  55.9 1.3 %collective-permute-start.16 = (bf16[96,512]{1,0:T(8,128)(2,1)S(1)}, bf16[96,512]{1,0:T(8,128)(2,1)S(1)}, u32[]{:S(2)}, u32[]{:S(2)}) collective-permute-start(bf16[96,512]{1,0:T(8,128)(2,1)S(1)} %collective-permute-done.8.refs_7_), channel_id=1, source_target_pairs={{0,1},{1,0},{2,3},{3,2},{4,5},{5,4},{6,7},{7,6},{8,9},{9,8},{10,11... | collective-permute-start | bytes 294920 | tf_op jit(solution)/shard_map/ppermute | solution.py:310

commit v8 on v7

--- a/solution.py
+++ b/solution.py
@@ -15,7 +15,6 @@
 LANES = 128
 GAIN, BIAS, CONV_BIAS, PROJ_BIAS = 0, 3, 6, 8
 VMEM_BYTES = 52 * 1024 * 1024
-SHADOW_BYTES = 256 * 1024 * 1024
 OUTER_BYTES = 52 * 1024 * 1024
 SECOND_BYTES = 51 * 1024 * 1024
 FAR = pl.BlockSpec(memory_space=pltpu.HBM)
@@ -80,7 +79,7 @@
     tiles = channels // LANES
     center = jnp.concatenate([totals[2 * tile : 2 * tile + 1] for tile in range(tiles)], axis=1)
     second = jnp.concatenate([totals[2 * tile + 1 : 2 * tile + 2] for tile in range(tiles)], axis=1)
-    return center, second - center * center
+    return center, jnp.maximum(second - center * center, 0.0)
 
 
 def column_sums(values):
@@ -139,9 +138,9 @@
     spread[:, 2 * channels :] = after.astype(jnp.bfloat16)
 
 
-def affine_kernel(which, entries, sums, table, *refs):
-    film, out = (None, *refs)[-2:]
+def affine_rows(which, cells, sums, table, film=None):
     channels = table.shape[1]
+    entries = sums.shape[0] * cells * (channels // GROUPS)
     center, variance = unpacked_moments(sums[...], entries, channels)
     factor = lax.rsqrt(variance + eps) * table[GAIN + which : GAIN + which + 1]
     offset = table[BIAS + which : BIAS + which + 1]
@@ -149,20 +148,20 @@
         scale = 1.0 + film[:, :channels]
         factor = factor * scale
         offset = offset * scale + film[:, channels:]
-    out[0:1, :] = center
-    out[1:2, :] = factor
-    out[2:3, :] = offset
-
-
-def affine(which, cells, sums, table, *film):
-    channels = table.shape[1]
-    entries = sums.shape[0] * cells * (channels // GROUPS)
-    return pl.pallas_call(
-        functools.partial(affine_kernel, which, entries),
-        out_shape=jax.ShapeDtypeStruct((3, channels), jnp.float32),
-        cost_estimate=pl.CostEstimate(flops=0, bytes_accessed=SHADOW_BYTES, transcendentals=0),
+    return center, factor, offset
+
+
+def affine_kernel(which, cells, sums, table, film, out):
+    for row, values in enumerate(affine_rows(which, cells, sums, table, film)):
+        out[row : row + 1, :] = values
+
+
+def affine(which, cells, sums, table, film):
+    return pl.pallas_call(
+        functools.partial(affine_kernel, which, cells),
+        out_shape=jax.ShapeDtypeStruct((3, table.shape[1]), jnp.float32),
         compiler_params=pltpu.CompilerParams(vmem_limit_bytes=VMEM_BYTES),
-    )(sums, table, *film)
+    )(sums, table, film)
 
 
 def tap_copies(source, target, sems):
@@ -178,7 +177,7 @@
     return total
 
 
-def first_kernel(height, breadth, outer, own, norm, table, taps, mate, other, *refs):
+def first_kernel(height, breadth, outer, own, sums, table, taps, mate, other, *refs):
     refs = list(refs)
     if outer:
         refs.pop(0)
@@ -191,7 +190,7 @@
     channels = own.shape[1]
     copies = tap_copies(taps, weight, sems)
     copies[0].start()
-    center, factor, offset = norm[0:1, :], norm[1:2, :], norm[2:3, :]
+    center, factor, offset = affine_rows(0, height * breadth, sums, table)
     if outer:
         needed = [-2, -1, 0, height - 1, height, height + 1]
     else:
@@ -226,7 +225,7 @@
         packed[...] = jnp.broadcast_to(packed_moments(total, squares), packed.shape)
 
 
-def first_convolution(height, breadth, own, norm, table, weight, mate, other, after=()):
+def first_convolution(height, breadth, own, sums, table, weight, mate, other, after=()):
     channels = own.shape[1]
     count = lax.axis_size("lat")
     outer = len(after) > 0
@@ -242,7 +241,7 @@
             pltpu.SemaphoreType.DMA((3,)),
         ],
         compiler_params=pltpu.CompilerParams(vmem_limit_bytes=OUTER_BYTES if outer else VMEM_BYTES),
-    )(own, norm, table, weight.reshape(3, 3 * channels, channels), mate, other, *after)
+    )(own, sums, table, weight.reshape(3, 3 * channels, channels), mate, other, *after)
 
 
 def second_kernel(
@@ -329,7 +328,8 @@
     entries = count * tokens * (channels // GROUPS)
     moments = group_total(jnp.where(row == 0, sums, squares)) / entries
     center = moments[0:1]
-    factor = lax.rsqrt(moments[1:2] - center * center + eps) * table[GAIN + 2 : GAIN + 3]
+    variance = jnp.maximum(moments[1:2] - center * center, 0.0)
+    factor = lax.rsqrt(variance + eps) * table[GAIN + 2 : GAIN + 3]
     offset = table[BIAS + 2 : BIAS + 3]
 
     def norm(values):
@@ -359,10 +359,11 @@
         scores = later
         if start + 2 * HEAD_DIM < channels:
             later = scored(start + 2 * HEAD_DIM)
-        weights = jnp.exp(scores - jnp.max(scores, axis=1, keepdims=True))
-        totals = jnp.sum(weights, axis=1, keepdims=True)
+        weights = jnp.exp(scores - jnp.max(scores, axis=1, keepdims=True)).astype(jnp.bfloat16)
         values = projected[:, channels + start : channels + start + 2 * HEAD_DIM]
-        blended = jnp.dot(weights.astype(jnp.bfloat16), values, preferred_element_type=jnp.float32) / totals
+        values = jnp.concatenate([values, jnp.ones_like(values)], axis=1)
+        blended = jnp.dot(weights, values, preferred_element_type=jnp.float32)
+        blended = blended[:, : 2 * HEAD_DIM] / blended[:, 2 * HEAD_DIM :]
         attended.append(jnp.where(first, blended[:tokens], blended[tokens:]).astype(jnp.bfloat16))
     result = jnp.dot(jnp.concatenate(attended, axis=1), proj_weight[...], preferred_element_type=jnp.float32)
     result = pooled[...] + result + table[PROJ_BIAS : PROJ_BIAS + 1]
@@ -404,8 +405,8 @@
     packed, own = moments(cells)
     mate = lax.ppermute(cells, "lat", [(i, i ^ 1) for i in range(count)])
     other = lax.ppermute(cells, "lat", [(i, (i - 1 ^ 1) + 1) for i in range(1, count - 1)])
-    norm = affine(0, height * breadth, shared(packed), table)
-    known = (own, norm, table, conv1_weight, mate, other)
+    sums = shared(packed)
+    known = (own, sums, table, conv1_weight, mate, other)
     first, packed = first_convolution(height, breadth, *known)
     outer = first_convolution(height, breadth, *known, [packed])
     film = film_terms(noise_index, sigma_table, affine_weight, packed)

time: 62.8 us -> 62.4 us (level)
  no operation moved by 1% of the time
where the time goes in v8:
time: 62.4 us; the launch traced here: 62 us
  starting transfers between devices  22.4 us (36%)
  Pallas kernels  19.9 us (32%)
  waiting for transfers between devices  17.2 us (28%)
  local copies, waits for them, and re-layouts  1.01 us (2%)
  between operations  0.78 us (1%)
  other arithmetic  0.76 us (1%)
    all_to_all x2, starting transfers between devices, shared(): lax.all_to_all(rows.reshape(count, 1, lanes), 'lat', 0, 0)  12.6 us
    ppermute x15, waiting for transfers between devices, exchange(): return lax.ppermute(block, 'lat', [(i, i ^ stride) for i in range(count)])  10.5 us
    pallas_call x2, Pallas kernels, first_convolution(): pl.pallas_call(functools.partial(first_kernel, height, breadth, outer), i...  9.03 us
    ppermute x15, starting transfers between devices, exchange(): return lax.ppermute(block, 'lat', [(i, i ^ stride) for i in range(count)])  8.7 us
    all_to_all x2, waiting for transfers between devices, shared(): lax.all_to_all(rows.reshape(count, 1, lanes), 'lat', 0, 0)  6.69 us
    pallas_call x1, Pallas kernels, attention(): pl.pallas_call(functools.partial(attention_kernel, count), out_shape=jax....  4.97 us
    pallas_call x1, Pallas kernels, second_convolution(): pl.pallas_call(functools.partial(second_kernel, height, breadth), in_spec...  4.27 us
  transfers between devices with their start and end apart: 19, of which 9 were waited for; matrix products, arithmetic and copies ran while one was open for 1% of the time, Pallas kernels for 9%

profile of v8, /device:TPU:0, one launch (start us, length us, event | category | flops | bytes accessed | tf_op | source)
XLA Modules:
  0.0 62.0 jit_solution(16229344452621103659)
XLA Ops:
  0.0 0.0 copy-start.5
  0.0 0.5 collective-permute-start
  0.5 0.7 %collective-permute-start.1 = (bf16[384,512]{1,0:T(8,128)(2,1)}, bf16[384,512]{1,0:T(8,128)(2,1)S(1)}, u32[]{:S(2)}, u32[]{:S(2)}) collective-permute-start(bf16[384,512]{1,0:T(8,128)(2,1)} %bitcast.15), channel_id=1, source_target_pairs={{1,2},{2,1},{3,4},{4,3},{5,6},{6,5},{7,8},{8,7},{9,10},{10,9},{11,... | collective-permute-start | bytes 1179656 | tf_op jit(solution)/shard_map/ppermute | solution.py:407
  1.1 0.0 copy-start
  1.1 1.0 %copy-done = bf16[1,2,192,512]{3,2,1,0:T(8,128)(2,1)S(1)} copy-done((bf16[1,2,192,512]{3,2,1,0:T(8,128)(2,1)S(1)}, bf16[1,2,192,512]{3,2,1,0:T(8,128)(2,1)}, u32[]{:S(2)}) %copy-start) | copy-done | bytes 393240
  2.1 0.0 copy-start.4
  2.1 1.0 %shard_map.118 = (f32[16,128]{1,0:T(8,128)}, bf16[384,512]{1,0:T(8,128)(2,1)S(1)}) custom-call(bf16[384,512]{1,0:T(8,128)(2,1)S(1)} %bitcast.16), custom_call_target="tpu_custom_call" | custom-call | tf_op jit(solution)/shard_map/pallas_call | solution.py:121
  3.2 8.8 %all-to-all-start = ((f32[16,1,128]{2,1,0:T(1,128)}), f32[16,1,128]{2,1,0:T(1,128)S(1)}, u32[]{:S(2)}, u32[]{:S(2)}) async-start(f32[16,1,128]{2,1,0:T(1,128)} %bitcast.2), calls=%async_computation | async-start | bytes 16384 | tf_op jit(solution)/shard_map/all_to_all | solution.py:99
  12.0 0.8 %pad_maximum_fusion.table.refs_17_ = f32[9,512]{1,0:T(8,128)S(1)} fusion(f32[1,512]{1,0:T(1,128)} %bitcast.25, f32[2,512]{1,0:T(2,128)} %param.20, f32[3,512]{1,0:T(4,128)} %param.17, f32[3,512]{1,0:T(4,128)} %param.16), kind=kLoop, calls=%fused_computation | loop fusion | flops 13824 | bytes 36864 | tf_op jit(solution)/shard_map/concatenate | solution.py:403
  12.7 5.6 %all-to-all-done = f32[16,1,128]{2,1,0:T(1,128)S(1)} async-done(((f32[16,1,128]{2,1,0:T(1,128)}), f32[16,1,128]{2,1,0:T(1,128)S(1)}, u32[]{:S(2)}, u32[]{:S(2)}) %all-to-all-start) | async-done | bytes 8224 | tf_op jit(solution)/shard_map/all_to_all | solution.py:99
  18.3 0.0 collective-permute-done.mate
  18.3 0.0 collective-permute-done.1.other
  18.3 5.0 %shard_map.119 = (f32[384,512]{1,0:T(8,128)S(1)}, f32[16,128]{1,0:T(8,128)}) custom-call(bf16[384,512]{1,0:T(8,128)(2,1)S(1)} %get-tuple-element.11.own, f32[16,128]{1,0:T(8,128)S(1)} %bitcast.18, f32[9,512]{1,0:T(8,128)S(1)} %pad_maximum_fusion.table.refs_17_, bf16[3,1536,512]{2,1,0:T(8,128)(2,1)} %bitcast.22, ...), custom_call_target="tpu_custom_call" | custom-call | tf_op jit(solution)/shard_map/pallas_call | solution.py:234
  23.3 0.0 copy-start.1
  23.3 3.8 %all-to-all-start.1 = ((f32[16,1,128]{2,1,0:T(1,128)}), f32[16,1,128]{2,1,0:T(1,128)S(1)}, u32[]{:S(2)}, u32[]{:S(2)}) async-start(f32[16,1,128]{2,1,0:T(1,128)} %bitcast.7), calls=%async_computation.1 | async-start | bytes 16384 | tf_op jit(solution)/shard_map/all_to_all | solution.py:99
  27.8 0.0 copy-done.5
  27.8 0.0 copy-done.4
  27.8 0.3 shard_map.121.film
  28.0 4.0 %shard_map.120.outer = f32[384,512]{1,0:T(8,128)S(1)} custom-call(bf16[384,512]{1,0:T(8,128)(2,1)S(1)} %get-tuple-element.11.own, f32[16,128]{1,0:T(8,128)S(1)} %bitcast.19, f32[9,512]{1,0:T(8,128)S(1)} %pad_maximum_fusion.table.refs_17_, bf16[3,1536,512]{2,1,0:T(8,128)(2,1)} %bitcast.23, bf16[384,512]{1,0:T(8,128)(2,1)S(1)} %collective-permute-done.mate, ...), custom_call_target="tpu_custom_call" | custom-call | tf_op jit(solution)/shard_map/pallas_call | solution.py:234
  32.1 0.0 copy-start.3
  32.1 1.1 %all-to-all-done.1 = f32[16,1,128]{2,1,0:T(1,128)S(1)} async-done(((f32[16,1,128]{2,1,0:T(1,128)}), f32[16,1,128]{2,1,0:T(1,128)S(1)}, u32[]{:S(2)}, u32[]{:S(2)}) %all-to-all-start.1) | async-done | bytes 8224 | tf_op jit(solution)/shard_map/all_to_all | solution.py:99
  33.2 0.0 copy-start.2
  33.2 0.3 shard_map.122.norm
  33.5 0.0 copy-done.1
  33.5 4.3 %shard_map.123 = (f32[96,512]{1,0:T(8,128)S(1)}, bf16[96,512]{1,0:T(8,128)(2,1)S(1)}) custom-call(f32[384,512]{1,0:T(8,128)S(1)} %get-tuple-element.13.first, f32[384,512]{1,0:T(8,128)S(1)} %shard_map.120.outer, bf16[384,512]{1,0:T(8,128)(2,1)S(1)} %bitcast.17, f32[3,512]{1,0:T(4,128)S(1)} %shard_map.122.norm, f32[9,512]{1,0:T(8,128)S(1)} %pad_maximum_fusion.table.refs_17_, ...), custom_call_target="tpu_custom_call" | custom-call | tf_op jit(solution)/shard_map/pallas_call | solution.py:290
  37.8 0.6 %collective-permute-start.2 = (bf16[96,512]{1,0:T(8,128)(2,1)S(1)}, bf16[96,512]{1,0:T(8,128)(2,1)S(1)}, u32[]{:S(2)}, u32[]{:S(2)}) collective-permute-start(bf16[96,512]{1,0:T(8,128)(2,1)S(1)} %get-tuple-element.15.refs_0_), channel_id=1, source_target_pairs={{0,4},{1,5},{2,6},{3,7},{4,0},{5,1},{6,2},{7,3},{8,12},{9,13},{10,... | collective-permute-start | bytes 294920 | tf_op jit(solution)/shard_map/ppermute | solution.py:309
  38.4 2.4 %collective-permute-start.3 = (bf16[96,512]{1,0:T(8,128)(2,1)S(1)}, bf16[96,512]{1,0:T(8,128)(2,1)S(1)}, u32[]{:S(2)}, u32[]{:S(2)}) collective-permute-start(bf16[96,512]{1,0:T(8,128)(2,1)S(1)} %get-tuple-element.15.refs_0_), channel_id=1, source_target_pairs={{0,8},{1,9},{2,10},{3,11},{4,12},{5,13},{6,14},{7,15},{8,0},{9,1},... | collective-permute-start | bytes 294920 | tf_op jit(solution)/shard_map/ppermute | solution.py:309
  40.8 1.4 %collective-permute-start.4 = (bf16[96,512]{1,0:T(8,128)(2,1)S(1)}, bf16[96,512]{1,0:T(8,128)(2,1)S(1)}, u32[]{:S(2)}, u32[]{:S(2)}) collective-permute-start(bf16[96,512]{1,0:T(8,128)(2,1)S(1)} %get-tuple-element.15.refs_0_), channel_id=1, source_target_pairs={{0,12},{1,13},{2,14},{3,15},{4,8},{5,9},{6,10},{7,11},{8,4},{9,5},... | collective-permute-start | bytes 294920 | tf_op jit(solution)/shard_map/ppermute | solution.py:309
  42.3 0.5 collective-permute-start.5
  42.8 0.0 collective-permute-start.9
  42.8 1.0 %collective-permute-done.2.refs_1_ = bf16[96,512]{1,0:T(8,128)(2,1)S(1)} collective-permute-done((bf16[96,512]{1,0:T(8,128)(2,1)S(1)}, bf16[96,512]{1,0:T(8,128)(2,1)S(1)}, u32[]{:S(2)}, u32[]{:S(2)}) %collective-permute-start.2) | collective-permute-done | bytes 98336 | tf_op jit(solution)/shard_map/ppermute | solution.py:309
  43.8 0.5 collective-permute-start.6
  44.3 4.9 %collective-permute-done.3.refs_2_ = bf16[96,512]{1,0:T(8,128)(2,1)S(1)} collective-permute-done((bf16[96,512]{1,0:T(8,128)(2,1)S(1)}, bf16[96,512]{1,0:T(8,128)(2,1)S(1)}, u32[]{:S(2)}, u32[]{:S(2)}) %collective-permute-start.3) | collective-permute-done | bytes 98336 | tf_op jit(solution)/shard_map/ppermute | solution.py:309
  49.2 1.5 %collective-permute-start.7 = (bf16[96,512]{1,0:T(8,128)(2,1)S(1)}, bf16[96,512]{1,0:T(8,128)(2,1)S(1)}, u32[]{:S(2)}, u32[]{:S(2)}) collective-permute-start(bf16[96,512]{1,0:T(8,128)(2,1)S(1)} %collective-permute-done.3.refs_2_), channel_id=1, source_target_pairs={{0,2},{1,3},{2,0},{3,1},{4,6},{5,7},{6,4},{7,5},{8,10},{9,11},{10,... | collective-permute-start | bytes 294920 | tf_op jit(solution)/shard_map/ppermute | solution.py:309
  50.6 0.0 collective-permute-done.4.refs_3_
  50.6 0.6 collective-permute-start.8
  51.2 0.0 collective-permute-done.5.refs_4_
  51.2 0.0 collective-permute-start.10
  51.2 0.0 collective-permute-done.9.refs_8_
  51.2 0.5 collective-permute-start.11
  51.7 0.0 collective-permute-done.6.refs_5_
  51.7 0.1 collective-permute-start.12
  51.8 2.0 %collective-permute-done.7.refs_6_ = bf16[96,512]{1,0:T(8,128)(2,1)S(1)} collective-permute-done((bf16[96,512]{1,0:T(8,128)(2,1)S(1)}, bf16[96,512]{1,0:T(8,128)(2,1)S(1)}, u32[]{:S(2)}, u32[]{:S(2)}) %collective-permute-start.7) | collective-permute-done | bytes 98336 | tf_op jit(solution)/shard_map/ppermute | solution.py:309
  53.8 0.0 collective-permute-start.13
  53.8 1.5 %collective-permute-done.8.refs_7_ = bf16[96,512]{1,0:T(8,128)(2,1)S(1)} collective-permute-done((bf16[96,512]{1,0:T(8,128)(2,1)S(1)}, bf16[96,512]{1,0:T(8,128)(2,1)S(1)}, u32[]{:S(2)}, u32[]{:S(2)}) %collective-permute-start.8) | collective-permute-done | bytes 98336 | tf_op jit(solution)/shard_map/ppermute | solution.py:309
  55.2 0.0 collective-permute-start.14
  55.2 0.0 collective-permute-done.10.refs_9_
  55.3 0.5 collective-permute-start.15
  55.8 0.0 collective-permute-done.11.refs_10_
  55.8 0.1 collective-permute-start.16
  55.8 0.0 collective-permute-done.12.refs_11_
  55.8 0.0 collective-permute-done.13.refs_12_
  55.8 0.7 %collective-permute-done.14.refs_13_ = bf16[96,512]{1,0:T(8,128)(2,1)S(1)} collective-permute-done((bf16[96,512]{1,0:T(8,128)(2,1)S(1)}, bf16[96,512]{1,0:T(8,128)(2,1)S(1)}, u32[]{:S(2)}, u32[]{:S(2)}) %collective-permute-start.14) | collective-permute-done | bytes 98336 | tf_op jit(solution)/shard_map/ppermute | solution.py:309
  56.5 0.2 collective-permute-done.15.refs_14_
  56.7 0.4 collective-permute-done.16.refs_15_
  57.1 0.0 copy-done.3
  57.1 0.0 copy-done.2
  57.1 5.0 %shard_map.124 = bf16[96,512]{1,0:T(8,128)(2,1)} custom-call(bf16[96,512]{1,0:T(8,128)(2,1)S(1)} %get-tuple-element.15.refs_0_, bf16[96,512]{1,0:T(8,128)(2,1)S(1)} %collective-permute-done.2.refs_1_, bf16[96,512]{1,0:T(8,128)(2,1)S(1)} %collective-permute-done.3.refs_2_, bf16[96,512]{1,0:T(8,128)(2,1)S(1)} %collective-permute-done.4.refs_3_, ...), custom_call_target="tpu_custom_call" | custom-call | tf_op jit(solution)/shard_map/pallas_call | solution.py:376
Async XLA Ops:
  0.0 27.8 %copy-start.5 = (f32[18]{0:T(128)S(1)}, f32[18]{0:T(128)}, u32[]{:S(2)}) copy-start(f32[18]{0:T(128)} %param.14) | copy-start | bytes 220
  0.0 18.3 %collective-permute-start = (bf16[384,512]{1,0:T(8,128)(2,1)}, bf16[384,512]{1,0:T(8,128)(2,1)S(1)}, u32[]{:S(2)}, u32[]{:S(2)}) collective-permute-start(bf16[384,512]{1,0:T(8,128)(2,1)} %bitcast.14), channel_id=1, source_target_pairs={{0,1},{1,0},{2,3},{3,2},{4,5},{5,4},{6,7},{7,6},{8,9},{9,8},{10,11... | collective-permute-start | bytes 1179656 | tf_op jit(solution)/shard_map/ppermute | solution.py:406
  0.5 17.8 %collective-permute-start.1 = (bf16[384,512]{1,0:T(8,128)(2,1)}, bf16[384,512]{1,0:T(8,128)(2,1)S(1)}, u32[]{:S(2)}, u32[]{:S(2)}) collective-permute-start(bf16[384,512]{1,0:T(8,128)(2,1)} %bitcast.15), channel_id=1, source_target_pairs={{1,2},{2,1},{3,4},{4,3},{5,6},{6,5},{7,8},{8,7},{9,10},{10,9},{11,... | collective-permute-start | bytes 1179656 | tf_op jit(solution)/shard_map/ppermute | solution.py:407
  1.1 1.0 %copy-start = (bf16[1,2,192,512]{3,2,1,0:T(8,128)(2,1)S(1)}, bf16[1,2,192,512]{3,2,1,0:T(8,128)(2,1)}, u32[]{:S(2)}) copy-start(bf16[1,2,192,512]{3,2,1,0:T(8,128)(2,1)} %param.12) | copy-start | bytes 1179652
  2.1 25.6 %copy-start.4 = (bf16[128,1024]{1,0:T(8,128)(2,1)S(1)}, bf16[128,1024]{1,0:T(8,128)(2,1)}, u32[]{:S(2)}) copy-start(bf16[128,1024]{1,0:T(8,128)(2,1)} %affine_weight.1) | copy-start | bytes 786436
  3.2 15.1 %all-to-all-start = ((f32[16,1,128]{2,1,0:T(1,128)}), f32[16,1,128]{2,1,0:T(1,128)S(1)}, u32[]{:S(2)}, u32[]{:S(2)}) async-start(f32[16,1,128]{2,1,0:T(1,128)} %bitcast.2), calls=%async_computation | async-start | bytes 16384 | tf_op jit(solution)/shard_map/all_to_all | solution.py:99
  23.3 10.2 %copy-start.1 = (bf16[1,2,192,512]{3,2,1,0:T(8,128)(2,1)S(1)}, bf16[1,2,192,512]{3,2,1,0:T(8,128)(2,1)}, u32[]{:S(2)}) copy-start(bf16[1,2,192,512]{3,2,1,0:T(8,128)(2,1)} %param.12) | copy-start | bytes 1179652
  23.3 9.9 %all-to-all-start.1 = ((f32[16,1,128]{2,1,0:T(1,128)}), f32[16,1,128]{2,1,0:T(1,128)S(1)}, u32[]{:S(2)}, u32[]{:S(2)}) async-start(f32[16,1,128]{2,1,0:T(1,128)} %bitcast.7), calls=%async_computation.1 | async-start | bytes 16384 | tf_op jit(solution)/shard_map/all_to_all | solution.py:99
  32.1 25.0 %copy-start.3 = (bf16[512,512]{1,0:T(8,128)(2,1)S(1)}, bf16[512,512]{1,0:T(8,128)(2,1)}, u32[]{:S(2)}) copy-start(bf16[512,512]{1,0:T(8,128)(2,1)} %refs_19_.1) | copy-start | bytes 1572868
  33.2 23.9 %copy-start.2 = (bf16[512,1536]{1,0:T(8,128)(2,1)S(1)}, bf16[512,1536]{1,0:T(8,128)(2,1)}, u32[]{:S(2)}) copy-start(bf16[512,1536]{1,0:T(8,128)(2,1)} %refs_18_.1) | copy-start | bytes 4718596
  37.8 6.0 %collective-permute-start.2 = (bf16[96,512]{1,0:T(8,128)(2,1)S(1)}, bf16[96,512]{1,0:T(8,128)(2,1)S(1)}, u32[]{:S(2)}, u32[]{:S(2)}) collective-permute-start(bf16[96,512]{1,0:T(8,128)(2,1)S(1)} %get-tuple-element.15.refs_0_), channel_id=1, source_target_pairs={{0,4},{1,5},{2,6},{3,7},{4,0},{5,1},{6,2},{7,3},{8,12},{9,13},{10,... | collective-permute-start | bytes 294920 | tf_op jit(solution)/shard_map/ppermute | solution.py:309
  38.4 10.7 %collective-permute-start.3 = (bf16[96,512]{1,0:T(8,128)(2,1)S(1)}, bf16[96,512]{1,0:T(8,128)(2,1)S(1)}, u32[]{:S(2)}, u32[]{:S(2)}) collective-permute-start(bf16[96,512]{1,0:T(8,128)(2,1)S(1)} %get-tuple-element.15.refs_0_), channel_id=1, source_target_pairs={{0,8},{1,9},{2,10},{3,11},{4,12},{5,13},{6,14},{7,15},{8,0},{9,1},... | collective-permute-start | bytes 294920 | tf_op jit(solution)/shard_map/ppermute | solution.py:309
  40.8 9.8 %collective-permute-start.4 = (bf16[96,512]{1,0:T(8,128)(2,1)S(1)}, bf16[96,512]{1,0:T(8,128)(2,1)S(1)}, u32[]{:S(2)}, u32[]{:S(2)}) collective-permute-start(bf16[96,512]{1,0:T(8,128)(2,1)S(1)} %get-tuple-element.15.refs_0_), channel_id=1, source_target_pairs={{0,12},{1,13},{2,14},{3,15},{4,8},{5,9},{6,10},{7,11},{8,4},{9,5},... | collective-permute-start | bytes 294920 | tf_op jit(solution)/shard_map/ppermute | solution.py:309
  42.3 8.9 %collective-permute-start.5 = (bf16[96,512]{1,0:T(8,128)(2,1)S(1)}, bf16[96,512]{1,0:T(8,128)(2,1)S(1)}, u32[]{:S(2)}, u32[]{:S(2)}) collective-permute-start(bf16[96,512]{1,0:T(8,128)(2,1)S(1)} %get-tuple-element.15.refs_0_), channel_id=1, source_target_pairs={{0,2},{1,3},{2,0},{3,1},{4,6},{5,7},{6,4},{7,5},{8,10},{9,11},{10,... | collective-permute-start | bytes 294920 | tf_op jit(solution)/shard_map/ppermute | solution.py:309
  42.8 8.4 %collective-permute-start.9 = (bf16[96,512]{1,0:T(8,128)(2,1)S(1)}, bf16[96,512]{1,0:T(8,128)(2,1)S(1)}, u32[]{:S(2)}, u32[]{:S(2)}) collective-permute-start(bf16[96,512]{1,0:T(8,128)(2,1)S(1)} %get-tuple-element.15.refs_0_), channel_id=1, source_target_pairs={{0,1},{1,0},{2,3},{3,2},{4,5},{5,4},{6,7},{7,6},{8,9},{9,8},{10,11... | collective-permute-start | bytes 294920 | tf_op jit(solution)/shard_map/ppermute | solution.py:309
  43.8 7.9 %collective-permute-start.6 = (bf16[96,512]{1,0:T(8,128)(2,1)S(1)}, bf16[96,512]{1,0:T(8,128)(2,1)S(1)}, u32[]{:S(2)}, u32[]{:S(2)}) collective-permute-start(bf16[96,512]{1,0:T(8,128)(2,1)S(1)} %collective-permute-done.2.refs_1_), channel_id=1, source_target_pairs={{0,2},{1,3},{2,0},{3,1},{4,6},{5,7},{6,4},{7,5},{8,10},{9,11},{10,... | collective-permute-start | bytes 294920 | tf_op jit(solution)/shard_map/ppermute | solution.py:309
  49.2 4.6 %collective-permute-start.7 = (bf16[96,512]{1,0:T(8,128)(2,1)S(1)}, bf16[96,512]{1,0:T(8,128)(2,1)S(1)}, u32[]{:S(2)}, u32[]{:S(2)}) collective-permute-start(bf16[96,512]{1,0:T(8,128)(2,1)S(1)} %collective-permute-done.3.refs_2_), channel_id=1, source_target_pairs={{0,2},{1,3},{2,0},{3,1},{4,6},{5,7},{6,4},{7,5},{8,10},{9,11},{10,... | collective-permute-start | bytes 294920 | tf_op jit(solution)/shard_map/ppermute | solution.py:309
  50.6 4.6 %collective-permute-start.8 = (bf16[96,512]{1,0:T(8,128)(2,1)S(1)}, bf16[96,512]{1,0:T(8,128)(2,1)S(1)}, u32[]{:S(2)}, u32[]{:S(2)}) collective-permute-start(bf16[96,512]{1,0:T(8,128)(2,1)S(1)} %collective-permute-done.4.refs_3_), channel_id=1, source_target_pairs={{0,2},{1,3},{2,0},{3,1},{4,6},{5,7},{6,4},{7,5},{8,10},{9,11},{10,... | collective-permute-start | bytes 294920 | tf_op jit(solution)/shard_map/ppermute | solution.py:309
  51.2 4.1 %collective-permute-start.10 = (bf16[96,512]{1,0:T(8,128)(2,1)S(1)}, bf16[96,512]{1,0:T(8,128)(2,1)S(1)}, u32[]{:S(2)}, u32[]{:S(2)}) collective-permute-start(bf16[96,512]{1,0:T(8,128)(2,1)S(1)} %collective-permute-done.2.refs_1_), channel_id=1, source_target_pairs={{0,1},{1,0},{2,3},{3,2},{4,5},{5,4},{6,7},{7,6},{8,9},{9,8},{10,11... | collective-permute-start | bytes 294920 | tf_op jit(solution)/shard_map/ppermute | solution.py:309
  51.2 4.6 %collective-permute-start.11 = (bf16[96,512]{1,0:T(8,128)(2,1)S(1)}, bf16[96,512]{1,0:T(8,128)(2,1)S(1)}, u32[]{:S(2)}, u32[]{:S(2)}) collective-permute-start(bf16[96,512]{1,0:T(8,128)(2,1)S(1)} %collective-permute-done.3.refs_2_), channel_id=1, source_target_pairs={{0,1},{1,0},{2,3},{3,2},{4,5},{5,4},{6,7},{7,6},{8,9},{9,8},{10,11... | collective-permute-start | bytes 294920 | tf_op jit(solution)/shard_map/ppermute | solution.py:309
  51.7 4.1 %collective-permute-start.12 = (bf16[96,512]{1,0:T(8,128)(2,1)S(1)}, bf16[96,512]{1,0:T(8,128)(2,1)S(1)}, u32[]{:S(2)}, u32[]{:S(2)}) collective-permute-start(bf16[96,512]{1,0:T(8,128)(2,1)S(1)} %collective-permute-done.4.refs_3_), channel_id=1, source_target_pairs={{0,1},{1,0},{2,3},{3,2},{4,5},{5,4},{6,7},{7,6},{8,9},{9,8},{10,11... | collective-permute-start | bytes 294920 | tf_op jit(solution)/shard_map/ppermute | solution.py:309
  53.8 2.1 %collective-permute-start.13 = (bf16[96,512]{1,0:T(8,128)(2,1)S(1)}, bf16[96,512]{1,0:T(8,128)(2,1)S(1)}, u32[]{:S(2)}, u32[]{:S(2)}) collective-permute-start(bf16[96,512]{1,0:T(8,128)(2,1)S(1)} %collective-permute-done.5.refs_4_), channel_id=1, source_target_pairs={{0,1},{1,0},{2,3},{3,2},{4,5},{5,4},{6,7},{7,6},{8,9},{9,8},{10,11... | collective-permute-start | bytes 294920 | tf_op jit(solution)/shard_map/ppermute | solution.py:309
  55.2 1.3 %collective-permute-start.14 = (bf16[96,512]{1,0:T(8,128)(2,1)S(1)}, bf16[96,512]{1,0:T(8,128)(2,1)S(1)}, u32[]{:S(2)}, u32[]{:S(2)}) collective-permute-start(bf16[96,512]{1,0:T(8,128)(2,1)S(1)} %collective-permute-done.6.refs_5_), channel_id=1, source_target_pairs={{0,1},{1,0},{2,3},{3,2},{4,5},{5,4},{6,7},{7,6},{8,9},{9,8},{10,11... | collective-permute-start | bytes 294920 | tf_op jit(solution)/shard_map/ppermute | solution.py:309
  55.3 1.5 %collective-permute-start.15 = (bf16[96,512]{1,0:T(8,128)(2,1)S(1)}, bf16[96,512]{1,0:T(8,128)(2,1)S(1)}, u32[]{:S(2)}, u32[]{:S(2)}) collective-permute-start(bf16[96,512]{1,0:T(8,128)(2,1)S(1)} %collective-permute-done.7.refs_6_), channel_id=1, source_target_pairs={{0,1},{1,0},{2,3},{3,2},{4,5},{5,4},{6,7},{7,6},{8,9},{9,8},{10,11... | collective-permute-start | bytes 294920 | tf_op jit(solution)/shard_map/ppermute | solution.py:309
  55.8 1.3 %collective-permute-start.16 = (bf16[96,512]{1,0:T(8,128)(2,1)S(1)}, bf16[96,512]{1,0:T(8,128)(2,1)S(1)}, u32[]{:S(2)}, u32[]{:S(2)}) collective-permute-start(bf16[96,512]{1,0:T(8,128)(2,1)S(1)} %collective-permute-done.8.refs_7_), channel_id=1, source_target_pairs={{0,1},{1,0},{2,3},{3,2},{4,5},{5,4},{6,7},{7,6},{8,9},{9,8},{10,11... | collective-permute-start | bytes 294920 | tf_op jit(solution)/shard_map/ppermute | solution.py:309

commit v9 on v8

--- a/solution.py
+++ b/solution.py
@@ -14,8 +14,8 @@
 GROUP_WIDTH = 16
 LANES = 128
 GAIN, BIAS, CONV_BIAS, PROJ_BIAS = 0, 3, 6, 8
-VMEM_BYTES = 52 * 1024 * 1024
-OUTER_BYTES = 52 * 1024 * 1024
+VMEM_BYTES = 51 * 1024 * 1024
+OUTER_BYTES = 51 * 1024 * 1024
 SECOND_BYTES = 51 * 1024 * 1024
 FAR = pl.BlockSpec(memory_space=pltpu.HBM)
 NEAR = pl.BlockSpec(memory_space=pltpu.VMEM)
@@ -210,8 +210,8 @@
         elif row >= height:
             values = jnp.where(place < count - 1, values, 0.0)
         shifted(values, spread.at[i * breadth : (i + 1) * breadth, :])
-        if i in (1, 3):
-            copies[(i + 1) // 2].start()
+        if i in ((2, 4) if outer else (1, 3)):
+            copies[i // 2 if outer else (i + 1) // 2].start()
 
     def patches(tap):
         if outer:

time: 62.4 us -> 62.4 us (level)
  no operation moved by 1% of the time
where the time goes in v9:
time: 62.4 us; the launch traced here: 62 us
  starting transfers between devices  22.4 us (36%)
  Pallas kernels  19.9 us (32%)
  waiting for transfers between devices  17.2 us (28%)
  local copies, waits for them, and re-layouts  1.01 us (2%)
  between operations  0.78 us (1%)
  other arithmetic  0.76 us (1%)
    all_to_all x2, starting transfers between devices, shared(): lax.all_to_all(rows.reshape(count, 1, lanes), 'lat', 0, 0)  12.6 us
    ppermute x15, waiting for transfers between devices, exchange(): return lax.ppermute(block, 'lat', [(i, i ^ stride) for i in range(count)])  10.5 us
    pallas_call x2, Pallas kernels, first_convolution(): pl.pallas_call(functools.partial(first_kernel, height, breadth, outer), i...  9.03 us
    ppermute x15, starting transfers between devices, exchange(): return lax.ppermute(block, 'lat', [(i, i ^ stride) for i in range(count)])  8.7 us
    all_to_all x2, waiting for transfers between devices, shared(): lax.all_to_all(rows.reshape(count, 1, lanes), 'lat', 0, 0)  6.69 us
    pallas_call x1, Pallas kernels, attention(): pl.pallas_call(functools.partial(attention_kernel, count), out_shape=jax....  4.97 us
    pallas_call x1, Pallas kernels, second_convolution(): pl.pallas_call(functools.partial(second_kernel, height, breadth), in_spec...  4.27 us
  transfers between devices with their start and end apart: 19, of which 9 were waited for; matrix products, arithmetic and copies ran while one was open for 1% of the time, Pallas kernels for 9%

profile of v9, /device:TPU:0, one launch (start us, length us, event | category | flops | bytes accessed | tf_op | source)
XLA Modules:
  0.0 62.0 jit_solution(2060392687595964109)
XLA Ops:
  0.0 0.0 copy-start.5
  0.0 0.5 collective-permute-start
  0.5 0.7 %collective-permute-start.1 = (bf16[384,512]{1,0:T(8,128)(2,1)}, bf16[384,512]{1,0:T(8,128)(2,1)S(1)}, u32[]{:S(2)}, u32[]{:S(2)}) collective-permute-start(bf16[384,512]{1,0:T(8,128)(2,1)} %bitcast.15), channel_id=1, source_target_pairs={{1,2},{2,1},{3,4},{4,3},{5,6},{6,5},{7,8},{8,7},{9,10},{10,9},{11,... | collective-permute-start | bytes 1179656 | tf_op jit(solution)/shard_map/ppermute | solution.py:407
  1.1 0.0 copy-start
  1.1 1.0 %copy-done = bf16[1,2,192,512]{3,2,1,0:T(8,128)(2,1)S(1)} copy-done((bf16[1,2,192,512]{3,2,1,0:T(8,128)(2,1)S(1)}, bf16[1,2,192,512]{3,2,1,0:T(8,128)(2,1)}, u32[]{:S(2)}) %copy-start) | copy-done | bytes 393240
  2.1 0.0 copy-start.4
  2.1 1.0 %shard_map.118 = (f32[16,128]{1,0:T(8,128)}, bf16[384,512]{1,0:T(8,128)(2,1)S(1)}) custom-call(bf16[384,512]{1,0:T(8,128)(2,1)S(1)} %bitcast.16), custom_call_target="tpu_custom_call" | custom-call | tf_op jit(solution)/shard_map/pallas_call | solution.py:121
  3.2 8.8 %all-to-all-start = ((f32[16,1,128]{2,1,0:T(1,128)}), f32[16,1,128]{2,1,0:T(1,128)S(1)}, u32[]{:S(2)}, u32[]{:S(2)}) async-start(f32[16,1,128]{2,1,0:T(1,128)} %bitcast.2), calls=%async_computation | async-start | bytes 16384 | tf_op jit(solution)/shard_map/all_to_all | solution.py:99
  12.0 0.8 %pad_maximum_fusion.table.refs_17_ = f32[9,512]{1,0:T(8,128)S(1)} fusion(f32[1,512]{1,0:T(1,128)} %bitcast.25, f32[2,512]{1,0:T(2,128)} %param.20, f32[3,512]{1,0:T(4,128)} %param.17, f32[3,512]{1,0:T(4,128)} %param.16), kind=kLoop, calls=%fused_computation | loop fusion | flops 13824 | bytes 36864 | tf_op jit(solution)/shard_map/concatenate | solution.py:403
  12.7 5.6 %all-to-all-done = f32[16,1,128]{2,1,0:T(1,128)S(1)} async-done(((f32[16,1,128]{2,1,0:T(1,128)}), f32[16,1,128]{2,1,0:T(1,128)S(1)}, u32[]{:S(2)}, u32[]{:S(2)}) %all-to-all-start) | async-done | bytes 8224 | tf_op jit(solution)/shard_map/all_to_all | solution.py:99
  18.3 0.0 collective-permute-done.mate
  18.3 0.0 collective-permute-done.1.other
  18.3 5.0 %shard_map.119 = (f32[384,512]{1,0:T(8,128)S(1)}, f32[16,128]{1,0:T(8,128)}) custom-call(bf16[384,512]{1,0:T(8,128)(2,1)S(1)} %get-tuple-element.11.own, f32[16,128]{1,0:T(8,128)S(1)} %bitcast.18, f32[9,512]{1,0:T(8,128)S(1)} %pad_maximum_fusion.table.refs_17_, bf16[3,1536,512]{2,1,0:T(8,128)(2,1)} %bitcast.22, ...), custom_call_target="tpu_custom_call" | custom-call | tf_op jit(solution)/shard_map/pallas_call | solution.py:234
  23.3 0.0 copy-start.1
  23.3 3.8 %all-to-all-start.1 = ((f32[16,1,128]{2,1,0:T(1,128)}), f32[16,1,128]{2,1,0:T(1,128)S(1)}, u32[]{:S(2)}, u32[]{:S(2)}) async-start(f32[16,1,128]{2,1,0:T(1,128)} %bitcast.7), calls=%async_computation.1 | async-start | bytes 16384 | tf_op jit(solution)/shard_map/all_to_all | solution.py:99
  27.8 0.0 copy-done.5
  27.8 0.0 copy-done.4
  27.8 0.3 shard_map.121.film
  28.0 4.0 %shard_map.120.outer = f32[384,512]{1,0:T(8,128)S(1)} custom-call(bf16[384,512]{1,0:T(8,128)(2,1)S(1)} %get-tuple-element.11.own, f32[16,128]{1,0:T(8,128)S(1)} %bitcast.19, f32[9,512]{1,0:T(8,128)S(1)} %pad_maximum_fusion.table.refs_17_, bf16[3,1536,512]{2,1,0:T(8,128)(2,1)} %bitcast.23, bf16[384,512]{1,0:T(8,128)(2,1)S(1)} %collective-permute-done.mate, ...), custom_call_target="tpu_custom_call" | custom-call | tf_op jit(solution)/shard_map/pallas_call | solution.py:234
  32.1 0.0 copy-start.3
  32.1 1.1 %all-to-all-done.1 = f32[16,1,128]{2,1,0:T(1,128)S(1)} async-done(((f32[16,1,128]{2,1,0:T(1,128)}), f32[16,1,128]{2,1,0:T(1,128)S(1)}, u32[]{:S(2)}, u32[]{:S(2)}) %all-to-all-start.1) | async-done | bytes 8224 | tf_op jit(solution)/shard_map/all_to_all | solution.py:99
  33.2 0.0 copy-start.2
  33.2 0.3 shard_map.122.norm
  33.5 0.0 copy-done.1
  33.5 4.3 %shard_map.123 = (f32[96,512]{1,0:T(8,128)S(1)}, bf16[96,512]{1,0:T(8,128)(2,1)S(1)}) custom-call(f32[384,512]{1,0:T(8,128)S(1)} %get-tuple-element.13.first, f32[384,512]{1,0:T(8,128)S(1)} %shard_map.120.outer, bf16[384,512]{1,0:T(8,128)(2,1)S(1)} %bitcast.17, f32[3,512]{1,0:T(4,128)S(1)} %shard_map.122.norm, f32[9,512]{1,0:T(8,128)S(1)} %pad_maximum_fusion.table.refs_17_, ...), custom_call_target="tpu_custom_call" | custom-call | tf_op jit(solution)/shard_map/pallas_call | solution.py:290
  37.8 0.6 %collective-permute-start.2 = (bf16[96,512]{1,0:T(8,128)(2,1)S(1)}, bf16[96,512]{1,0:T(8,128)(2,1)S(1)}, u32[]{:S(2)}, u32[]{:S(2)}) collective-permute-start(bf16[96,512]{1,0:T(8,128)(2,1)S(1)} %get-tuple-element.15.refs_0_), channel_id=1, source_target_pairs={{0,4},{1,5},{2,6},{3,7},{4,0},{5,1},{6,2},{7,3},{8,12},{9,13},{10,... | collective-permute-start | bytes 294920 | tf_op jit(solution)/shard_map/ppermute | solution.py:309
  38.4 2.4 %collective-permute-start.3 = (bf16[96,512]{1,0:T(8,128)(2,1)S(1)}, bf16[96,512]{1,0:T(8,128)(2,1)S(1)}, u32[]{:S(2)}, u32[]{:S(2)}) collective-permute-start(bf16[96,512]{1,0:T(8,128)(2,1)S(1)} %get-tuple-element.15.refs_0_), channel_id=1, source_target_pairs={{0,8},{1,9},{2,10},{3,11},{4,12},{5,13},{6,14},{7,15},{8,0},{9,1},... | collective-permute-start | bytes 294920 | tf_op jit(solution)/shard_map/ppermute | solution.py:309
  40.8 1.4 %collective-permute-start.4 = (bf16[96,512]{1,0:T(8,128)(2,1)S(1)}, bf16[96,512]{1,0:T(8,128)(2,1)S(1)}, u32[]{:S(2)}, u32[]{:S(2)}) collective-permute-start(bf16[96,512]{1,0:T(8,128)(2,1)S(1)} %get-tuple-element.15.refs_0_), channel_id=1, source_target_pairs={{0,12},{1,13},{2,14},{3,15},{4,8},{5,9},{6,10},{7,11},{8,4},{9,5},... | collective-permute-start | bytes 294920 | tf_op jit(solution)/shard_map/ppermute | solution.py:309
  42.3 0.5 collective-permute-start.5
  42.8 0.0 collective-permute-start.9
  42.8 1.0 %collective-permute-done.2.refs_1_ = bf16[96,512]{1,0:T(8,128)(2,1)S(1)} collective-permute-done((bf16[96,512]{1,0:T(8,128)(2,1)S(1)}, bf16[96,512]{1,0:T(8,128)(2,1)S(1)}, u32[]{:S(2)}, u32[]{:S(2)}) %collective-permute-start.2) | collective-permute-done | bytes 98336 | tf_op jit(solution)/shard_map/ppermute | solution.py:309
  43.8 0.5 collective-permute-start.6
  44.3 4.9 %collective-permute-done.3.refs_2_ = bf16[96,512]{1,0:T(8,128)(2,1)S(1)} collective-permute-done((bf16[96,512]{1,0:T(8,128)(2,1)S(1)}, bf16[96,512]{1,0:T(8,128)(2,1)S(1)}, u32[]{:S(2)}, u32[]{:S(2)}) %collective-permute-start.3) | collective-permute-done | bytes 98336 | tf_op jit(solution)/shard_map/ppermute | solution.py:309
  49.2 1.5 %collective-permute-start.7 = (bf16[96,512]{1,0:T(8,128)(2,1)S(1)}, bf16[96,512]{1,0:T(8,128)(2,1)S(1)}, u32[]{:S(2)}, u32[]{:S(2)}) collective-permute-start(bf16[96,512]{1,0:T(8,128)(2,1)S(1)} %collective-permute-done.3.refs_2_), channel_id=1, source_target_pairs={{0,2},{1,3},{2,0},{3,1},{4,6},{5,7},{6,4},{7,5},{8,10},{9,11},{10,... | collective-permute-start | bytes 294920 | tf_op jit(solution)/shard_map/ppermute | solution.py:309
  50.6 0.0 collective-permute-done.4.refs_3_
  50.6 0.6 collective-permute-start.8
  51.2 0.0 collective-permute-done.5.refs_4_
  51.2 0.0 collective-permute-start.10
  51.2 0.0 collective-permute-done.9.refs_8_
  51.2 0.5 collective-permute-start.11
  51.7 0.0 collective-permute-done.6.refs_5_
  51.7 0.1 collective-permute-start.12
  51.8 2.0 %collective-permute-done.7.refs_6_ = bf16[96,512]{1,0:T(8,128)(2,1)S(1)} collective-permute-done((bf16[96,512]{1,0:T(8,128)(2,1)S(1)}, bf16[96,512]{1,0:T(8,128)(2,1)S(1)}, u32[]{:S(2)}, u32[]{:S(2)}) %collective-permute-start.7) | collective-permute-done | bytes 98336 | tf_op jit(solution)/shard_map/ppermute | solution.py:309
  53.8 0.0 collective-permute-start.13
  53.8 1.5 %collective-permute-done.8.refs_7_ = bf16[96,512]{1,0:T(8,128)(2,1)S(1)} collective-permute-done((bf16[96,512]{1,0:T(8,128)(2,1)S(1)}, bf16[96,512]{1,0:T(8,128)(2,1)S(1)}, u32[]{:S(2)}, u32[]{:S(2)}) %collective-permute-start.8) | collective-permute-done | bytes 98336 | tf_op jit(solution)/shard_map/ppermute | solution.py:309
  55.2 0.0 collective-permute-start.14
  55.2 0.0 collective-permute-done.10.refs_9_
  55.3 0.5 collective-permute-start.15
  55.8 0.0 collective-permute-done.11.refs_10_
  55.8 0.1 collective-permute-start.16
  55.8 0.0 collective-permute-done.12.refs_11_
  55.8 0.0 collective-permute-done.13.refs_12_
  55.8 0.7 %collective-permute-done.14.refs_13_ = bf16[96,512]{1,0:T(8,128)(2,1)S(1)} collective-permute-done((bf16[96,512]{1,0:T(8,128)(2,1)S(1)}, bf16[96,512]{1,0:T(8,128)(2,1)S(1)}, u32[]{:S(2)}, u32[]{:S(2)}) %collective-permute-start.14) | collective-permute-done | bytes 98336 | tf_op jit(solution)/shard_map/ppermute | solution.py:309
  56.5 0.2 collective-permute-done.15.refs_14_
  56.7 0.4 collective-permute-done.16.refs_15_
  57.1 0.0 copy-done.3
  57.1 0.0 copy-done.2
  57.1 5.0 %shard_map.124 = bf16[96,512]{1,0:T(8,128)(2,1)} custom-call(bf16[96,512]{1,0:T(8,128)(2,1)S(1)} %get-tuple-element.15.refs_0_, bf16[96,512]{1,0:T(8,128)(2,1)S(1)} %collective-permute-done.2.refs_1_, bf16[96,512]{1,0:T(8,128)(2,1)S(1)} %collective-permute-done.3.refs_2_, bf16[96,512]{1,0:T(8,128)(2,1)S(1)} %collective-permute-done.4.refs_3_, ...), custom_call_target="tpu_custom_call" | custom-call | tf_op jit(solution)/shard_map/pallas_call | solution.py:376
Async XLA Ops:
  0.0 27.8 %copy-start.5 = (f32[18]{0:T(128)S(1)}, f32[18]{0:T(128)}, u32[]{:S(2)}) copy-start(f32[18]{0:T(128)} %param.14) | copy-start | bytes 220
  0.0 18.3 %collective-permute-start = (bf16[384,512]{1,0:T(8,128)(2,1)}, bf16[384,512]{1,0:T(8,128)(2,1)S(1)}, u32[]{:S(2)}, u32[]{:S(2)}) collective-permute-start(bf16[384,512]{1,0:T(8,128)(2,1)} %bitcast.14), channel_id=1, source_target_pairs={{0,1},{1,0},{2,3},{3,2},{4,5},{5,4},{6,7},{7,6},{8,9},{9,8},{10,11... | collective-permute-start | bytes 1179656 | tf_op jit(solution)/shard_map/ppermute | solution.py:406
  0.5 17.8 %collective-permute-start.1 = (bf16[384,512]{1,0:T(8,128)(2,1)}, bf16[384,512]{1,0:T(8,128)(2,1)S(1)}, u32[]{:S(2)}, u32[]{:S(2)}) collective-permute-start(bf16[384,512]{1,0:T(8,128)(2,1)} %bitcast.15), channel_id=1, source_target_pairs={{1,2},{2,1},{3,4},{4,3},{5,6},{6,5},{7,8},{8,7},{9,10},{10,9},{11,... | collective-permute-start | bytes 1179656 | tf_op jit(solution)/shard_map/ppermute | solution.py:407
  1.1 1.0 %copy-start = (bf16[1,2,192,512]{3,2,1,0:T(8,128)(2,1)S(1)}, bf16[1,2,192,512]{3,2,1,0:T(8,128)(2,1)}, u32[]{:S(2)}) copy-start(bf16[1,2,192,512]{3,2,1,0:T(8,128)(2,1)} %param.12) | copy-start | bytes 1179652
  2.1 25.6 %copy-start.4 = (bf16[128,1024]{1,0:T(8,128)(2,1)S(1)}, bf16[128,1024]{1,0:T(8,128)(2,1)}, u32[]{:S(2)}) copy-start(bf16[128,1024]{1,0:T(8,128)(2,1)} %affine_weight.1) | copy-start | bytes 786436
  3.2 15.1 %all-to-all-start = ((f32[16,1,128]{2,1,0:T(1,128)}), f32[16,1,128]{2,1,0:T(1,128)S(1)}, u32[]{:S(2)}, u32[]{:S(2)}) async-start(f32[16,1,128]{2,1,0:T(1,128)} %bitcast.2), calls=%async_computation | async-start | bytes 16384 | tf_op jit(solution)/shard_map/all_to_all | solution.py:99
  23.3 10.2 %copy-start.1 = (bf16[1,2,192,512]{3,2,1,0:T(8,128)(2,1)S(1)}, bf16[1,2,192,512]{3,2,1,0:T(8,128)(2,1)}, u32[]{:S(2)}) copy-start(bf16[1,2,192,512]{3,2,1,0:T(8,128)(2,1)} %param.12) | copy-start | bytes 1179652
  23.3 9.9 %all-to-all-start.1 = ((f32[16,1,128]{2,1,0:T(1,128)}), f32[16,1,128]{2,1,0:T(1,128)S(1)}, u32[]{:S(2)}, u32[]{:S(2)}) async-start(f32[16,1,128]{2,1,0:T(1,128)} %bitcast.7), calls=%async_computation.1 | async-start | bytes 16384 | tf_op jit(solution)/shard_map/all_to_all | solution.py:99
  32.1 25.0 %copy-start.3 = (bf16[512,512]{1,0:T(8,128)(2,1)S(1)}, bf16[512,512]{1,0:T(8,128)(2,1)}, u32[]{:S(2)}) copy-start(bf16[512,512]{1,0:T(8,128)(2,1)} %refs_19_.1) | copy-start | bytes 1572868
  33.2 23.9 %copy-start.2 = (bf16[512,1536]{1,0:T(8,128)(2,1)S(1)}, bf16[512,1536]{1,0:T(8,128)(2,1)}, u32[]{:S(2)}) copy-start(bf16[512,1536]{1,0:T(8,128)(2,1)} %refs_18_.1) | copy-start | bytes 4718596
  37.8 6.0 %collective-permute-start.2 = (bf16[96,512]{1,0:T(8,128)(2,1)S(1)}, bf16[96,512]{1,0:T(8,128)(2,1)S(1)}, u32[]{:S(2)}, u32[]{:S(2)}) collective-permute-start(bf16[96,512]{1,0:T(8,128)(2,1)S(1)} %get-tuple-element.15.refs_0_), channel_id=1, source_target_pairs={{0,4},{1,5},{2,6},{3,7},{4,0},{5,1},{6,2},{7,3},{8,12},{9,13},{10,... | collective-permute-start | bytes 294920 | tf_op jit(solution)/shard_map/ppermute | solution.py:309
  38.4 10.7 %collective-permute-start.3 = (bf16[96,512]{1,0:T(8,128)(2,1)S(1)}, bf16[96,512]{1,0:T(8,128)(2,1)S(1)}, u32[]{:S(2)}, u32[]{:S(2)}) collective-permute-start(bf16[96,512]{1,0:T(8,128)(2,1)S(1)} %get-tuple-element.15.refs_0_), channel_id=1, source_target_pairs={{0,8},{1,9},{2,10},{3,11},{4,12},{5,13},{6,14},{7,15},{8,0},{9,1},... | collective-permute-start | bytes 294920 | tf_op jit(solution)/shard_map/ppermute | solution.py:309
  40.8 9.8 %collective-permute-start.4 = (bf16[96,512]{1,0:T(8,128)(2,1)S(1)}, bf16[96,512]{1,0:T(8,128)(2,1)S(1)}, u32[]{:S(2)}, u32[]{:S(2)}) collective-permute-start(bf16[96,512]{1,0:T(8,128)(2,1)S(1)} %get-tuple-element.15.refs_0_), channel_id=1, source_target_pairs={{0,12},{1,13},{2,14},{3,15},{4,8},{5,9},{6,10},{7,11},{8,4},{9,5},... | collective-permute-start | bytes 294920 | tf_op jit(solution)/shard_map/ppermute | solution.py:309
  42.3 8.9 %collective-permute-start.5 = (bf16[96,512]{1,0:T(8,128)(2,1)S(1)}, bf16[96,512]{1,0:T(8,128)(2,1)S(1)}, u32[]{:S(2)}, u32[]{:S(2)}) collective-permute-start(bf16[96,512]{1,0:T(8,128)(2,1)S(1)} %get-tuple-element.15.refs_0_), channel_id=1, source_target_pairs={{0,2},{1,3},{2,0},{3,1},{4,6},{5,7},{6,4},{7,5},{8,10},{9,11},{10,... | collective-permute-start | bytes 294920 | tf_op jit(solution)/shard_map/ppermute | solution.py:309
  42.8 8.4 %collective-permute-start.9 = (bf16[96,512]{1,0:T(8,128)(2,1)S(1)}, bf16[96,512]{1,0:T(8,128)(2,1)S(1)}, u32[]{:S(2)}, u32[]{:S(2)}) collective-permute-start(bf16[96,512]{1,0:T(8,128)(2,1)S(1)} %get-tuple-element.15.refs_0_), channel_id=1, source_target_pairs={{0,1},{1,0},{2,3},{3,2},{4,5},{5,4},{6,7},{7,6},{8,9},{9,8},{10,11... | collective-permute-start | bytes 294920 | tf_op jit(solution)/shard_map/ppermute | solution.py:309
  43.8 7.9 %collective-permute-start.6 = (bf16[96,512]{1,0:T(8,128)(2,1)S(1)}, bf16[96,512]{1,0:T(8,128)(2,1)S(1)}, u32[]{:S(2)}, u32[]{:S(2)}) collective-permute-start(bf16[96,512]{1,0:T(8,128)(2,1)S(1)} %collective-permute-done.2.refs_1_), channel_id=1, source_target_pairs={{0,2},{1,3},{2,0},{3,1},{4,6},{5,7},{6,4},{7,5},{8,10},{9,11},{10,... | collective-permute-start | bytes 294920 | tf_op jit(solution)/shard_map/ppermute | solution.py:309
  49.2 4.6 %collective-permute-start.7 = (bf16[96,512]{1,0:T(8,128)(2,1)S(1)}, bf16[96,512]{1,0:T(8,128)(2,1)S(1)}, u32[]{:S(2)}, u32[]{:S(2)}) collective-permute-start(bf16[96,512]{1,0:T(8,128)(2,1)S(1)} %collective-permute-done.3.refs_2_), channel_id=1, source_target_pairs={{0,2},{1,3},{2,0},{3,1},{4,6},{5,7},{6,4},{7,5},{8,10},{9,11},{10,... | collective-permute-start | bytes 294920 | tf_op jit(solution)/shard_map/ppermute | solution.py:309
  50.6 4.6 %collective-permute-start.8 = (bf16[96,512]{1,0:T(8,128)(2,1)S(1)}, bf16[96,512]{1,0:T(8,128)(2,1)S(1)}, u32[]{:S(2)}, u32[]{:S(2)}) collective-permute-start(bf16[96,512]{1,0:T(8,128)(2,1)S(1)} %collective-permute-done.4.refs_3_), channel_id=1, source_target_pairs={{0,2},{1,3},{2,0},{3,1},{4,6},{5,7},{6,4},{7,5},{8,10},{9,11},{10,... | collective-permute-start | bytes 294920 | tf_op jit(solution)/shard_map/ppermute | solution.py:309
  51.2 4.1 %collective-permute-start.10 = (bf16[96,512]{1,0:T(8,128)(2,1)S(1)}, bf16[96,512]{1,0:T(8,128)(2,1)S(1)}, u32[]{:S(2)}, u32[]{:S(2)}) collective-permute-start(bf16[96,512]{1,0:T(8,128)(2,1)S(1)} %collective-permute-done.2.refs_1_), channel_id=1, source_target_pairs={{0,1},{1,0},{2,3},{3,2},{4,5},{5,4},{6,7},{7,6},{8,9},{9,8},{10,11... | collective-permute-start | bytes 294920 | tf_op jit(solution)/shard_map/ppermute | solution.py:309
  51.2 4.6 %collective-permute-start.11 = (bf16[96,512]{1,0:T(8,128)(2,1)S(1)}, bf16[96,512]{1,0:T(8,128)(2,1)S(1)}, u32[]{:S(2)}, u32[]{:S(2)}) collective-permute-start(bf16[96,512]{1,0:T(8,128)(2,1)S(1)} %collective-permute-done.3.refs_2_), channel_id=1, source_target_pairs={{0,1},{1,0},{2,3},{3,2},{4,5},{5,4},{6,7},{7,6},{8,9},{9,8},{10,11... | collective-permute-start | bytes 294920 | tf_op jit(solution)/shard_map/ppermute | solution.py:309
  51.7 4.1 %collective-permute-start.12 = (bf16[96,512]{1,0:T(8,128)(2,1)S(1)}, bf16[96,512]{1,0:T(8,128)(2,1)S(1)}, u32[]{:S(2)}, u32[]{:S(2)}) collective-permute-start(bf16[96,512]{1,0:T(8,128)(2,1)S(1)} %collective-permute-done.4.refs_3_), channel_id=1, source_target_pairs={{0,1},{1,0},{2,3},{3,2},{4,5},{5,4},{6,7},{7,6},{8,9},{9,8},{10,11... | collective-permute-start | bytes 294920 | tf_op jit(solution)/shard_map/ppermute | solution.py:309
  53.8 2.1 %collective-permute-start.13 = (bf16[96,512]{1,0:T(8,128)(2,1)S(1)}, bf16[96,512]{1,0:T(8,128)(2,1)S(1)}, u32[]{:S(2)}, u32[]{:S(2)}) collective-permute-start(bf16[96,512]{1,0:T(8,128)(2,1)S(1)} %collective-permute-done.5.refs_4_), channel_id=1, source_target_pairs={{0,1},{1,0},{2,3},{3,2},{4,5},{5,4},{6,7},{7,6},{8,9},{9,8},{10,11... | collective-permute-start | bytes 294920 | tf_op jit(solution)/shard_map/ppermute | solution.py:309
  55.2 1.3 %collective-permute-start.14 = (bf16[96,512]{1,0:T(8,128)(2,1)S(1)}, bf16[96,512]{1,0:T(8,128)(2,1)S(1)}, u32[]{:S(2)}, u32[]{:S(2)}) collective-permute-start(bf16[96,512]{1,0:T(8,128)(2,1)S(1)} %collective-permute-done.6.refs_5_), channel_id=1, source_target_pairs={{0,1},{1,0},{2,3},{3,2},{4,5},{5,4},{6,7},{7,6},{8,9},{9,8},{10,11... | collective-permute-start | bytes 294920 | tf_op jit(solution)/shard_map/ppermute | solution.py:309
  55.3 1.5 %collective-permute-start.15 = (bf16[96,512]{1,0:T(8,128)(2,1)S(1)}, bf16[96,512]{1,0:T(8,128)(2,1)S(1)}, u32[]{:S(2)}, u32[]{:S(2)}) collective-permute-start(bf16[96,512]{1,0:T(8,128)(2,1)S(1)} %collective-permute-done.7.refs_6_), channel_id=1, source_target_pairs={{0,1},{1,0},{2,3},{3,2},{4,5},{5,4},{6,7},{7,6},{8,9},{9,8},{10,11... | collective-permute-start | bytes 294920 | tf_op jit(solution)/shard_map/ppermute | solution.py:309
  55.8 1.3 %collective-permute-start.16 = (bf16[96,512]{1,0:T(8,128)(2,1)S(1)}, bf16[96,512]{1,0:T(8,128)(2,1)S(1)}, u32[]{:S(2)}, u32[]{:S(2)}) collective-permute-start(bf16[96,512]{1,0:T(8,128)(2,1)S(1)} %collective-permute-done.8.refs_7_), channel_id=1, source_target_pairs={{0,1},{1,0},{2,3},{3,2},{4,5},{5,4},{6,7},{7,6},{8,9},{9,8},{10,11... | collective-permute-start | bytes 294920 | tf_op jit(solution)/shard_map/ppermute | solution.py:309
